TPU v7x, 256 devices: a whole 4x4x8 slice. The times are simulated.
256 devices in a mesh: dom: 16 (over z, x_hi), orb: 16 (over x_lo, y, core).
Axes of the slice: x: 4 (x_hi: 2, x_lo: 2; x = x_hi * 2 + x_lo), y: 4, z: 8, core: 2. Of those that a mesh axis runs over, the one named last changes fastest.
Arguments:
- rhs: float32 [128, 32, 32, 128], P('orb', 'dom'), may hold values from -6 to 6
- potential: float32 [32, 32, 128], P('dom'), may hold values from 0.5 to 2
- eigen_table: float32 [4096], replicated, may hold values from -1 to -0.1
- win_index: int32 [128], P('orb'), may hold values from 0 to 4095
- occupied: bfloat16 [32, 128, 32, 32, 128], P('orb', None, 'dom'), may hold values from -6 to 6
- block_ids: int32 [4], replicated, may hold values from 0 to 31, as said below
- psi_win: bfloat16 [128, 32, 32, 128], P('orb', 'dom'), may hold values from -6 to 6
- smoother: float32 [32, 32], replicated, may hold values from -1 to 1
Outputs:
- solution: float32 [128, 32, 32, 128], P('orb', 'dom')
- correlations: float32 [4, 128, 128], P(None, None, 'orb')
- gradient: float32 [32, 32, 128], P(None, 'dom', 'orb')
Inputs may be any that keep to these rules, and one draw needn't show every extreme that they name: `block_ids`: distinct block numbers; block 0 and block 31 are always among them.
All inputs are finite; a program needn't handle non-finite values.
Results may differ from a plain program's by a relative error of at most 0.0047.
Values may be sent and summed in bfloat16 or wider, within the bound.
No kernel may reach another device: no remote copies, remote signals or barrier semaphores. Data moves between devices by JAX's collectives and lax.ppermute only.
A program may use at most 64 MiB of HBM per device.

v0:
```python
import math

import jax
import jax.numpy as jnp
from jax import lax
from jax.sharding import PartitionSpec as P

ITERS = 3


def extended(block, sides, width):
    for axis, dim in sides:
        count = lax.axis_size(axis)
        forward = [(i, i + 1) for i in range(count - 1)]
        backward = [(target, source) for source, target in forward]
        low = lax.ppermute(
            lax.slice_in_dim(block, block.shape[dim] - width, None, axis=dim), axis, forward
        )
        high = lax.ppermute(lax.slice_in_dim(block, 0, width, axis=dim), axis, backward)
        block = jnp.concatenate([low, block, high], axis=dim)
    return block


def spread(block, axis, holder):
    block = jnp.where(lax.axis_index(axis) == holder, block, jnp.zeros_like(block))
    return lax.psum(block, axis)


def apply_operator(field, diag):
    padded = extended(field, (("dom", 1),), 1)
    padded = jnp.pad(padded, ((0, 0), (0, 0), (1, 1), (1, 1)))
    beside = padded[:, 2:, 1:-1, 1:-1] + padded[:, :-2, 1:-1, 1:-1]
    beside = beside + padded[:, 1:-1, 2:, 1:-1] + padded[:, 1:-1, :-2, 1:-1]
    beside = beside + padded[:, 1:-1, 1:-1, 2:] + padded[:, 1:-1, 1:-1, :-2]
    return diag * field - 0.5 * beside


def per_device(rhs, potential, eigen_table, win_index, occupied, block_ids, psi_win, smoother):
    local_orbs, planes, rows_y, rows_z = rhs.shape
    cells = planes * rows_y * rows_z
    n_dom = lax.axis_size("dom")
    n_orb = lax.axis_size("orb")
    width = local_orbs * n_orb
    scale = 1.0 / math.sqrt(planes * n_dom * rows_y * rows_z)
    n_occ = eigen_table.shape[0]
    picks = win_index[:, None] == jnp.arange(n_occ, dtype=jnp.int32)[None, :]
    eps = jnp.sum(jnp.where(picks, eigen_table[None, :], 0.0), axis=1)
    diag = 3.0 + potential[None] - eps[:, None, None, None]
    per_dev = occupied.shape[0]
    blk_rows = occupied.shape[1]
    nproj = block_ids.shape[0]
    owners = block_ids // per_dev
    slots = block_ids % per_dev
    mine = jnp.stack(
        [lax.dynamic_index_in_dim(occupied, slots[j], 0, keepdims=False) for j in range(nproj)]
    )
    received = []
    for j in range(nproj):
        received.append(spread(mine[j], "orb", owners[j]))
    blocks = jnp.stack(received).reshape(nproj * blk_rows, cells)
    solution = jnp.zeros(rhs.shape, jnp.float32)
    coeff = jnp.zeros((nproj * blk_rows, local_orbs), jnp.float32)
    for step in range(ITERS):
        resid = rhs - apply_operator(solution, diag)
        resid_b = resid.astype(jnp.bfloat16).reshape(local_orbs, cells)
        part = jnp.einsum("kc,wc->kw", blocks, resid_b, preferred_element_type=jnp.float32) * scale
        project_coeff = lax.psum(part, "dom")
        coeff_b = project_coeff.astype(jnp.bfloat16)
        corr = jnp.einsum("kw,kc->wc", coeff_b, blocks, preferred_element_type=jnp.float32) * scale
        coeff, corr = (project_coeff, corr)
        solution = solution + (resid - corr.reshape(resid.shape)) / diag
    correlations = coeff.reshape(nproj, blk_rows, local_orbs)
    raw_part = jnp.sum(solution * psi_win.astype(jnp.float32), axis=0) / math.sqrt(width)
    full_x = planes * n_dom
    pencil = lax.all_to_all(raw_part, "dom", split_axis=1, concat_axis=0, tiled=True)
    smoothed = jnp.dot(
        smoother, pencil.reshape(full_x, -1), precision=lax.Precision.HIGHEST
    ).reshape(pencil.shape)
    gradient = lax.psum_scatter(smoothed, "orb", scatter_dimension=2, tiled=True)
    return (solution, correlations, gradient)


def solution(mesh):
    return jax.shard_map(
        per_device,
        mesh=mesh,
        in_specs=(
            P("orb", "dom", None, None),
            P("dom", None, None),
            P(),
            P("orb"),
            P("orb", None, "dom", None, None),
            P(),
            P("orb", "dom", None, None),
            P(),
        ),
        out_specs=(P("orb", "dom", None, None), P(None, None, "orb"), P(None, "dom", "orb")),
        check_vma=False,
    )
```

profile of v0, /device:TPU:1, one launch (start us, length us, event | category | flops | bytes accessed | tf_op | source)
XLA Modules:
  0.0 549.9 jit_solution(14928761977190360467)
XLA Ops:
  7.2 0.0 copy-start
  7.2 0.0 all-reduce.8.cloned.1.call-start
  7.2 0.7 and_select_fusion.1
  7.9 0.7 fusion.41
  18.5 6.8 %dynamic-slice_select_fusion.3 = (bf16[1,128,2,32,128]{4,3,2,1,0:T(8,128)(2,1)}, bf16[1,128,2,32,128]{4,3,2,1,0:T(8,128)(2,1)}, bf16[1,128,2,32,128]{4,3,2,1,0:T(8,128)(2,1)}, bf16[1,128,2,32,128]{4,3,2,1,0:T(8,128)(2,1)}) fusion(bf16[2,128,2,32,128]{4,3,2,1,0:T(8,128)(2,1)} %param.12, s32[]{:T(128)S(6)} %select_n.71, pred[]{:T(512)S(6)} %eq.30, ...), kind=kLoop, calls=%fused_computation.7 | loop fusion | flops 4194304 | bytes 16777236 | tf_op jit(solution)/shard_map/jit(_where)/select_n | solution.py:25
  25.3 0.0 all-reduce.8.cloned.1.call-update
  25.4 0.0 copy-start.2
  25.4 0.0 reduce-scatter.2.cloned.1.call-start
  25.4 1.4 collective-permute-start
  26.9 6.1 %collective-permute-start.1 = (f32[8,1,32,128]{3,2,1,0:T(8,128)S(1)}, f32[8,1,32,128]{3,2,1,0:T(8,128)S(1)}, u32[]{:S(2)}, u32[]{:S(2)}) collective-permute-start(f32[8,1,32,128]{3,2,1,0:T(8,128)S(1)} %broadcast.59), channel_id=1, source_target_pairs={{0,16},{16,32},{32,48},{48,64},{64,80},{80,96},{96,112},{112,128},... | collective-permute-start | bytes 393224 | tf_op jit(solution)/shard_map/ppermute | solution.py:16
  33.0 0.2 select_reduce_fusion
  33.3 0.2 collective-permute-done
  33.4 3.3 collective-permute-done.1
  36.7 0.4 select_maximum_fusion.4
  37.1 0.3 fusion.37
  37.4 138.7 %all-reduce.8.cloned.1.call-done = (bf16[1,128,2,32,128]{4,3,2,1,0:T(8,128)(2,1)}, bf16[1,128,2,32,128]{4,3,2,1,0:T(8,128)(2,1)}, bf16[1,128,2,32,128]{4,3,2,1,0:T(8,128)(2,1)}, bf16[1,128,2,32,128]{4,3,2,1,0:T(8,128)(2,1)}) async-done(((bf16[1,128,2,32,128]{4,3,2,1,0:T(8,128)(2,1)}, bf16[1,128,2,32,128]{4,3,2,1,0:T(8,128)(2,1)}, bf16[1,128,2,32,128]{4,3,2,1,0:T(8,128)(2,1)}, ...) | async-done | bytes 8388624 | tf_op jit(solution)/shard_map/psum | solution.py:26
  176.1 7.1 %pad_maximum_fusion = bf16[4,128,2,32,128]{4,3,2,1,0:T(8,128)(2,1)} fusion(bf16[1,128,2,32,128]{4,3,2,1,0:T(8,128)(2,1)} %get-tuple-element.3, bf16[1,128,2,32,128]{4,3,2,1,0:T(8,128)(2,1)} %get-tuple-element.4, bf16[1,128,2,32,128]{4,3,2,1,0:T(8,128)(2,1)} %get-tuple-element.5, bf16[1,128,2,32,128]{4,3,2,1,0:T(8,128)(2,1)} %get-tuple-element.6), kind=kLoop, calls=%fused_computation.3 | loop fusion | flops 12582912 | bytes 16777216 | tf_op jit(solution)/shard_map/stack | solution.py:60
  183.3 13.3 %reshape.54 = bf16[512,8192]{1,0:T(8,128)(2,1)} reshape(bf16[4,128,2,32,128]{4,3,2,1,0:T(8,128)(2,1)} %pad_maximum_fusion) | data formatting | bytes 16777216 | tf_op jit(solution)/shard_map/reshape | solution.py:60
  196.5 5.6 %convolution_multiply_fusion.5 = f32[512,8]{0,1:T(8,128)S(1)} fusion(bf16[512,8192]{1,0:T(8,128)(2,1)} %reshape.54, bf16[1,8,64,128]{3,2,1,0:T(8,128)(2,1)S(1)} %bitcast.52), kind=kOutput, calls=%fused_computation.24 | convolution fusion | flops 67112960 | bytes 8536064 | tf_op jit(solution)/shard_map/kc,wc->kw/dot_general | solution.py:66
  202.2 63.3 %psum.53 = bf16[512,8]{0,1:T(8,128)(2,1)S(1)} all-reduce(f32[512,8]{0,1:T(8,128)S(1)} %convolution_multiply_fusion.5), channel_id=1, replica_groups=mesh['dom'=16,'orb'=16] {'dom'}, use_global_device_ids=true, to_apply=%region_5.6 | all-reduce | flops 4096 | bytes 24576 | tf_op jit(solution)/shard_map/psum | solution.py:67
  265.5 4.7 convolution_multiply_fusion.2
  270.2 0.1 subtract_divide_fusion.2
  270.3 1.3 collective-permute-start.2
  271.6 5.5 collective-permute-start.3
  277.1 0.4 collective-permute-done.2
  277.5 1.5 collective-permute-done.3
  279.1 0.4 select_maximum_fusion.2
  279.5 0.3 fusion.35
  279.8 2.3 convolution_multiply_fusion.4
  282.1 61.8 %psum.54 = bf16[512,8]{0,1:T(8,128)(2,1)S(1)} all-reduce(f32[512,8]{0,1:T(8,128)S(1)} %convolution_multiply_fusion.4), channel_id=1, replica_groups=mesh['dom'=16,'orb'=16] {'dom'}, use_global_device_ids=true, to_apply=%region_6.7 | all-reduce | flops 4096 | bytes 24576 | tf_op jit(solution)/shard_map/psum | solution.py:67
  343.9 4.6 convolution_multiply_fusion.1
  348.5 0.1 fusion.13
  348.6 1.3 collective-permute-start.4
  349.9 5.7 %collective-permute-start.5 = (f32[8,1,32,128]{3,2,1,0:T(8,128)S(1)}, f32[8,1,32,128]{3,2,1,0:T(8,128)S(1)}, u32[]{:S(2)}, u32[]{:S(2)}) collective-permute-start(f32[8,1,32,128]{3,2,1,0:T(8,128)S(1)} %get-tuple-element.19), channel_id=1, source_target_pairs={{0,16},{16,32},{32,48},{48,64},{64,80},{80,96},{96,112},{112,128},... | collective-permute-start | bytes 393224 | tf_op jit(solution)/shard_map/ppermute | solution.py:16
  355.6 0.6 collective-permute-done.4
  356.2 1.2 collective-permute-done.5
  357.4 0.4 select_maximum_fusion
  357.8 0.3 fusion.33
  358.1 5.6 %convolution_multiply_fusion.3 = f32[512,8]{0,1:T(8,128)S(1)} fusion(bf16[512,8192]{1,0:T(8,128)(2,1)} %reshape.54, bf16[1,8,64,128]{3,2,1,0:T(8,128)(2,1)S(1)} %bitcast.54), kind=kOutput, calls=%fused_computation.22 | convolution fusion | flops 67112960 | bytes 8536064 | tf_op jit(solution)/shard_map/kc,wc->kw/dot_general | solution.py:66
  363.8 61.3 %psum.55 = f32[512,8]{0,1:T(8,128)S(1)} all-reduce(f32[512,8]{0,1:T(8,128)S(1)} %convolution_multiply_fusion.3), channel_id=1, replica_groups=mesh['dom'=16,'orb'=16] {'dom'}, use_global_device_ids=true, to_apply=%region_7.8 | all-reduce | flops 4096 | bytes 32768 | tf_op jit(solution)/shard_map/psum | solution.py:67
  425.1 4.6 convolution_multiply_fusion
  429.7 0.0 copy-done.3
  429.7 0.9 multiply_reduce_fusion
  430.6 13.4 %all_to_all.15 = f32[2,32,128]{2,0,1:T(2,128)S(1)} all-to-all(f32[2,32,128]{2,0,1:T(2,128)S(1)} %copy.40), channel_id=1, replica_groups=mesh['dom'=16,'orb'=16] {'dom'}, dimensions={1} | all-to-all | bytes 65536 | tf_op jit(solution)/shard_map/all_to_all | solution.py:75
  444.0 0.2 convolution_bitcast_fusion
  444.1 0.7 copy.44
  444.9 0.0 reduce-scatter.2.cloned.1.call-update
  444.9 98.1 %reduce-scatter.2.cloned.1.call-done = f32[32,2,8]{0,2,1:T(8,128)} async-done(((f32[32,2,128]{0,2,1:T(8,128)}), f32[32,2,8]{0,2,1:T(8,128)}) %reduce-scatter.2.cloned.1.call-update) | async-done | bytes 2064 | tf_op jit(solution)/shard_map/reduce_scatter | solution.py:79
  (22 shorter events, 0.1 us)
Async XLA Ops:
  7.2 436.8 %copy-start = (f32[32,32]{1,0:T(8,128)S(1)}, f32[32,32]{1,0:T(8,128)}, u32[]{:S(2)}) copy-start(f32[32,32]{1,0:T(8,128)} %param.15) | copy-start | bytes 12292
  7.2 168.9 %all-reduce.8.cloned.1.call-start = ((), (), s32[]{:S(2)}) async-start(), calls=%async_computation.3 | async-start | bytes 16777216 | tf_op jit(solution)/shard_map/psum | solution.py:26
  25.3 7.7 %copy-start.5 = (f32[2,32,128]{2,1,0:T(8,128)S(1)}, f32[2,32,128]{2,1,0:T(8,128)}, u32[]{:S(2)}) copy-start(f32[2,32,128]{2,1,0:T(8,128)} %param.9) | copy-start | bytes 98308
  25.3 7.7 %copy-start.6 = (f32[4096]{0:T(1024)S(1)}, f32[4096]{0:T(1024)}, u32[]{:S(2)}) copy-start(f32[4096]{0:T(1024)} %param.10) | copy-start | bytes 49156
  25.3 7.7 %copy-start.7 = (s32[8]{0:T(128)S(1)}, s32[8]{0:T(128)}, u32[]{:S(2)}) copy-start(s32[8]{0:T(128)} %param.11) | copy-start | bytes 100
  25.4 11.8 %copy-start.2 = (f32[8,2,32,128]{3,2,1,0:T(8,128)S(1)}, f32[8,2,32,128]{3,2,1,0:T(8,128)}, u32[]{:S(2)}) copy-start(f32[8,2,32,128]{3,2,1,0:T(8,128)} %param.8) | copy-start | bytes 786436
  25.4 517.7 %reduce-scatter.2.cloned.1.call-start = ((), (), s32[]{:S(2)}) async-start(), calls=%async_computation.2 | async-start | bytes 139264 | tf_op jit(solution)/shard_map/reduce_scatter | solution.py:79
  25.4 8.0 %collective-permute-start = (f32[8,1,32,128]{3,2,1,0:T(8,128)S(1)}, f32[8,1,32,128]{3,2,1,0:T(8,128)S(1)}, u32[]{:S(2)}, u32[]{:S(2)}) collective-permute-start(f32[8,1,32,128]{3,2,1,0:T(8,128)S(1)} %broadcast.59), channel_id=1, source_target_pairs={{16,0},{32,16},{48,32},{64,48},{80,64},{96,80},{112,96},{128,112},... | collective-permute-start | bytes 393224 | tf_op jit(solution)/shard_map/ppermute | solution.py:19
  26.9 9.8 %collective-permute-start.1 = (f32[8,1,32,128]{3,2,1,0:T(8,128)S(1)}, f32[8,1,32,128]{3,2,1,0:T(8,128)S(1)}, u32[]{:S(2)}, u32[]{:S(2)}) collective-permute-start(f32[8,1,32,128]{3,2,1,0:T(8,128)S(1)} %broadcast.59), channel_id=1, source_target_pairs={{0,16},{16,32},{32,48},{48,64},{64,80},{80,96},{96,112},{112,128},... | collective-permute-start | bytes 393224 | tf_op jit(solution)/shard_map/ppermute | solution.py:16
  265.5 14.4 %copy-start.1 = (bf16[512,8192]{1,0:T(8,128)(2,1)S(1)}, bf16[512,8192]{1,0:T(8,128)(2,1)}, u32[]{:S(2)}) copy-start(bf16[512,8192]{1,0:T(8,128)(2,1)} %reshape.54) | copy-start | bytes 25165828
  270.3 7.2 %collective-permute-start.2 = (f32[8,1,32,128]{3,2,1,0:T(8,128)S(1)}, f32[8,1,32,128]{3,2,1,0:T(8,128)S(1)}, u32[]{:S(2)}, u32[]{:S(2)}) collective-permute-start(f32[8,1,32,128]{3,2,1,0:T(8,128)S(1)} %get-tuple-element.22), channel_id=1, source_target_pairs={{16,0},{32,16},{48,32},{64,48},{80,64},{96,80},{112,96},{128,112},... | collective-permute-start | bytes 393224 | tf_op jit(solution)/shard_map/ppermute | solution.py:19
  271.6 7.4 %collective-permute-start.3 = (f32[8,1,32,128]{3,2,1,0:T(8,128)S(1)}, f32[8,1,32,128]{3,2,1,0:T(8,128)S(1)}, u32[]{:S(2)}, u32[]{:S(2)}) collective-permute-start(f32[8,1,32,128]{3,2,1,0:T(8,128)S(1)} %get-tuple-element.21), channel_id=1, source_target_pairs={{0,16},{16,32},{32,48},{48,64},{64,80},{80,96},{96,112},{112,128},... | collective-permute-start | bytes 393224 | tf_op jit(solution)/shard_map/ppermute | solution.py:16
  348.6 7.6 %collective-permute-start.4 = (f32[8,1,32,128]{3,2,1,0:T(8,128)S(1)}, f32[8,1,32,128]{3,2,1,0:T(8,128)S(1)}, u32[]{:S(2)}, u32[]{:S(2)}) collective-permute-start(f32[8,1,32,128]{3,2,1,0:T(8,128)S(1)} %get-tuple-element.20), channel_id=1, source_target_pairs={{16,0},{32,16},{48,32},{64,48},{80,64},{96,80},{112,96},{128,112},... | collective-permute-start | bytes 393224 | tf_op jit(solution)/shard_map/ppermute | solution.py:19
  349.9 7.4 %collective-permute-start.5 = (f32[8,1,32,128]{3,2,1,0:T(8,128)S(1)}, f32[8,1,32,128]{3,2,1,0:T(8,128)S(1)}, u32[]{:S(2)}, u32[]{:S(2)}) collective-permute-start(f32[8,1,32,128]{3,2,1,0:T(8,128)S(1)} %get-tuple-element.19), channel_id=1, source_target_pairs={{0,16},{16,32},{32,48},{48,64},{64,80},{80,96},{96,112},{112,128},... | collective-permute-start | bytes 393224 | tf_op jit(solution)/shard_map/ppermute | solution.py:16
  425.1 4.6 copy-start.4
  425.1 4.6 copy-start.3
Sparse Core Ops, SparseCore 0:
  25.5 150.5 all-reduce.7
  445.0 97.9 reduce-scatter.1
where the time goes:
time: 553 us; the launch traced here: 550 us
  waiting for transfers between devices  244 us (44%)
  blocking collectives  200 us (36%)
  matrix products  27.6 us (5%)
  between operations  24.2 us (4%)
  starting transfers between devices  21.4 us (4%)
  other arithmetic  18.1 us (3%)
  local copies, waits for them, and re-layouts  14.9 us (3%)
    psum x3, blocking collectives, per_device(): project_coeff = lax.psum(part, 'dom')  186 us
    psum x1, waiting for transfers between devices, spread(): return lax.psum(block, axis)  139 us
    reduce_scatter x1, waiting for transfers between devices, per_device(): lax.psum_scatter(smoothed, 'orb', scatter_dimension=2, tiled=True)  98.1 us
    ppermute x3, starting transfers between devices, extended(): lax.ppermute(lax.slice_in_dim(block, block.shape[dim] - width, None, axis...  17.3 us
    dot_general x3, matrix products, per_device(): jnp.einsum('kw,kc->wc', coeff_b, blocks, preferred_element_type=jnp.float32)  13.9 us
    dot_general x3, matrix products, per_device(): jnp.einsum('kc,wc->kw', blocks, resid_b, preferred_element_type=jnp.float32)  13.5 us
    all_to_all x1, blocking collectives, per_device(): lax.all_to_all(raw_part, 'dom', split_axis=1, concat_axis=0, tiled=True)  13.4 us
    reshape x1, local copies, waits for them, and re-layouts, per_device(): blocks = jnp.stack(received).reshape(nproj * blk_rows, cells)  13.3 us
  transfers between devices with their start and end apart: 8, of which 8 were waited for; matrix products, arithmetic and copies ran while one was open for 0% of the time, Pallas kernels for 0%

commit v1 on v0

v1 whole, which is shorter than its diff:
```python
import functools
import math

import jax
import jax.numpy as jnp
from jax import lax
from jax.experimental import pallas as pl
from jax.experimental.pallas import tpu as pltpu
from jax.sharding import PartitionSpec as P

ITERS = 3
VMEM_LIMIT = 40 * 1024 * 1024
NT = (((1,), (1,)), ((), ()))


def project(resid_b, blocks, part_ref, scale):
    start = 0
    for ref in blocks:
        rows = ref.shape[0]
        part_ref[:, start : start + rows] = (
            lax.dot_general(resid_b, ref[...], NT, preferred_element_type=jnp.float32) * scale
        )
        start += rows


def first_kernel(scale, rhs_ref, *refs):
    *blocks, part_ref = refs
    project(rhs_ref[...].astype(jnp.bfloat16), blocks, part_ref, scale)


def resid_kernel(scale, row, x_ref, sib_ref, off_ref, rhs_ref, diag_ref, *refs):
    *blocks, resid_ref, part_ref, rb_ref = refs
    cells = x_ref.shape[1]
    lane = lax.broadcasted_iota(jnp.int32, (x_ref.shape[0], row), 1)
    for at in range(0, cells, row):
        here = slice(at, at + row)
        x = x_ref[:, here]
        beside = sib_ref[:, here].astype(jnp.float32) + off_ref[:, here].astype(jnp.float32)
        if at > 0:
            beside = beside + x_ref[:, at - row : at]
        if at + row < cells:
            beside = beside + x_ref[:, at + row : at + 2 * row]
        beside = beside + jnp.where(lane == 0, 0.0, pltpu.roll(x, 1, 1))
        beside = beside + jnp.where(lane == row - 1, 0.0, pltpu.roll(x, row - 1, 1))
        resid = rhs_ref[:, here] - (diag_ref[:, here] * x - 0.5 * beside)
        resid_ref[:, here] = resid
        rb_ref[:, here] = resid.astype(jnp.bfloat16)
    project(rb_ref[...], blocks, part_ref, scale)


def update_kernel(scale, tile, has_x, last, coeff_ref, resid_ref, diag_ref, *refs):
    refs = list(refs)
    x_ref = refs.pop(0) if has_x else None
    psi_ref = refs.pop(0) if last else None
    *blocks, out_ref, side_ref = refs
    cells = resid_ref.shape[1]
    for at in range(0, cells, tile):
        here = slice(at, at + tile)
        corr = 0.0
        start = 0
        for ref in blocks:
            rows = ref.shape[0]
            corr = corr + jnp.dot(
                coeff_ref[:, start : start + rows], ref[:, here], preferred_element_type=jnp.float32
            )
            start += rows
        x = (resid_ref[:, here] - corr * scale) / diag_ref[:, here]
        if has_x:
            x = x + x_ref[:, here]
        out_ref[:, here] = x
        if last:
            side_ref[:, here] = jnp.sum(x * psi_ref[:, here].astype(jnp.float32), axis=0, keepdims=True)
        else:
            side_ref[:, here] = x.astype(jnp.bfloat16)


def call(kernel, out_shape, scratch=()):
    return pl.pallas_call(
        kernel,
        out_shape=out_shape,
        scratch_shapes=scratch,
        compiler_params=pltpu.CompilerParams(vmem_limit_bytes=VMEM_LIMIT),
    )


def per_device(rhs, potential, eigen_table, win_index, occupied, block_ids, psi_win, smoother):
    local_orbs, planes, rows_y, rows_z = rhs.shape
    n_dom = lax.axis_size("dom")
    n_orb = lax.axis_size("orb")
    cells = rows_y * rows_z
    wide = 2 * local_orbs
    width = local_orbs * n_orb
    scale = 1.0 / math.sqrt(planes * n_dom * rows_y * rows_z)
    n_occ = eigen_table.shape[0]
    per_dev, blk_rows = occupied.shape[:2]
    nproj = block_ids.shape[0]
    chips = n_orb // 2
    ring = chips // 2
    share = blk_rows // chips
    o = lax.axis_index("orb")
    core = o % 2
    chip = o // 2
    low = core == 0
    groups = [[2 * k + c for k in range(chips)] for c in range(2)]

    def chip_perm(target):
        return [(2 * k + c, 2 * target(k) + c) for k in range(chips) for c in range(2)]

    swap_core = [(i, i ^ 1) for i in range(n_orb)]
    swap_x = chip_perm(lambda k: (k + ring) % chips)
    up_y = chip_perm(lambda k: k // ring * ring + (k + 1) % ring)
    down_y = chip_perm(lambda k: k // ring * ring + (k - 1) % ring)

    def permute(value, pairs):
        return lax.ppermute(value, "orb", pairs)

    def pair(own, other):
        return jnp.concatenate([jnp.where(low, own, other), jnp.where(low, other, own)], axis=0)

    def plane_of(slot, plane):
        got = lax.dynamic_slice(
            occupied, (slot, 0, plane, 0, 0), (1, blk_rows, 1, rows_y, rows_z)
        )
        return got.reshape(blk_rows, rows_y, rows_z)

    last_id = per_dev * n_orb - 1
    middle = jnp.logical_and(block_ids != 0, block_ids != last_id)
    rank = jnp.cumsum(middle.astype(jnp.int32)) - 1
    mids = [jnp.sum(jnp.where(jnp.logical_and(middle, rank == k), block_ids, 0)) for k in range(nproj - 2)]
    order = jnp.where(block_ids == 0, 0, jnp.where(block_ids == last_id, 1, 2 + rank))

    ends = jnp.logical_or(o == 0, o == n_orb - 1)
    over = permute(plane_of(core * (per_dev - 1), 1 - core), [(0, 1), (n_orb - 1, n_orb - 2)])
    fixed = jnp.where(ends, plane_of(core * (per_dev - 1), core), over)
    fixed = fixed.reshape(chips, share, rows_y, rows_z)
    at_zero = fixed[0]
    at_last = fixed[chips - 1]
    for s in range(1, chips):
        piece = lax.dynamic_index_in_dim(fixed, jnp.where(chip == 0, s, chips - 1 - s), 0, keepdims=False)
        pairs = [(c, 2 * s + c) for c in range(2)]
        pairs += [(n_orb - 2 + c, 2 * (chips - 1 - s) + c) for c in range(2)]
        got = permute(piece, pairs)
        at_zero = jnp.where(chip == s, got, at_zero)
        at_last = jnp.where(chip == chips - 1 - s, got, at_last)
    ends_share = jnp.concatenate([at_zero, at_last], axis=0).reshape(2 * share, cells)
    blocks_ends = lax.all_gather(ends_share, "orb", axis_index_groups=groups, tiled=True)

    offers = []
    for mid in mids:
        slot = mid % per_dev
        owner_core = (mid // per_dev) % 2
        other = permute(plane_of(slot, 1 - core), swap_core)
        offer = jnp.where(owner_core == core, plane_of(slot, core), other)
        offers.append(offer.reshape(chips, share, rows_y, rows_z))
    offered = lax.all_to_all(
        jnp.stack(offers, axis=1), "orb", 0, 0, axis_index_groups=groups, tiled=True
    )
    shares = []
    for k, mid in enumerate(mids):
        got = lax.dynamic_index_in_dim(offered[:, k], mid // (2 * per_dev), 0, keepdims=False)
        shares.append(got.reshape(share, cells))

    half = share // 2
    pieces = []
    places = []
    own = jnp.concatenate([shares[0], permute(shares[0], swap_x)], axis=0)
    above = permute(own, up_y)
    below = permute(own, down_y)
    far0 = permute(above[:share], up_y)
    far1 = permute(below[share:], down_y)
    pieces += [own, above, below, far0, far1]
    places += [(0, 0, 0), (0, 0, 1), (0, -1, 0), (0, -1, 1), (0, 1, 0), (0, 1, 1), (0, 2, 0), (0, 2, 1)]
    own = shares[1]
    above = permute(own, up_y)
    below = permute(own, down_y)
    far0 = permute(above[:half], up_y)
    far1 = permute(below[half:], down_y)
    line = jnp.concatenate([own, above, below], axis=0)
    far = jnp.concatenate([far0, far1], axis=0)
    pieces += [line, far, permute(line, swap_x), permute(far, swap_x)]
    places += [(1, dy, rx) for rx in range(2) for dy in (0, -1, 1, 2)]
    blocks_mid = jnp.concatenate(pieces, axis=0)
    blocks = [blocks_ends, blocks_mid]
    n_rows = nproj * blk_rows

    def both(field):
        mine = lax.dynamic_index_in_dim(field, core, 1, keepdims=False).reshape(local_orbs, cells)
        send = lax.dynamic_index_in_dim(field, 1 - core, 1, keepdims=False).reshape(local_orbs, cells)
        return pair(mine, permute(send, swap_core))

    picks = win_index[:, None] == jnp.arange(n_occ, dtype=jnp.int32)[None, :]
    eps = jnp.sum(jnp.where(picks, eigen_table[None, :], 0.0), axis=1)[:, None]
    eps = pair(eps, permute(eps, swap_core))
    plane_pot = lax.dynamic_index_in_dim(potential, core, 0, keepdims=True).reshape(1, cells)
    diag = 3.0 + plane_pot - eps
    rhs_wide = both(rhs)
    psi_wide = both(psi_win)

    part_shape = jax.ShapeDtypeStruct((wide, n_rows), jnp.float32)
    field_shape = jax.ShapeDtypeStruct((wide, cells), jnp.float32)
    halo_shape = jax.ShapeDtypeStruct((wide, cells), jnp.bfloat16)
    row_shape = jax.ShapeDtypeStruct((1, cells), jnp.float32)

    def total(part):
        first, second = part[:local_orbs], part[local_orbs:]
        mine = jnp.where(low, first, second) + permute(jnp.where(low, second, first), swap_core)
        spread = jnp.broadcast_to(mine.astype(jnp.bfloat16)[None], (n_dom,) + mine.shape)
        got = lax.all_to_all(spread, "dom", 0, 0, tiled=True)
        coeff = jnp.sum(got.astype(jnp.float32), axis=0)
        coeff_b = coeff.astype(jnp.bfloat16)
        return coeff, pair(coeff_b, permute(coeff_b, swap_core))

    across = []
    for d in range(n_dom - 1):
        for k in range(chips):
            left, right = d * n_orb + 2 * k + 1, (d + 1) * n_orb + 2 * k
            across += [(left, right), (right, left)]

    x = None
    for step in range(ITERS):
        if step == 0:
            resid = rhs_wide
            part = call(functools.partial(first_kernel, scale), part_shape)(rhs_wide, *blocks)
        else:
            sib = permute(x_b, swap_core)
            off = lax.ppermute(x_b, ("dom", "orb"), across)
            resid, part = call(
                functools.partial(resid_kernel, scale, rows_z),
                (field_shape, part_shape),
                (pltpu.VMEM((wide, cells), jnp.bfloat16),),
            )(x, sib, off, rhs_wide, diag, *blocks)
        coeff, coeff_b = total(part)
        final = step == ITERS - 1
        extra = ([x] if step else []) + ([psi_wide] if final else [])
        x, x_b = call(
            functools.partial(update_kernel, scale, 512, step > 0, final),
            (field_shape, row_shape if final else halo_shape),
        )(coeff_b, resid, diag, *extra, *blocks)

    raw = (x_b / math.sqrt(width)).reshape(n_dom, 1, rows_y // n_dom, rows_z)
    raw = jnp.broadcast_to(raw, (n_dom, n_orb) + raw.shape[2:])
    raw = raw.reshape(n_dom * n_orb, -1)
    terms = lax.all_to_all(raw, ("dom", "orb"), 0, 0, tiled=True)
    terms = jnp.sum(terms.reshape(n_dom, chips, 2, -1), axis=1).reshape(2 * n_dom, -1)
    smoothed = jnp.dot(smoother, terms, precision=lax.Precision.HIGHEST)
    smoothed = smoothed.reshape(2 * n_dom, rows_y // n_dom, rows_z)
    z_part = rows_z // n_orb
    gradient = lax.dynamic_slice_in_dim(smoothed, o * z_part, z_part, axis=2)

    first, second = x[:local_orbs], x[local_orbs:]
    mine = jnp.where(low, first, second)
    other = permute(jnp.where(low, second, first), swap_core)
    solution = jnp.stack([jnp.where(low, mine, other), jnp.where(low, other, mine)], axis=1)
    solution = solution.reshape(rhs.shape)

    table = coeff.T
    ends_rows = table[: 2 * blk_rows].reshape(chips, 2, share, local_orbs)
    mid_rows = table[2 * blk_rows :].reshape(len(places), share, local_orbs)
    y_of, x_of = chip % ring, chip // ring
    where_from = []
    for k in range(nproj - 2):
        for q in range(chips):
            index = jnp.int32(0)
            for i, (blk, dy, rx) in enumerate(places):
                if blk == k:
                    hit = jnp.logical_and((y_of + dy) % ring == q % ring, (x_of + rx) % 2 == q // ring)
                    index = jnp.where(hit, i, index)
            where_from.append(index)
    mid_rows = jnp.take(mid_rows, jnp.stack(where_from), axis=0)
    mid_rows = mid_rows.reshape(nproj - 2, blk_rows, local_orbs)
    ends_rows = ends_rows.transpose(1, 0, 2, 3).reshape(2, blk_rows, local_orbs)
    correlations = jnp.take(jnp.concatenate([ends_rows, mid_rows], axis=0), order, axis=0)
    return (solution, correlations, gradient)


def solution(mesh):
    return jax.shard_map(
        per_device,
        mesh=mesh,
        in_specs=(
            P("orb", "dom", None, None),
            P("dom", None, None),
            P(),
            P("orb"),
            P("orb", None, "dom", None, None),
            P(),
            P("orb", "dom", None, None),
            P(),
        ),
        out_specs=(P("orb", "dom", None, None), P(None, None, "orb"), P(None, "dom", "orb")),
        check_vma=False,
    )
```

time: 553 us -> 253 us (0.46)
  blocking collectives: 200 us -> 0 us
  waiting for transfers between devices: 244 us -> 107 us
  starting transfers between devices: 21.4 us -> 80.7 us
  matrix products: 27.6 us -> 0.16 us
  local copies, waits for them, and re-layouts: 14.9 us -> 23.1 us
  Pallas kernels: 0 us -> 5.6 us
    psum x3 -> x0, blocking collectives: 186 us -> none  [per_device(): project_coeff = lax.psum(part, 'dom')]
    psum x1 -> x0, waiting for transfers between devices: 139 us -> none  [spread(): return lax.psum(block, axis)]
    reduce_scatter x1 -> x0, waiting for transfers between devices: 98.1 us -> none  [per_device(): lax.psum_scatter(smoothed, 'orb', scatter_dimension=2, tiled=True)]
    all_to_all x0 -> x5, waiting for transfers between devices: none -> 42.9 us  [the longest x3 29 us: total(): got = lax.all_to_all(spread, 'dom', 0, 0, tiled=True)]
    ppermute x6 -> x35, waiting for transfers between devices: 7.08 us -> 49.5 us  [the longest x33 41.9 us: permute(): return lax.ppermute(value, 'orb', pairs)]
    ppermute x6 -> x35, starting transfers between devices: 21.3 us -> 55.1 us  [the longest x33 50.3 us: permute(): return lax.ppermute(value, 'orb', pairs)]
    dot_general x7 -> x1, matrix products: 27.6 us -> 0.16 us  [per_device(): smoothed = jnp.dot(smoother, terms, precision=lax.Precision.HIGHEST)]
    all_to_all x0 -> x5, starting transfers between devices: none -> 25.6 us  [the longest x3 16.7 us: total(): got = lax.all_to_all(spread, 'dom', 0, 0, tiled=True)]
  transfers between devices with their start and end apart: 8 -> 41, of which waited for: 8 -> 21; matrix products, arithmetic and copies ran while one was open for 0% -> 8% of each run, Pallas kernels for 0% -> 1%
where the time goes in v1:
time: 253 us; the launch traced here: 252 us
  waiting for transfers between devices  107 us (42%)
  starting transfers between devices  80.7 us (32%)
  local copies, waits for them, and re-layouts  23.1 us (9%)
  between operations  20.2 us (8%)
  other arithmetic  15 us (6%)
  Pallas kernels  5.6 us (2%)
    ppermute x33, starting transfers between devices, permute(): return lax.ppermute(value, 'orb', pairs)  50.3 us
    ppermute x33, waiting for transfers between devices, permute(): return lax.ppermute(value, 'orb', pairs)  41.9 us
    all_to_all x3, waiting for transfers between devices, total(): got = lax.all_to_all(spread, 'dom', 0, 0, tiled=True)  29 us
    all_to_all x3, starting transfers between devices, total(): got = lax.all_to_all(spread, 'dom', 0, 0, tiled=True)  16.7 us
    all_gather x1, waiting for transfers between devices, per_device(): lax.all_gather(ends_share, 'orb', axis_index_groups=groups, tiled=True)  14.6 us
    all_to_all x1, waiting for transfers between devices, per_device(): terms = lax.all_to_all(raw, ('dom', 'orb'), 0, 0, tiled=True)  13.9 us
    unnamed x48, local copies, waits for them, and re-layouts  10.5 us
    ppermute x2, waiting for transfers between devices, per_device(): off = lax.ppermute(x_b, ('dom', 'orb'), across)  7.61 us
  transfers between devices with their start and end apart: 41, of which 21 were waited for; matrix products, arithmetic and copies ran while one was open for 8% of the time, Pallas kernels for 1%

profile of v1, /device:TPU:1, one launch (start us, length us, event | category | flops | bytes accessed | tf_op | source)
XLA Modules:
  0.0 251.8 jit_solution(9199457328485268943)
XLA Ops:
  8.0 1.3 fusion.15
  13.3 3.7 %dynamic-slice_bitcast_fusion.1 = (bf16[128,32,128]{2,1,0:T(8,128)(2,1)S(1)}, bf16[128,32,128]{2,1,0:T(8,128)(2,1)}, bf16[128,32,128]{2,1,0:T(8,128)(2,1)S(1)}) fusion(bf16[2,128,2,32,128]{4,3,2,1,0:T(8,128)(2,1)} %param.12, s32[]{:T(128)S(6)} %select_n.1298, s32[]{:T(128)S(6)} %select_n.1258, s32[]{:T(128)S(6)} %select_n.1257, s32[]{:T(128)S(6)} %select_n.1305), kind=kLoop, calls=%fused_computation.8 | loop fusion | bytes 6291472 | tf_op jit(solution)/shard_map/reshape | solution.py:124
  18.3 4.2 %collective-permute-start.10 = (bf16[128,32,128]{2,1,0:T(8,128)(2,1)S(1)}, bf16[128,32,128]{2,1,0:T(8,128)(2,1)}, u32[]{:S(2)}, u32[]{:S(2)}) collective-permute-start(bf16[128,32,128]{2,1,0:T(8,128)(2,1)S(1)} %get-tuple-element.32), channel_id=1, source_target_pairs={{0,1},{1,0},{2,3},{3,2},{4,5},{5,4},{6,7},{7,6},{8,9},{9,8},{10,11... | collective-permute-start | bytes 3145736 | tf_op jit(solution)/shard_map/ppermute | solution.py:115
  25.2 1.7 collective-permute-done.9
  26.9 3.6 %bitcast_select_fusion.1 = (bf16[128,32,128]{2,1,0:T(8,128)(2,1)S(1)}, bf16[128,32,128]{2,1,0:T(8,128)(2,1)}, bf16[128,32,128]{2,1,0:T(8,128)(2,1)S(1)}) fusion(bf16[128,32,128]{2,1,0:T(8,128)(2,1)} %collective-permute-done.9, bf16[2,128,2,32,128]{4,3,2,1,0:T(8,128)(2,1)} %param.12, s32[]{:T(128)S(6)} %select_n.1298, s32[]{:T(128)S(6)} %select_n.1257, ...), kind=kLoop, calls=%fused_computation.5 | loop fusion | flops 1572864 | bytes 9437199 | tf_op jit(solution)/shard_map/jit(_where)/select_n | solution.py:153
  30.5 1.6 pad_maximum_fusion
  32.0 3.7 %all-to-all-start = ((bf16[8,2,16,32,128]{4,3,2,1,0:T(8,128)(2,1)}), bf16[8,2,16,32,128]{4,3,2,1,0:T(8,128)(2,1)S(1)}, u32[]{:S(2)}, u32[]{:S(2)}) async-start(bf16[8,2,16,32,128]{4,3,2,1,0:T(8,128)(2,1)} %pad_maximum_fusion), calls=%async_computation | async-start | bytes 4194304 | tf_op jit(solution)/shard_map/all_to_all | solution.py:155
  35.8 1.3 dynamic-slice_bitcast_fusion.3
  37.1 5.4 %collective-permute-start.2 = (bf16[16,32,128]{2,1,0:T(8,128)(2,1)S(1)}, bf16[16,32,128]{2,1,0:T(8,128)(2,1)S(1)}, u32[]{:S(2)}, u32[]{:S(2)}) collective-permute-start(bf16[16,32,128]{2,1,0:T(8,128)(2,1)S(1)} %get-tuple-element.43), channel_id=1, source_target_pairs={{0,14},{1,15},{14,0},{15,1},{16,30},{17,31},{30,16},{31,17},{32,46... | collective-permute-start | bytes 393224 | tf_op jit(solution)/shard_map/ppermute | solution.py:115
  42.5 1.3 collective-permute-start.3
  44.0 1.3 collective-permute-start.4
  45.3 1.3 collective-permute-start.5
  46.6 1.3 collective-permute-start.6
  47.9 16.3 %collective-permute-done.2 = bf16[16,32,128]{2,1,0:T(8,128)(2,1)S(1)} collective-permute-done((bf16[16,32,128]{2,1,0:T(8,128)(2,1)S(1)}, bf16[16,32,128]{2,1,0:T(8,128)(2,1)S(1)}, u32[]{:S(2)}, u32[]{:S(2)}) %collective-permute-start.2) | collective-permute-done | bytes 131104 | tf_op jit(solution)/shard_map/ppermute | solution.py:115
  65.5 4.0 %collective-permute-start.8 = (bf16[16,32,128]{2,1,0:T(8,128)(2,1)S(1)}, bf16[16,32,128]{2,1,0:T(8,128)(2,1)S(1)}, u32[]{:S(2)}, u32[]{:S(2)}) collective-permute-start(bf16[16,32,128]{2,1,0:T(8,128)(2,1)S(1)} %get-tuple-element.37), channel_id=1, source_target_pairs={{0,2},{1,3},{14,12},{15,13},{16,18},{17,19},{30,28},{31,29},{32,34... | collective-permute-start | bytes 393224 | tf_op jit(solution)/shard_map/ppermute | solution.py:115
  69.5 5.1 %collective-permute-start.24 = (f32[8,1]{0,1:T(1,128)S(1)}, f32[8,1]{0,1:T(1,128)S(1)}, u32[]{:S(2)}, u32[]{:S(2)}) collective-permute-start(f32[8,1]{0,1:T(1,128)S(1)} %bitcast.174), channel_id=1, source_target_pairs={{0,1},{1,0},{2,3},{3,2},{4,5},{5,4},{6,7},{7,6},{8,9},{9,8},{10,11... | collective-permute-start | bytes 104 | tf_op jit(solution)/shard_map/ppermute | solution.py:115
  77.1 2.7 %collective-permute-start.17 = (bf16[16,4096]{1,0:T(8,128)(2,1)S(1)}, bf16[16,4096]{1,0:T(8,128)(2,1)S(1)}, u32[]{:S(2)}, u32[]{:S(2)}) collective-permute-start(bf16[16,4096]{1,0:T(8,128)(2,1)S(1)} %bitcast.166), channel_id=1, source_target_pairs={{0,6},{1,7},{2,0},{3,1},{4,2},{5,3},{6,4},{7,5},{8,14},{9,15},{10,... | collective-permute-start | bytes 393224 | tf_op jit(solution)/shard_map/ppermute | solution.py:115
  80.0 4.0 %collective-permute-done.11 = bf16[16,4096]{1,0:T(8,128)(2,1)S(1)} collective-permute-done((bf16[16,4096]{1,0:T(8,128)(2,1)S(1)}, bf16[16,4096]{1,0:T(8,128)(2,1)S(1)}, u32[]{:S(2)}, u32[]{:S(2)}) %collective-permute-start.11) | collective-permute-done | bytes 131104 | tf_op jit(solution)/shard_map/ppermute | solution.py:115
  84.1 2.7 %collective-permute-start.13 = (bf16[32,4096]{1,0:T(8,128)(2,1)S(1)}, bf16[32,4096]{1,0:T(8,128)(2,1)S(1)}, u32[]{:S(2)}, u32[]{:S(2)}) collective-permute-start(bf16[32,4096]{1,0:T(8,128)(2,1)S(1)} %get-tuple-element.54), channel_id=1, source_target_pairs={{0,6},{1,7},{2,0},{3,1},{4,2},{5,3},{6,4},{7,5},{8,14},{9,15},{10,... | collective-permute-start | bytes 786440 | tf_op jit(solution)/shard_map/ppermute | solution.py:115
  86.9 2.7 %collective-permute-start.19 = (bf16[8,4096]{1,0:T(8,128)(2,1)S(1)}, bf16[8,4096]{1,0:T(8,128)(2,1)S(1)}, u32[]{:S(2)}, u32[]{:S(2)}) collective-permute-start(bf16[8,4096]{1,0:T(8,128)(2,1)S(1)} %slice.85), channel_id=1, source_target_pairs={{0,6},{1,7},{2,0},{3,1},{4,2},{5,3},{6,4},{7,5},{8,14},{9,15},{10,... | collective-permute-start | bytes 196616 | tf_op jit(solution)/shard_map/ppermute | solution.py:115
  89.7 1.6 collective-permute-done.18
  91.3 1.7 collective-permute-start.21
  93.1 2.7 %collective-permute-start.15 = (bf16[16,4096]{1,0:T(8,128)(2,1)S(1)}, bf16[16,4096]{1,0:T(8,128)(2,1)S(1)}, u32[]{:S(2)}, u32[]{:S(2)}) collective-permute-start(bf16[16,4096]{1,0:T(8,128)(2,1)S(1)} %slice.82), channel_id=1, source_target_pairs={{0,6},{1,7},{2,0},{3,1},{4,2},{5,3},{6,4},{7,5},{8,14},{9,15},{10,... | collective-permute-start | bytes 393224 | tf_op jit(solution)/shard_map/ppermute | solution.py:115
  95.9 4.9 %collective-permute-done.14 = bf16[16,4096]{1,0:T(8,128)(2,1)S(1)} collective-permute-done((bf16[16,4096]{1,0:T(8,128)(2,1)S(1)}, bf16[16,4096]{1,0:T(8,128)(2,1)S(1)}, u32[]{:S(2)}, u32[]{:S(2)}) %collective-permute-start.14) | collective-permute-done | bytes 131104 | tf_op jit(solution)/shard_map/ppermute | solution.py:115
  101.7 4.0 %collective-permute-done.20 = bf16[48,4096]{1,0:T(8,128)(2,1)S(1)} collective-permute-done((bf16[48,4096]{1,0:T(8,128)(2,1)S(1)}, bf16[48,4096]{1,0:T(8,128)(2,1)S(1)}, u32[]{:S(2)}, u32[]{:S(2)}) %collective-permute-start.20) | collective-permute-done | bytes 393248 | tf_op jit(solution)/shard_map/ppermute | solution.py:115
  105.7 5.5 %collective-permute-done.21 = bf16[16,4096]{1,0:T(8,128)(2,1)S(1)} collective-permute-done((bf16[16,4096]{1,0:T(8,128)(2,1)S(1)}, bf16[16,4096]{1,0:T(8,128)(2,1)S(1)}, u32[]{:S(2)}, u32[]{:S(2)}) %collective-permute-start.21) | collective-permute-done | bytes 131104 | tf_op jit(solution)/shard_map/ppermute | solution.py:115
  111.2 14.6 %all-gather.2.cloned.1.call-done.refs_0_.refs_1_.refs_2_ = bf16[256,4096]{1,0:T(8,128)(2,1)} async-done(((bf16[32,4096]{1,0:T(8,128)(2,1)}), bf16[256,4096]{1,0:T(8,128)(2,1)}) %all-gather.2.cloned.1.call-update) | async-done | bytes 2097168 | tf_op jit(solution)/shard_map/all_gather | solution.py:146
  125.8 1.6 copy-done.1
  128.6 2.2 collective-permute-start.22
  132.3 8.6 %all-to-all-start.1 = ((bf16[16,8,512]{2,1,0:T(8,128)(2,1)}), bf16[16,8,512]{2,1,0:T(8,128)(2,1)S(1)}, u32[]{:S(2)}, u32[]{:S(2)}) async-start(bf16[16,8,512]{2,1,0:T(8,128)(2,1)} %broadcast_in_dim.75), calls=%async_computation.1 | async-start | bytes 262144 | tf_op jit(solution)/shard_map/all_to_all | solution.py:208
  141.1 9.9 %all-to-all-done.1 = bf16[16,8,512]{2,1,0:T(8,128)(2,1)S(1)} async-done(((bf16[16,8,512]{2,1,0:T(8,128)(2,1)}), bf16[16,8,512]{2,1,0:T(8,128)(2,1)S(1)}, u32[]{:S(2)}, u32[]{:S(2)}) %all-to-all-start.1) | async-done | bytes 131104 | tf_op jit(solution)/shard_map/all_to_all | solution.py:208
  151.0 2.1 collective-permute-start.23
  154.0 1.6 copy-done.2
  156.6 2.4 collective-permute-start.26
  159.0 5.4 %collective-permute-done.26.off_ref = bf16[16,4096]{1,0:T(8,128)(2,1)S(1)} collective-permute-done((bf16[16,4096]{1,0:T(8,128)(2,1)S(1)}, bf16[16,4096]{1,0:T(8,128)(2,1)S(1)}, u32[]{:S(2)}, u32[]{:S(2)}) %collective-permute-start.26) | collective-permute-done | bytes 131104 | tf_op jit(solution)/shard_map/ppermute | solution.py:226
  168.4 4.0 %all-to-all-start.2 = ((bf16[16,8,512]{2,1,0:T(8,128)(2,1)}), bf16[16,8,512]{2,1,0:T(8,128)(2,1)S(1)}, u32[]{:S(2)}, u32[]{:S(2)}) async-start(bf16[16,8,512]{2,1,0:T(8,128)(2,1)} %broadcast_in_dim.79), calls=%async_computation.2 | async-start | bytes 262144 | tf_op jit(solution)/shard_map/all_to_all | solution.py:208
  173.6 8.9 %all-to-all-done.2 = bf16[16,8,512]{2,1,0:T(8,128)(2,1)S(1)} async-done(((bf16[16,8,512]{2,1,0:T(8,128)(2,1)}), bf16[16,8,512]{2,1,0:T(8,128)(2,1)S(1)}, u32[]{:S(2)}, u32[]{:S(2)}) %all-to-all-start.2) | async-done | bytes 131104 | tf_op jit(solution)/shard_map/all_to_all | solution.py:208
  182.6 2.0 collective-permute-start.28
  185.4 1.6 copy-done.3
  188.1 2.4 collective-permute-start.30
  193.6 2.3 collective-permute-done.30.off_ref
  195.9 1.6 copy-done.4
  200.7 4.0 %all-to-all-start.3 = ((bf16[16,8,512]{2,1,0:T(8,128)(2,1)}), bf16[16,8,512]{2,1,0:T(8,128)(2,1)S(1)}, u32[]{:S(2)}, u32[]{:S(2)}) async-start(bf16[16,8,512]{2,1,0:T(8,128)(2,1)} %broadcast_in_dim.80), calls=%async_computation.3 | async-start | bytes 262144 | tf_op jit(solution)/shard_map/all_to_all | solution.py:208
  204.7 10.2 %all-to-all-done.3 = bf16[16,8,512]{2,1,0:T(8,128)(2,1)S(1)} async-done(((bf16[16,8,512]{2,1,0:T(8,128)(2,1)}), bf16[16,8,512]{2,1,0:T(8,128)(2,1)S(1)}, u32[]{:S(2)}, u32[]{:S(2)}) %all-to-all-start.3) | async-done | bytes 131104 | tf_op jit(solution)/shard_map/all_to_all | solution.py:208
  216.1 2.1 collective-permute-start.32
  219.1 1.6 copy-done.5
  222.6 5.2 %all-to-all-start.4 = ((f32[256,1,256]{2,1,0:T(1,128)}), f32[256,1,256]{2,1,0:T(1,128)S(1)}, u32[]{:S(2)}, u32[]{:S(2)}) async-start(f32[256,1,256]{2,1,0:T(1,128)} %bitcast.61), calls=%async_computation.4 | async-start | bytes 524288 | tf_op jit(solution)/shard_map/all_to_all | solution.py:243
  229.3 13.9 %all-to-all-done.4 = f32[256,1,256]{2,1,0:T(1,128)S(1)} async-done(((f32[256,1,256]{2,1,0:T(1,128)}), f32[256,1,256]{2,1,0:T(1,128)S(1)}, u32[]{:S(2)}, u32[]{:S(2)}) %all-to-all-start.4) | async-done | bytes 262176 | tf_op jit(solution)/shard_map/all_to_all | solution.py:243
  (174 shorter events, 34.0 us)
Async XLA Ops:
  7.2 236.9 %copy-start = (f32[32,32]{1,0:T(8,128)S(1)}, f32[32,32]{1,0:T(8,128)}, u32[]{:S(2)}) copy-start(f32[32,32]{1,0:T(8,128)} %param.15) | copy-start | bytes 12292
  13.3 9.2 %copy-start.6 = (f32[8,2,32,128]{3,2,1,0:T(8,128)S(1)}, f32[8,2,32,128]{3,2,1,0:T(8,128)}, u32[]{:S(2)}) copy-start(f32[8,2,32,128]{3,2,1,0:T(8,128)} %param.8) | copy-start | bytes 786436
  13.3 11.3 %copy-start.9 = (f32[4096]{0:T(1024)S(1)}, f32[4096]{0:T(1024)}, u32[]{:S(2)}) copy-start(f32[4096]{0:T(1024)} %param.10) | copy-start | bytes 49156
  13.3 11.3 %copy-start.14 = (s32[8]{0:T(128)S(1)}, s32[8]{0:T(128)}, u32[]{:S(2)}) copy-start(s32[8]{0:T(128)} %param.11) | copy-start | bytes 100
  17.0 7.9 %collective-permute-start.1 = (bf16[128,32,128]{2,1,0:T(8,128)(2,1)}, bf16[128,32,128]{2,1,0:T(8,128)(2,1)}, u32[]{:S(2)}, u32[]{:S(2)}) collective-permute-start(bf16[128,32,128]{2,1,0:T(8,128)(2,1)} %get-tuple-element.31), channel_id=1, source_target_pairs={{0,1},{15,14},{16,17},{31,30},{32,33},{47,46},{48,49},{63,62},{64,... | collective-permute-start | bytes 3145736 | tf_op jit(solution)/shard_map/ppermute | solution.py:115
  18.3 6.9 %collective-permute-start.10 = (bf16[128,32,128]{2,1,0:T(8,128)(2,1)S(1)}, bf16[128,32,128]{2,1,0:T(8,128)(2,1)}, u32[]{:S(2)}, u32[]{:S(2)}) collective-permute-start(bf16[128,32,128]{2,1,0:T(8,128)(2,1)S(1)} %get-tuple-element.32), channel_id=1, source_target_pairs={{0,1},{1,0},{2,3},{3,2},{4,5},{5,4},{6,7},{7,6},{8,9},{9,8},{10,11... | collective-permute-start | bytes 3145736 | tf_op jit(solution)/shard_map/ppermute | solution.py:115
  22.4 4.5 %collective-permute-start.9 = (bf16[128,32,128]{2,1,0:T(8,128)(2,1)S(1)}, bf16[128,32,128]{2,1,0:T(8,128)(2,1)}, u32[]{:S(2)}, u32[]{:S(2)}) collective-permute-start(bf16[128,32,128]{2,1,0:T(8,128)(2,1)S(1)} %get-tuple-element.30), channel_id=1, source_target_pairs={{0,1},{1,0},{2,3},{3,2},{4,5},{5,4},{6,7},{7,6},{8,9},{9,8},{10,11... | collective-permute-start | bytes 3145736 | tf_op jit(solution)/shard_map/ppermute | solution.py:115
  22.6 21.3 %collective-permute-start = (f32[8,4096]{1,0:T(8,128)S(1)}, f32[8,4096]{1,0:T(8,128)S(1)}, u32[]{:S(2)}, u32[]{:S(2)}) collective-permute-start(f32[8,4096]{1,0:T(8,128)S(1)} %bitcast.171), channel_id=1, source_target_pairs={{0,1},{1,0},{2,3},{3,2},{4,5},{5,4},{6,7},{7,6},{8,9},{9,8},{10,11... | collective-permute-start | bytes 393224 | tf_op jit(solution)/shard_map/ppermute | solution.py:115
  32.0 44.5 %all-to-all-start = ((bf16[8,2,16,32,128]{4,3,2,1,0:T(8,128)(2,1)}), bf16[8,2,16,32,128]{4,3,2,1,0:T(8,128)(2,1)S(1)}, u32[]{:S(2)}, u32[]{:S(2)}) async-start(bf16[8,2,16,32,128]{4,3,2,1,0:T(8,128)(2,1)} %pad_maximum_fusion), calls=%async_computation | async-start | bytes 4194304 | tf_op jit(solution)/shard_map/all_to_all | solution.py:155
  35.7 90.1 %all-gather.2.cloned.1.call-start = ((), (), s32[]{:S(2)}) async-start(), calls=%async_computation.5 | async-start | bytes 2359296 | tf_op jit(solution)/shard_map/all_gather | solution.py:146
  37.1 27.0 %collective-permute-start.2 = (bf16[16,32,128]{2,1,0:T(8,128)(2,1)S(1)}, bf16[16,32,128]{2,1,0:T(8,128)(2,1)S(1)}, u32[]{:S(2)}, u32[]{:S(2)}) collective-permute-start(bf16[16,32,128]{2,1,0:T(8,128)(2,1)S(1)} %get-tuple-element.43), channel_id=1, source_target_pairs={{0,14},{1,15},{14,0},{15,1},{16,30},{17,31},{30,16},{31,17},{32,46... | collective-permute-start | bytes 393224 | tf_op jit(solution)/shard_map/ppermute | solution.py:115
  42.5 22.9 %collective-permute-start.3 = (bf16[16,32,128]{2,1,0:T(8,128)(2,1)S(1)}, bf16[16,32,128]{2,1,0:T(8,128)(2,1)S(1)}, u32[]{:S(2)}, u32[]{:S(2)}) collective-permute-start(bf16[16,32,128]{2,1,0:T(8,128)(2,1)S(1)} %get-tuple-element.42), channel_id=1, source_target_pairs={{0,12},{1,13},{14,2},{15,3},{16,28},{17,29},{30,18},{31,19},{32,44... | collective-permute-start | bytes 393224 | tf_op jit(solution)/shard_map/ppermute | solution.py:115
  44.0 25.5 %collective-permute-start.4 = (bf16[16,32,128]{2,1,0:T(8,128)(2,1)S(1)}, bf16[16,32,128]{2,1,0:T(8,128)(2,1)S(1)}, u32[]{:S(2)}, u32[]{:S(2)}) collective-permute-start(bf16[16,32,128]{2,1,0:T(8,128)(2,1)S(1)} %get-tuple-element.41), channel_id=1, source_target_pairs={{0,10},{1,11},{14,4},{15,5},{16,26},{17,27},{30,20},{31,21},{32,42... | collective-permute-start | bytes 393224 | tf_op jit(solution)/shard_map/ppermute | solution.py:115
  45.3 29.3 %collective-permute-start.5 = (bf16[16,32,128]{2,1,0:T(8,128)(2,1)S(1)}, bf16[16,32,128]{2,1,0:T(8,128)(2,1)S(1)}, u32[]{:S(2)}, u32[]{:S(2)}) collective-permute-start(bf16[16,32,128]{2,1,0:T(8,128)(2,1)S(1)} %get-tuple-element.40), channel_id=1, source_target_pairs={{0,8},{1,9},{14,6},{15,7},{16,24},{17,25},{30,22},{31,23},{32,40},... | collective-permute-start | bytes 393224 | tf_op jit(solution)/shard_map/ppermute | solution.py:115
  46.6 28.0 %collective-permute-start.6 = (bf16[16,32,128]{2,1,0:T(8,128)(2,1)S(1)}, bf16[16,32,128]{2,1,0:T(8,128)(2,1)S(1)}, u32[]{:S(2)}, u32[]{:S(2)}) collective-permute-start(bf16[16,32,128]{2,1,0:T(8,128)(2,1)S(1)} %get-tuple-element.39), channel_id=1, source_target_pairs={{0,6},{1,7},{14,8},{15,9},{16,22},{17,23},{30,24},{31,25},{32,38},... | collective-permute-start | bytes 393224 | tf_op jit(solution)/shard_map/ppermute | solution.py:115
  64.2 10.4 %collective-permute-start.7 = (bf16[16,32,128]{2,1,0:T(8,128)(2,1)S(1)}, bf16[16,32,128]{2,1,0:T(8,128)(2,1)S(1)}, u32[]{:S(2)}, u32[]{:S(2)}) collective-permute-start(bf16[16,32,128]{2,1,0:T(8,128)(2,1)S(1)} %get-tuple-element.38), channel_id=1, source_target_pairs={{0,4},{1,5},{14,10},{15,11},{16,20},{17,21},{30,26},{31,27},{32,36... | collective-permute-start | bytes 393224 | tf_op jit(solution)/shard_map/ppermute | solution.py:115
  65.5 9.1 %collective-permute-start.8 = (bf16[16,32,128]{2,1,0:T(8,128)(2,1)S(1)}, bf16[16,32,128]{2,1,0:T(8,128)(2,1)S(1)}, u32[]{:S(2)}, u32[]{:S(2)}) collective-permute-start(bf16[16,32,128]{2,1,0:T(8,128)(2,1)S(1)} %get-tuple-element.37), channel_id=1, source_target_pairs={{0,2},{1,3},{14,12},{15,13},{16,18},{17,19},{30,28},{31,29},{32,34... | collective-permute-start | bytes 393224 | tf_op jit(solution)/shard_map/ppermute | solution.py:115
  69.5 71.5 %collective-permute-start.24 = (f32[8,1]{0,1:T(1,128)S(1)}, f32[8,1]{0,1:T(1,128)S(1)}, u32[]{:S(2)}, u32[]{:S(2)}) collective-permute-start(f32[8,1]{0,1:T(1,128)S(1)} %bitcast.174), channel_id=1, source_target_pairs={{0,1},{1,0},{2,3},{3,2},{4,5},{5,4},{6,7},{7,6},{8,9},{9,8},{10,11... | collective-permute-start | bytes 104 | tf_op jit(solution)/shard_map/ppermute | solution.py:115
  77.0 9.8 %collective-permute-start.16 = (bf16[16,4096]{1,0:T(8,128)(2,1)S(1)}, bf16[16,4096]{1,0:T(8,128)(2,1)S(1)}, u32[]{:S(2)}, u32[]{:S(2)}) collective-permute-start(bf16[16,4096]{1,0:T(8,128)(2,1)S(1)} %bitcast.165), channel_id=1, source_target_pairs={{0,2},{1,3},{2,4},{3,5},{4,6},{5,7},{6,0},{7,1},{8,10},{9,11},{10,... | collective-permute-start | bytes 393224 | tf_op jit(solution)/shard_map/ppermute | solution.py:115
  77.1 9.8 %collective-permute-start.17 = (bf16[16,4096]{1,0:T(8,128)(2,1)S(1)}, bf16[16,4096]{1,0:T(8,128)(2,1)S(1)}, u32[]{:S(2)}, u32[]{:S(2)}) collective-permute-start(bf16[16,4096]{1,0:T(8,128)(2,1)S(1)} %bitcast.166), channel_id=1, source_target_pairs={{0,6},{1,7},{2,0},{3,1},{4,2},{5,3},{6,4},{7,5},{8,14},{9,15},{10,... | collective-permute-start | bytes 393224 | tf_op jit(solution)/shard_map/ppermute | solution.py:115
  79.8 4.2 %collective-permute-start.11 = (bf16[16,4096]{1,0:T(8,128)(2,1)S(1)}, bf16[16,4096]{1,0:T(8,128)(2,1)S(1)}, u32[]{:S(2)}, u32[]{:S(2)}) collective-permute-start(bf16[16,4096]{1,0:T(8,128)(2,1)S(1)} %bitcast.172), channel_id=1, source_target_pairs={{0,8},{1,9},{2,10},{3,11},{4,12},{5,13},{6,14},{7,15},{8,0},{9,1},... | collective-permute-start | bytes 393224 | tf_op jit(solution)/shard_map/ppermute | solution.py:115
  84.0 9.0 %collective-permute-start.12 = (bf16[32,4096]{1,0:T(8,128)(2,1)S(1)}, bf16[32,4096]{1,0:T(8,128)(2,1)S(1)}, u32[]{:S(2)}, u32[]{:S(2)}) collective-permute-start(bf16[32,4096]{1,0:T(8,128)(2,1)S(1)} %get-tuple-element.54), channel_id=1, source_target_pairs={{0,2},{1,3},{2,4},{3,5},{4,6},{5,7},{6,0},{7,1},{8,10},{9,11},{10,... | collective-permute-start | bytes 786440 | tf_op jit(solution)/shard_map/ppermute | solution.py:115
  84.1 9.0 %collective-permute-start.13 = (bf16[32,4096]{1,0:T(8,128)(2,1)S(1)}, bf16[32,4096]{1,0:T(8,128)(2,1)S(1)}, u32[]{:S(2)}, u32[]{:S(2)}) collective-permute-start(bf16[32,4096]{1,0:T(8,128)(2,1)S(1)} %get-tuple-element.54), channel_id=1, source_target_pairs={{0,6},{1,7},{2,0},{3,1},{4,2},{5,3},{6,4},{7,5},{8,14},{9,15},{10,... | collective-permute-start | bytes 786440 | tf_op jit(solution)/shard_map/ppermute | solution.py:115
  86.8 4.4 %collective-permute-start.18 = (bf16[8,4096]{1,0:T(8,128)(2,1)S(1)}, bf16[8,4096]{1,0:T(8,128)(2,1)S(1)}, u32[]{:S(2)}, u32[]{:S(2)}) collective-permute-start(bf16[8,4096]{1,0:T(8,128)(2,1)S(1)} %slice.84), channel_id=1, source_target_pairs={{0,2},{1,3},{2,4},{3,5},{4,6},{5,7},{6,0},{7,1},{8,10},{9,11},{10,... | collective-permute-start | bytes 196616 | tf_op jit(solution)/shard_map/ppermute | solution.py:115
  86.9 4.3 %collective-permute-start.19 = (bf16[8,4096]{1,0:T(8,128)(2,1)S(1)}, bf16[8,4096]{1,0:T(8,128)(2,1)S(1)}, u32[]{:S(2)}, u32[]{:S(2)}) collective-permute-start(bf16[8,4096]{1,0:T(8,128)(2,1)S(1)} %slice.85), channel_id=1, source_target_pairs={{0,6},{1,7},{2,0},{3,1},{4,2},{5,3},{6,4},{7,5},{8,14},{9,15},{10,... | collective-permute-start | bytes 196616 | tf_op jit(solution)/shard_map/ppermute | solution.py:115
  91.3 14.4 %collective-permute-start.20 = (bf16[48,4096]{1,0:T(8,128)(2,1)S(1)}, bf16[48,4096]{1,0:T(8,128)(2,1)S(1)}, u32[]{:S(2)}, u32[]{:S(2)}) collective-permute-start(bf16[48,4096]{1,0:T(8,128)(2,1)S(1)} %pad_maximum_fusion.1), channel_id=1, source_target_pairs={{0,8},{1,9},{2,10},{3,11},{4,12},{5,13},{6,14},{7,15},{8,0},{9,1},... | collective-permute-start | bytes 1179656 | tf_op jit(solution)/shard_map/ppermute | solution.py:115
  91.3 19.9 %collective-permute-start.21 = (bf16[16,4096]{1,0:T(8,128)(2,1)S(1)}, bf16[16,4096]{1,0:T(8,128)(2,1)S(1)}, u32[]{:S(2)}, u32[]{:S(2)}) collective-permute-start(bf16[16,4096]{1,0:T(8,128)(2,1)S(1)} %pad_maximum_fusion.5), channel_id=1, source_target_pairs={{0,8},{1,9},{2,10},{3,11},{4,12},{5,13},{6,14},{7,15},{8,0},{9,1},... | collective-permute-start | bytes 393224 | tf_op jit(solution)/shard_map/ppermute | solution.py:115
  93.0 7.8 %collective-permute-start.14 = (bf16[16,4096]{1,0:T(8,128)(2,1)S(1)}, bf16[16,4096]{1,0:T(8,128)(2,1)S(1)}, u32[]{:S(2)}, u32[]{:S(2)}) collective-permute-start(bf16[16,4096]{1,0:T(8,128)(2,1)S(1)} %slice.81), channel_id=1, source_target_pairs={{0,2},{1,3},{2,4},{3,5},{4,6},{5,7},{6,0},{7,1},{8,10},{9,11},{10,... | collective-permute-start | bytes 393224 | tf_op jit(solution)/shard_map/ppermute | solution.py:115
  93.1 8.5 %collective-permute-start.15 = (bf16[16,4096]{1,0:T(8,128)(2,1)S(1)}, bf16[16,4096]{1,0:T(8,128)(2,1)S(1)}, u32[]{:S(2)}, u32[]{:S(2)}) collective-permute-start(bf16[16,4096]{1,0:T(8,128)(2,1)S(1)} %slice.82), channel_id=1, source_target_pairs={{0,6},{1,7},{2,0},{3,1},{4,2},{5,3},{6,4},{7,5},{8,14},{9,15},{10,... | collective-permute-start | bytes 393224 | tf_op jit(solution)/shard_map/ppermute | solution.py:115
  128.6 3.1 %collective-permute-start.22 = (f32[8,512]{1,0:T(8,128)S(1)}, f32[8,512]{1,0:T(8,128)S(1)}, u32[]{:S(2)}, u32[]{:S(2)}) collective-permute-start(f32[8,512]{1,0:T(8,128)S(1)} %slice_select_fusion.4), channel_id=1, source_target_pairs={{0,1},{1,0},{2,3},{3,2},{4,5},{5,4},{6,7},{7,6},{8,9},{9,8},{10,11... | collective-permute-start | bytes 49160 | tf_op jit(solution)/shard_map/ppermute | solution.py:115
  132.3 18.6 %all-to-all-start.1 = ((bf16[16,8,512]{2,1,0:T(8,128)(2,1)}), bf16[16,8,512]{2,1,0:T(8,128)(2,1)S(1)}, u32[]{:S(2)}, u32[]{:S(2)}) async-start(bf16[16,8,512]{2,1,0:T(8,128)(2,1)} %broadcast_in_dim.75), calls=%async_computation.1 | async-start | bytes 262144 | tf_op jit(solution)/shard_map/all_to_all | solution.py:208
  151.0 3.0 %collective-permute-start.23 = (bf16[8,512]{1,0:T(8,128)(2,1)S(1)}, bf16[8,512]{1,0:T(8,128)(2,1)S(1)}, u32[]{:S(2)}, u32[]{:S(2)}) collective-permute-start(bf16[8,512]{1,0:T(8,128)(2,1)S(1)} %reduce_sum.71), channel_id=1, source_target_pairs={{0,1},{1,0},{2,3},{3,2},{4,5},{5,4},{6,7},{7,6},{8,9},{9,8},{10,11... | collective-permute-start | bytes 24584 | tf_op jit(solution)/shard_map/ppermute | solution.py:115
  156.2 2.8 %collective-permute-start.25 = (bf16[16,4096]{1,0:T(8,128)(2,1)S(1)}, bf16[16,4096]{1,0:T(8,128)(2,1)S(1)}, u32[]{:S(2)}, u32[]{:S(2)}) collective-permute-start(bf16[16,4096]{1,0:T(8,128)(2,1)S(1)} %get-tuple-element.14), channel_id=1, source_target_pairs={{0,1},{1,0},{2,3},{3,2},{4,5},{5,4},{6,7},{7,6},{8,9},{9,8},{10,11... | collective-permute-start | bytes 393224 | tf_op jit(solution)/shard_map/ppermute | solution.py:115
  156.6 7.8 %collective-permute-start.26 = (bf16[16,4096]{1,0:T(8,128)(2,1)S(1)}, bf16[16,4096]{1,0:T(8,128)(2,1)S(1)}, u32[]{:S(2)}, u32[]{:S(2)}) collective-permute-start(bf16[16,4096]{1,0:T(8,128)(2,1)S(1)} %get-tuple-element.14), channel_id=1, source_target_pairs={{1,16},{16,1},{3,18},{18,3},{5,20},{20,5},{7,22},{22,7},{9,24},{24... | collective-permute-start | bytes 393224 | tf_op jit(solution)/shard_map/ppermute | solution.py:226
  164.4 8.6 %copy-start.13 = (s32[4]{0:T(128)S(1)}, s32[4]{0:T(128)}, u32[]{:S(2)}) copy-start(s32[4]{0:T(128)} %param.13) | copy-start | bytes 52
  165.6 2.0 collective-permute-start.27
  167.0 31.8 %collective-permute-start.33 = (bf16[8,4096]{1,0:T(8,128)(2,1)}, bf16[8,4096]{1,0:T(8,128)(2,1)}, u32[]{:S(2)}, u32[]{:S(2)}) collective-permute-start(bf16[8,4096]{1,0:T(8,128)(2,1)} %bitcast.154), channel_id=1, source_target_pairs={{0,1},{1,0},{2,3},{3,2},{4,5},{5,4},{6,7},{7,6},{8,9},{9,8},{10,11... | collective-permute-start | bytes 196616 | tf_op jit(solution)/shard_map/ppermute | solution.py:115
  168.4 14.2 %all-to-all-start.2 = ((bf16[16,8,512]{2,1,0:T(8,128)(2,1)}), bf16[16,8,512]{2,1,0:T(8,128)(2,1)S(1)}, u32[]{:S(2)}, u32[]{:S(2)}) async-start(bf16[16,8,512]{2,1,0:T(8,128)(2,1)} %broadcast_in_dim.79), calls=%async_computation.2 | async-start | bytes 262144 | tf_op jit(solution)/shard_map/all_to_all | solution.py:208
  182.6 2.8 %collective-permute-start.28 = (bf16[8,512]{1,0:T(8,128)(2,1)S(1)}, bf16[8,512]{1,0:T(8,128)(2,1)S(1)}, u32[]{:S(2)}, u32[]{:S(2)}) collective-permute-start(bf16[8,512]{1,0:T(8,128)(2,1)S(1)} %reduce_sum.73), channel_id=1, source_target_pairs={{0,1},{1,0},{2,3},{3,2},{4,5},{5,4},{6,7},{7,6},{8,9},{9,8},{10,11... | collective-permute-start | bytes 24584 | tf_op jit(solution)/shard_map/ppermute | solution.py:115
  187.7 5.9 %collective-permute-start.29 = (bf16[16,4096]{1,0:T(8,128)(2,1)S(1)}, bf16[16,4096]{1,0:T(8,128)(2,1)S(1)}, u32[]{:S(2)}, u32[]{:S(2)}) collective-permute-start(bf16[16,4096]{1,0:T(8,128)(2,1)S(1)} %get-tuple-element.18), channel_id=1, source_target_pairs={{0,1},{1,0},{2,3},{3,2},{4,5},{5,4},{6,7},{7,6},{8,9},{9,8},{10,11... | collective-permute-start | bytes 393224 | tf_op jit(solution)/shard_map/ppermute | solution.py:115
  188.1 7.8 %collective-permute-start.30 = (bf16[16,4096]{1,0:T(8,128)(2,1)S(1)}, bf16[16,4096]{1,0:T(8,128)(2,1)S(1)}, u32[]{:S(2)}, u32[]{:S(2)}) collective-permute-start(bf16[16,4096]{1,0:T(8,128)(2,1)S(1)} %get-tuple-element.18), channel_id=1, source_target_pairs={{1,16},{16,1},{3,18},{18,3},{5,20},{20,5},{7,22},{22,7},{9,24},{24... | collective-permute-start | bytes 393224 | tf_op jit(solution)/shard_map/ppermute | solution.py:226
  198.7 19.6 %copy-start.12 = (pred[2,128]{1,0:T(4,128)(4,1)S(1)}, pred[2,128]{1,0:T(4,128)(4,1)}, u32[]{:S(2)}) copy-start(pred[2,128]{1,0:T(4,128)(4,1)} %broadcast_in_dim.83) | copy-start | bytes 772
  198.7 1.3 collective-permute-start.31
  200.7 14.2 %all-to-all-start.3 = ((bf16[16,8,512]{2,1,0:T(8,128)(2,1)}), bf16[16,8,512]{2,1,0:T(8,128)(2,1)S(1)}, u32[]{:S(2)}, u32[]{:S(2)}) async-start(bf16[16,8,512]{2,1,0:T(8,128)(2,1)} %broadcast_in_dim.80), calls=%async_computation.3 | async-start | bytes 262144 | tf_op jit(solution)/shard_map/all_to_all | solution.py:208
  216.1 3.0 %collective-permute-start.32 = (bf16[8,512]{1,0:T(8,128)(2,1)S(1)}, bf16[8,512]{1,0:T(8,128)(2,1)S(1)}, u32[]{:S(2)}, u32[]{:S(2)}) collective-permute-start(bf16[8,512]{1,0:T(8,128)(2,1)S(1)} %convert_element_type.24), channel_id=1, source_target_pairs={{0,1},{1,0},{2,3},{3,2},{4,5},{5,4},{6,7},{7,6},{8,9},{9,8},{10,11... | collective-permute-start | bytes 24584 | tf_op jit(solution)/shard_map/ppermute | solution.py:115
  220.7 7.1 %copy-start.11 = (pred[4]{0:T(512)(128)(4,1)S(1)}, pred[4]{0:T(512)(128)(4,1)}, u32[]{:S(2)}) copy-start(pred[4]{0:T(512)(128)(4,1)} %get-tuple-element.25) | copy-start | bytes 16
  221.4 7.1 %collective-permute-start.34 = (f32[8,4096]{1,0:T(8,128)S(1)}, f32[8,4096]{1,0:T(8,128)S(1)}, u32[]{:S(2)}, u32[]{:S(2)}) collective-permute-start(f32[8,4096]{1,0:T(8,128)S(1)} %slice_select_fusion.2), channel_id=1, source_target_pairs={{0,1},{1,0},{2,3},{3,2},{4,5},{5,4},{6,7},{7,6},{8,9},{9,8},{10,11... | collective-permute-start | bytes 393224 | tf_op jit(solution)/shard_map/ppermute | solution.py:115
  222.6 20.6 %all-to-all-start.4 = ((f32[256,1,256]{2,1,0:T(1,128)}), f32[256,1,256]{2,1,0:T(1,128)S(1)}, u32[]{:S(2)}, u32[]{:S(2)}) async-start(f32[256,1,256]{2,1,0:T(1,128)} %bitcast.61), calls=%async_computation.4 | async-start | bytes 524288 | tf_op jit(solution)/shard_map/all_to_all | solution.py:243
  (8 other events, 14.0 us)
Sparse Core Ops, SparseCore 0:
  76.6 49.1 all-gather.1

commit v2 on v0

v2 whole, which is shorter than its diff:
```python
import functools
import math

import jax
import jax.numpy as jnp
from jax import lax
from jax.experimental import pallas as pl
from jax.experimental.pallas import tpu as pltpu
from jax.sharding import PartitionSpec as P

ITERS = 3
VMEM_LIMIT = 24 * 1024 * 1024
NT = (((1,), (1,)), ((), ()))
SMEM = pl.BlockSpec(memory_space=pltpu.SMEM)
ANY = pl.BlockSpec(memory_space=pl.ANY)
VMEM = pl.BlockSpec(memory_space=pltpu.VMEM)

MID, CHIP, SAME, SLOT, CORE, DEV, TABLE = 0, 2, 4, 5, 6, 7, 8


def shape(dims, dtype=jnp.float32):
    return jax.ShapeDtypeStruct(dims, dtype)


def plan_kernel(per_dev, n_orb, ids_ref, dev_ref, out_ref):
    nproj = ids_ref.shape[0]
    chips = n_orb // 2
    ring = chips // 2
    last = per_dev * n_orb - 1
    dev = dev_ref[0]
    chip = dev // 2
    seen = jnp.int32(0)
    mids = [jnp.int32(0)] * (nproj - 2)
    order = []
    for j in range(nproj):
        block = ids_ref[j]
        middle = jnp.logical_and(block != 0, block != last)
        for k in range(nproj - 2):
            mids[k] = jnp.where(jnp.logical_and(middle, seen == k), block, mids[k])
        order.append(jnp.where(block == 0, 0, jnp.where(block == last, 1, 2 + seen)))
        seen = seen + jnp.where(middle, 1, 0)
    owners = [mid // (2 * per_dev) for mid in mids]
    for k in range(nproj - 2):
        out_ref[MID + k] = mids[k]
        out_ref[CHIP + k] = owners[k]
    out_ref[SAME] = jnp.where(owners[0] == owners[1], 1, 0)
    offer = jnp.where(chip == owners[0], mids[0], mids[1])
    out_ref[SLOT] = offer % per_dev
    out_ref[CORE] = (offer // per_dev) % 2
    out_ref[DEV] = dev
    y, x = chip % ring, chip // ring
    for j in range(nproj):
        for q in range(chips):
            down = (q % ring + ring - y) % ring
            side = (q // ring + x) % 2
            out_ref[TABLE + j * chips + q] = order[j] * chips + down * 2 + side


def offer_kernel(plan_ref, occupied_ref, fixed_ref, offer_ref, sem):
    core = plan_ref[DEV] % 2
    last = occupied_ref.shape[0] - 1
    one = pltpu.make_async_copy(occupied_ref.at[core * last, :, 1 - core], fixed_ref, sem.at[0])
    two = pltpu.make_async_copy(occupied_ref.at[plan_ref[SLOT], :, 1 - core], offer_ref, sem.at[1])
    one.start()
    two.start()
    one.wait()
    two.wait()


def pick_kernel(chips, plan_ref, occupied_ref, fixed_ref, offer_ref, *refs):
    *piece_refs, out_ref, sem = refs
    dev = plan_ref[DEV]
    core = dev % 2
    chip = dev // 2
    last = occupied_ref.shape[0] - 1
    rows = piece_refs[0].shape[0]
    ends = jnp.logical_or(dev == 0, dev == 2 * chips - 1)

    def run(copies):
        for copy in copies:
            copy.start()
        for copy in copies:
            copy.wait()

    def pieces(source):
        copies = []
        for s, ref in enumerate(piece_refs):
            at = jnp.where(chip == 0, s, chips - 1 - s) * rows
            copies.append(pltpu.make_async_copy(source(pl.ds(at, rows)), ref, sem.at[s]))
        return copies

    mine = plan_ref[CORE] == core

    @pl.when(mine)
    def _():
        run([pltpu.make_async_copy(occupied_ref.at[plan_ref[SLOT], :, core], out_ref, sem.at[chips])])

    @pl.when(jnp.logical_not(mine))
    def _():
        run([pltpu.make_async_copy(offer_ref, out_ref, sem.at[chips])])

    @pl.when(ends)
    def _():
        run(pieces(lambda at: occupied_ref.at[core * last, at, core]))

    @pl.when(jnp.logical_not(ends))
    def _():
        run(pieces(lambda at: fixed_ref.at[at]))


def share_kernel(chips, plan_ref, *refs):
    *piece_refs, out_ref, sem = refs
    chip = plan_ref[DEV] // 2
    for s, ref in enumerate(piece_refs):

        @pl.when(chip == s)
        def _(ref=ref):
            copy = pltpu.make_async_copy(ref, out_ref.at[0], sem.at[0])
            copy.start()
            copy.wait()

        @pl.when(chip == chips - 1 - s)
        def _(ref=ref):
            copy = pltpu.make_async_copy(ref, out_ref.at[1], sem.at[1])
            copy.start()
            copy.wait()


def split(plan_ref, value, mine_ref, other_ref):
    half = value.shape[0] // 2
    low = plan_ref[DEV] % 2 == 0
    first, second = value[:half], value[half:]
    mine_ref[...] = jnp.where(low, first, second)
    other_ref[...] = jnp.where(low, second, first)


def project(scale, plan_ref, resid_b, blocks_ref, mine_ref, other_ref):
    part = lax.dot_general(resid_b, blocks_ref[...], NT, preferred_element_type=jnp.float32)
    split(plan_ref, part * scale, mine_ref, other_ref)


def first_kernel(scale, plan_ref, rhs_ref, blocks_ref, mine_ref, other_ref):
    project(scale, plan_ref, rhs_ref[...].astype(jnp.bfloat16), blocks_ref, mine_ref, other_ref)


def resid_kernel(
    scale, row, plan_ref, x_ref, sib_ref, off_ref, rhs_ref, diag_ref, blocks_ref,
    resid_ref, mine_ref, other_ref, rb_ref,
):
    cells = x_ref.shape[1]
    lane = lax.broadcasted_iota(jnp.int32, (x_ref.shape[0], row), 1)
    for at in range(0, cells, row):
        here = slice(at, at + row)
        x = x_ref[:, here]
        beside = sib_ref[:, here] + off_ref[:, here]
        if at > 0:
            beside = beside + x_ref[:, at - row : at]
        if at + row < cells:
            beside = beside + x_ref[:, at + row : at + 2 * row]
        beside = beside + jnp.where(lane == 0, 0.0, pltpu.roll(x, 1, 1))
        beside = beside + jnp.where(lane == row - 1, 0.0, pltpu.roll(x, row - 1, 1))
        resid = rhs_ref[:, here] - (diag_ref[:, here] * x - 0.5 * beside)
        resid_ref[:, here] = resid
        rb_ref[:, here] = resid.astype(jnp.bfloat16)
    project(scale, plan_ref, rb_ref[...], blocks_ref, mine_ref, other_ref)


def stacked(value):
    half = value.shape[1] // 2
    return jnp.concatenate([value[:, :half], value[:, half:]], axis=0)


def unstacked(value):
    half = value.shape[0] // 2
    return jnp.concatenate([value[:half], value[half:]], axis=1)


def spread_kernel(mine_ref, other_ref, out_ref):
    total = stacked(mine_ref[...] + other_ref[...]).astype(jnp.bfloat16)
    for d in range(out_ref.shape[0]):
        out_ref[d] = total


def total_kernel(parts_ref, coeff_ref, coeff_b_ref):
    total = parts_ref[0].astype(jnp.float32)
    for d in range(1, parts_ref.shape[0]):
        total = total + parts_ref[d].astype(jnp.float32)
    coeff_ref[...] = unstacked(total)
    coeff_b_ref[...] = total.astype(jnp.bfloat16)


def update_kernel(scale, tile, has_x, last, root, plan_ref, mine_ref, other_ref, resid_ref, diag_ref, *refs):
    refs = list(refs)
    x_ref = refs.pop(0) if has_x else None
    psi_ref = refs.pop(0) if last else None
    blocks_ref, *outs = refs
    low = plan_ref[DEV] % 2 == 0
    mine = unstacked(mine_ref[...].astype(jnp.float32))
    other = unstacked(other_ref[...].astype(jnp.float32))
    coeff = jnp.concatenate([jnp.where(low, mine, other), jnp.where(low, other, mine)], axis=0)
    coeff = coeff.astype(jnp.bfloat16)
    cells = resid_ref.shape[1]
    for at in range(0, cells, tile):
        here = slice(at, at + tile)
        corr = jnp.dot(coeff, blocks_ref[:, here], preferred_element_type=jnp.float32)
        x = (resid_ref[:, here] - corr * scale) / diag_ref[:, here]
        if has_x:
            x = x + x_ref[:, here]
        if last:
            half = x.shape[0] // 2
            outs[0][:, here] = jnp.where(low, x[:half], x[half:])
            outs[1][:, here] = jnp.where(low, x[half:], x[:half])
            raw = jnp.sum(x * psi_ref[:, here].astype(jnp.float32), axis=0, keepdims=True) / root
            wide = outs[2].shape[2]
            for k in range(tile // wide):
                row = raw[:, k * wide : (k + 1) * wide]
                outs[2][at // wide + k] = jnp.broadcast_to(row, outs[2].shape[1:])
        else:
            outs[0][:, here] = x


def table_kernel(plan_ref, coeff_ref, out_ref, rows_ref):
    rows_ref[...] = coeff_ref[...].T
    share = 16
    for j in range(out_ref.shape[0] // share):
        at = pl.multiple_of(plan_ref[TABLE + j] * share, share)
        out_ref[j * share : (j + 1) * share] = rows_ref[pl.ds(at, share)]


def call(kernel, out_shape, in_specs=None, out_specs=None, scratch=()):
    specs = {}
    if in_specs is not None:
        specs["in_specs"] = in_specs
    if out_specs is not None:
        specs["out_specs"] = out_specs
    return pl.pallas_call(
        kernel,
        out_shape=out_shape,
        scratch_shapes=scratch,
        compiler_params=pltpu.CompilerParams(vmem_limit_bytes=VMEM_LIMIT),
        **specs,
    )


def per_device(rhs, potential, eigen_table, win_index, occupied, block_ids, psi_win, smoother):
    local_orbs, planes, rows_y, rows_z = rhs.shape
    n_dom = lax.axis_size("dom")
    n_orb = lax.axis_size("orb")
    cells = rows_y * rows_z
    wide = 2 * local_orbs
    width = local_orbs * n_orb
    scale = 1.0 / math.sqrt(planes * n_dom * rows_y * rows_z)
    n_occ = eigen_table.shape[0]
    per_dev, blk_rows = occupied.shape[:2]
    nproj = block_ids.shape[0]
    chips = n_orb // 2
    ring = chips // 2
    share = blk_rows // chips
    n_rows = nproj * blk_rows
    o = lax.axis_index("orb")
    core = o % 2
    low = core == 0
    groups = [[2 * k + c for k in range(chips)] for c in range(2)]

    def chip_perm(target):
        return [(2 * k + c, 2 * target(k) + c) for k in range(chips) for c in range(2)]

    swap_core = [(i, i ^ 1) for i in range(n_orb)]
    swap_x = chip_perm(lambda k: (k + ring) % chips)
    up_y = chip_perm(lambda k: k // ring * ring + (k + 1) % ring)
    down_y = chip_perm(lambda k: k // ring * ring + (k - 1) % ring)

    def permute(value, pairs):
        return lax.ppermute(value, "orb", pairs)

    def pair(own, other):
        return jnp.concatenate([jnp.where(low, own, other), jnp.where(low, other, own)], axis=0)

    plan = call(
        functools.partial(plan_kernel, per_dev, n_orb),
        shape((TABLE + nproj * chips,), jnp.int32),
        [SMEM, SMEM],
        SMEM,
    )(block_ids, o.astype(jnp.int32).reshape(1))

    plane_shape = shape((blk_rows, rows_y, rows_z), jnp.bfloat16)
    piece_shape = shape((share, rows_y, rows_z), jnp.bfloat16)
    fixed, offer = call(
        offer_kernel, (plane_shape, plane_shape), [SMEM, ANY], (ANY, ANY),
        (pltpu.SemaphoreType.DMA((2,)),),
    )(plan, occupied)
    fixed = permute(fixed, [(0, 1), (n_orb - 1, n_orb - 2)])
    offer = permute(offer, swap_core)
    *pieces, offer = call(
        functools.partial(pick_kernel, chips),
        [piece_shape] * chips + [plane_shape],
        [SMEM, ANY, ANY, ANY],
        [ANY] * (chips + 1),
        (pltpu.SemaphoreType.DMA((chips + 1,)),),
    )(plan, occupied, fixed, offer)

    got = [pieces[0]]
    for s in range(1, chips):
        pairs = [(c, 2 * s + c) for c in range(2)]
        pairs += [(n_orb - 2 + c, 2 * (chips - 1 - s) + c) for c in range(2)]
        got.append(permute(pieces[s], pairs))
    fixed_shares = call(
        functools.partial(share_kernel, chips),
        shape((2, share, rows_y, rows_z), jnp.bfloat16),
        [SMEM] + [ANY] * chips,
        ANY,
        (pltpu.SemaphoreType.DMA((2,)),),
    )(plan, *got).reshape(2, share, cells)

    def scatter(value):
        value = value.reshape(chips, share, rows_y, rows_z)
        return lax.all_to_all(value, "orb", 0, 0, axis_index_groups=groups, tiled=True)

    def take(value, owner):
        return lax.dynamic_index_in_dim(value, owner, 0, keepdims=False).reshape(share, cells)

    def apart(plan, occupied, offer):
        offered = scatter(offer)
        return tuple(take(offered, plan[CHIP + k]) for k in range(nproj - 2))

    def together(plan, occupied, offer):
        def plane_of(slot, plane):
            dims = (1, blk_rows, 1, rows_y, rows_z)
            return lax.dynamic_slice(occupied, (slot, 0, plane, 0, 0), dims).reshape(offer.shape)

        out = [take(scatter(offer), plan[CHIP])]
        for k in range(1, nproj - 2):
            mid = plan[MID + k]
            other = permute(plane_of(mid % per_dev, 1 - core), swap_core)
            here = (mid // per_dev) % 2 == core
            again = jnp.where(here, plane_of(mid % per_dev, core), other)
            out.append(take(scatter(again), plan[CHIP + k]))
        return tuple(out)

    mid_shares = lax.cond(plan[SAME] == 1, together, apart, plan, occupied, offer)

    def gather(one, two):
        own = jnp.concatenate([one, permute(one, swap_x)], axis=0)
        above = permute(own, up_y)
        below = permute(own, down_y)
        near_y = permute(two, up_y)
        back_y = permute(two, down_y)
        far0 = permute(above[:share], up_y)
        far1 = permute(below[share:], down_y)
        half = share // 2
        line = jnp.concatenate([two, back_y, near_y], axis=0)
        line_x = permute(line, swap_x)
        far = jnp.concatenate([permute(near_y[:half], up_y), permute(back_y[half:], down_y)], axis=0)
        far_x = permute(far, swap_x)
        first = [own, below, far0, far1, above]
        second = [two, line_x[:share], back_y, line_x[share : 2 * share], far, far_x, near_y, line_x[2 * share :]]
        return first, second

    held = gather(fixed_shares[0], fixed_shares[1]) + gather(*mid_shares)
    blocks = jnp.concatenate([piece for part in held for piece in part], axis=0)

    def both(field):
        mine = lax.dynamic_index_in_dim(field, core, 1, keepdims=False).reshape(local_orbs, cells)
        send = lax.dynamic_index_in_dim(field, 1 - core, 1, keepdims=False).reshape(local_orbs, cells)
        return pair(mine, permute(send, swap_core))

    picks = win_index[:, None] == jnp.arange(n_occ, dtype=jnp.int32)[None, :]
    eps = jnp.sum(jnp.where(picks, eigen_table[None, :], 0.0), axis=1)[:, None]
    eps = pair(eps, permute(eps, swap_core))
    plane_pot = lax.dynamic_index_in_dim(potential, core, 0, keepdims=True).reshape(1, cells)
    diag = 3.0 + plane_pot - eps
    rhs_wide = both(rhs)
    psi_wide = both(psi_win)

    half_shape = shape((local_orbs, n_rows))
    field_shape = shape((wide, cells))
    flat_shape = (wide, n_rows // 2)

    def total(mine, other):
        other = permute(other, swap_core)
        spread = call(spread_kernel, shape((n_dom,) + flat_shape, jnp.bfloat16))(mine, other)
        parts = lax.all_to_all(spread, "dom", 0, 0, tiled=True)
        coeff, coeff_b = call(total_kernel, (half_shape, shape(flat_shape, jnp.bfloat16)))(parts)
        return coeff, coeff_b, permute(coeff_b, swap_core)

    across = []
    for d in range(n_dom - 1):
        for k in range(chips):
            left, right = d * n_orb + 2 * k + 1, (d + 1) * n_orb + 2 * k
            across += [(left, right), (right, left)]

    x = None
    for step in range(ITERS):
        if step == 0:
            resid = rhs_wide
            mine, other = call(
                functools.partial(first_kernel, scale),
                (half_shape, half_shape),
                [SMEM, VMEM, VMEM],
            )(plan, rhs_wide, blocks)
        else:
            sib = permute(x, swap_core)
            off = lax.ppermute(x, ("dom", "orb"), across)
            resid, mine, other = call(
                functools.partial(resid_kernel, scale, rows_z),
                (field_shape, half_shape, half_shape),
                [SMEM] + [VMEM] * 6,
                scratch=(pltpu.VMEM((wide, cells), jnp.bfloat16),),
            )(plan, x, sib, off, rhs_wide, diag, blocks)
        coeff, coeff_b, coeff_o = total(mine, other)
        final = step == ITERS - 1
        extra = ([x] if step else []) + ([psi_wide] if final else [])
        outs = [field_shape]
        if final:
            outs = [shape((local_orbs, cells))] * 2 + [shape((n_dom, n_orb, cells // n_dom))]
        x, *rest = call(
            functools.partial(update_kernel, scale, 512, step > 0, final, math.sqrt(width)),
            outs,
            [SMEM] + [VMEM] * (5 + len(extra)),
        )(plan, coeff_b, coeff_o, resid, diag, *extra, blocks)
    other, raw = rest

    weights = jnp.broadcast_to(
        smoother.reshape(2 * n_dom, n_dom, 1, 2), (2 * n_dom, n_dom, chips, 2)
    ).reshape(2 * n_dom, n_dom * n_orb)
    terms = lax.all_to_all(raw.reshape(n_dom * n_orb, -1), ("dom", "orb"), 0, 0, tiled=True)
    smoothed = jnp.dot(weights, terms, precision=lax.Precision.HIGHEST)
    smoothed = smoothed.reshape(2 * n_dom, rows_y // n_dom, rows_z)
    z_part = rows_z // n_orb
    gradient = lax.dynamic_slice_in_dim(smoothed, o * z_part, z_part, axis=2)

    other = permute(other, swap_core)
    solution = jnp.stack([jnp.where(low, x, other), jnp.where(low, other, x)], axis=1)
    solution = solution.reshape(rhs.shape)

    coeff, raw = lax.optimization_barrier((coeff, raw))
    correlations = call(
        table_kernel,
        shape((n_rows, local_orbs)),
        [SMEM, VMEM],
        scratch=(pltpu.VMEM((n_rows, local_orbs), jnp.float32),),
    )(plan, coeff).reshape(nproj, blk_rows, local_orbs)
    return (solution, correlations, gradient)


def solution(mesh):
    return jax.shard_map(
        per_device,
        mesh=mesh,
        in_specs=(
            P("orb", "dom", None, None),
            P("dom", None, None),
            P(),
            P("orb"),
            P("orb", None, "dom", None, None),
            P(),
            P("orb", "dom", None, None),
            P(),
        ),
        out_specs=(P("orb", "dom", None, None), P(None, None, "orb"), P(None, "dom", "orb")),
        check_vma=False,
    )
```

time: 553 us -> 312 us (0.56)
  blocking collectives: 200 us -> 14.6 us
  waiting for transfers between devices: 244 us -> 94.3 us
  starting transfers between devices: 21.4 us -> 127 us
  Pallas kernels: 0 us -> 50.9 us
  matrix products: 27.6 us -> 0.35 us
  between operations: 24.2 us -> 2.12 us
  other arithmetic: 18.1 us -> 2.06 us
    psum x3 -> x0, blocking collectives: 186 us -> none  [per_device(): project_coeff = lax.psum(part, 'dom')]
    psum x1 -> x0, waiting for transfers between devices: 139 us -> none  [spread(): return lax.psum(block, axis)]
    reduce_scatter x1 -> x0, waiting for transfers between devices: 98.1 us -> none  [per_device(): lax.psum_scatter(smoothed, 'orb', scatter_dimension=2, tiled=True)]
    ppermute x6 -> x45, starting transfers between devices: 21.3 us -> 102 us  [the longest x43 96.9 us: permute(): return lax.ppermute(value, 'orb', pairs)]
    pallas_call x0 -> x17, Pallas kernels: none -> 50.9 us  [the longest x1 33.4 us: per_device(): call(offer_kernel, (plane_shape, plane_shape), [SMEM, ANY], (ANY, ANY), (...]
    ppermute x6 -> x45, waiting for transfers between devices: 7.08 us -> 54.6 us  [the longest x43 41.4 us: permute(): return lax.ppermute(value, 'orb', pairs)]
    all_to_all x0 -> x4, waiting for transfers between devices: none -> 39.7 us  [the longest x2 20.2 us: total(): parts = lax.all_to_all(spread, 'dom', 0, 0, tiled=True)]
    dot_general x7 -> x1, matrix products: 27.6 us -> 0.35 us  [per_device(): smoothed = jnp.dot(weights, terms, precision=lax.Precision.HIGHEST)]
  transfers between devices with their start and end apart: 8 -> 49, of which waited for: 8 -> 25; matrix products, arithmetic and copies ran while one was open for 0% -> 4% of each run, Pallas kernels for 0% -> 2%
where the time goes in v2:
time: 312 us; the launch traced here: 311 us
  starting transfers between devices  127 us (41%)
  waiting for transfers between devices  94.3 us (30%)
  Pallas kernels  50.9 us (16%)
  local copies, waits for them, and re-layouts  18.2 us (6%)
  blocking collectives  14.6 us (5%)
    ppermute x43, starting transfers between devices, permute(): return lax.ppermute(value, 'orb', pairs)  96.9 us
    ppermute x43, waiting for transfers between devices, permute(): return lax.ppermute(value, 'orb', pairs)  41.4 us
    pallas_call x1, Pallas kernels, per_device(): call(offer_kernel, (plane_shape, plane_shape), [SMEM, ANY], (ANY, ANY), (...  33.4 us
    all_to_all x2, waiting for transfers between devices, total(): parts = lax.all_to_all(spread, 'dom', 0, 0, tiled=True)  20.2 us
    all_to_all x2, starting transfers between devices, total(): parts = lax.all_to_all(spread, 'dom', 0, 0, tiled=True)  15.2 us
    all_to_all x1, blocking collectives, total(): parts = lax.all_to_all(spread, 'dom', 0, 0, tiled=True)  14.6 us
    ppermute x2, waiting for transfers between devices, per_device(): off = lax.ppermute(x, ('dom', 'orb'), across)  13.2 us
    all_to_all x1, waiting for transfers between devices, per_device(): lax.all_to_all(raw.reshape(n_dom * n_orb, -1), ('dom', 'orb'), 0, 0, tile...  10.7 us
  transfers between devices with their start and end apart: 49, of which 25 were waited for; matrix products, arithmetic and copies ran while one was open for 4% of the time, Pallas kernels for 2%

profile of v2, /device:TPU:1, one launch (start us, length us, event | category | flops | bytes accessed | tf_op | source)
XLA Modules:
  0.0 311.1 jit_solution(18333597765961278710)
XLA Ops:
  2.5 33.4 %shard_map.104 = (bf16[128,32,128]{2,1,0:T(8,128)(2,1)}, bf16[128,32,128]{2,1,0:T(8,128)(2,1)S(1)}) custom-call(s32[40]{0:T(128)S(1)} %shard_map.103.plan_ref, bf16[2,128,2,32,128]{4,3,2,1,0:T(8,128)(2,1)} %occupied_ref.3), custom_call_target="tpu_custom_call" | custom-call | tf_op jit(solution)/shard_map/pallas_call | solution.py:288
  37.3 3.4 %collective-permute-start.3 = (bf16[128,32,128]{2,1,0:T(8,128)(2,1)S(1)}, bf16[128,32,128]{2,1,0:T(8,128)(2,1)S(1)}, u32[]{:S(2)}, u32[]{:S(2)}) collective-permute-start(bf16[128,32,128]{2,1,0:T(8,128)(2,1)S(1)} %get-tuple-element.66), channel_id=1, source_target_pairs={{0,1},{1,0},{2,3},{3,2},{4,5},{5,4},{6,7},{7,6},{8,9},{9,8},{10,11... | collective-permute-start | bytes 3145736 | tf_op jit(solution)/shard_map/ppermute | solution.py:274
  44.4 3.1 %shard_map.105 = (bf16[16,32,128]{2,1,0:T(8,128)(2,1)S(1)}, bf16[16,32,128]{2,1,0:T(8,128)(2,1)S(1)}, bf16[16,32,128]{2,1,0:T(8,128)(2,1)S(1)}, bf16[16,32,128]{...) custom-call(s32[40]{0:T(128)S(1)} %shard_map.103.plan_ref, ...), custom_call_target="tpu_custom_call" | custom-call | tf_op jit(solution)/shard_map/pallas_call | solution.py:294
  50.2 19.5 %conditional.1 = (bf16[8,16,32,128]{3,2,1,0:T(8,128)(2,1)}, bf16[8,16,32,128]{3,2,1,0:T(8,128)(2,1)}, s32[]{:T(128)}, s32[]{:T(128)}, bf16[8,16,32,128]{3,2,1,0:...) conditional(s32[]{:T(128)} %bitcast.11, ...), branch_computations={%region_0.1_spmd, %region_1.2_spmd} | conditional | flops 524329 | bytes 17826492 | solution.py:340
  50.2 4.3 %all-to-all-start = ((bf16[8,16,32,128]{3,2,1,0:T(8,128)(2,1)}), bf16[8,16,32,128]{3,2,1,0:T(8,128)(2,1)}, u32[]{:S(2)}, u32[]{:S(2)}) async-start(bf16[8,16,32,128]{3,2,1,0:T(8,128)(2,1)} %bitcast), calls=%async_computation | async-start | bytes 2097152 | tf_op jit(solution)/shard_map/cond/branch_0_fun/all_to_all | solution.py:317
  55.1 8.8 %all-to-all-done = bf16[8,16,32,128]{3,2,1,0:T(8,128)(2,1)} async-done(((bf16[8,16,32,128]{3,2,1,0:T(8,128)(2,1)}), bf16[8,16,32,128]{3,2,1,0:T(8,128)(2,1)}, u32[]{:S(2)}, u32[]{:S(2)}) %all-to-all-start) | async-done | bytes 1048608 | tf_op jit(solution)/shard_map/cond/branch_0_fun/all_to_all | solution.py:317
  63.9 2.3 copy.129
  66.2 2.3 copy.78
  69.7 3.5 %collective-permute-start.6 = (bf16[16,32,128]{2,1,0:T(8,128)(2,1)S(1)}, bf16[16,32,128]{2,1,0:T(8,128)(2,1)S(1)}, u32[]{:S(2)}, u32[]{:S(2)}) collective-permute-start(bf16[16,32,128]{2,1,0:T(8,128)(2,1)S(1)} %get-tuple-element.70), channel_id=1, source_target_pairs={{0,6},{1,7},{14,8},{15,9},{16,22},{17,23},{30,24},{31,25},{32,38},... | collective-permute-start | bytes 393224 | tf_op jit(solution)/shard_map/ppermute | solution.py:274
  77.2 3.9 %collective-permute-start.10 = (bf16[16,32,128]{2,1,0:T(8,128)(2,1)S(1)}, bf16[16,32,128]{2,1,0:T(8,128)(2,1)S(1)}, u32[]{:S(2)}, u32[]{:S(2)}) collective-permute-start(bf16[16,32,128]{2,1,0:T(8,128)(2,1)S(1)} %get-tuple-element.74), channel_id=1, source_target_pairs={{0,14},{1,15},{14,0},{15,1},{16,30},{17,31},{30,16},{31,17},{32,46... | collective-permute-start | bytes 393224 | tf_op jit(solution)/shard_map/ppermute | solution.py:274
  83.1 34.1 %collective-permute-start.35 = (f32[8,1]{0,1:T(1,128)S(1)}, f32[8,1]{0,1:T(1,128)S(1)}, u32[]{:S(2)}, u32[]{:S(2)}) collective-permute-start(f32[8,1]{0,1:T(1,128)S(1)} %bitcast.115), channel_id=1, source_target_pairs={{0,1},{1,0},{2,3},{3,2},{4,5},{5,4},{6,7},{7,6},{8,9},{9,8},{10,11... | collective-permute-start | bytes 104 | tf_op jit(solution)/shard_map/ppermute | solution.py:274
  117.3 2.7 collective-permute-start.27
  121.2 2.3 collective-permute-done.28
  123.9 1.5 collective-permute-start.11
  128.0 2.6 collective-permute-start.20
  130.6 1.5 collective-permute-done.19
  133.6 5.2 %collective-permute-done.13 = bf16[32,4096]{1,0:T(8,128)(2,1)S(1)} collective-permute-done((bf16[32,4096]{1,0:T(8,128)(2,1)S(1)}, bf16[32,4096]{1,0:T(8,128)(2,1)S(1)}, u32[]{:S(2)}, u32[]{:S(2)}) %collective-permute-start.13) | collective-permute-done | bytes 262176 | tf_op jit(solution)/shard_map/ppermute | solution.py:274
  139.3 6.5 %collective-permute-done.14 = bf16[16,4096]{1,0:T(8,128)(2,1)S(1)} collective-permute-done((bf16[16,4096]{1,0:T(8,128)(2,1)S(1)}, bf16[16,4096]{1,0:T(8,128)(2,1)S(1)}, u32[]{:S(2)}, u32[]{:S(2)}) %collective-permute-start.14) | collective-permute-done | bytes 131104 | tf_op jit(solution)/shard_map/ppermute | solution.py:274
  145.8 1.6 collective-permute-start.15
  147.4 2.2 collective-permute-done.15
  151.0 5.5 %collective-permute-done.18 = bf16[48,4096]{1,0:T(8,128)(2,1)S(1)} collective-permute-done((bf16[48,4096]{1,0:T(8,128)(2,1)S(1)}, bf16[48,4096]{1,0:T(8,128)(2,1)S(1)}, u32[]{:S(2)}, u32[]{:S(2)}) %collective-permute-start.18) | collective-permute-done | bytes 393248 | tf_op jit(solution)/shard_map/ppermute | solution.py:274
  157.7 2.6 collective-permute-done.21
  160.4 3.3 %collective-permute-start.31 = (bf16[8,4096]{1,0:T(8,128)(2,1)S(1)}, bf16[8,4096]{1,0:T(8,128)(2,1)S(1)}, u32[]{:S(2)}, u32[]{:S(2)}) collective-permute-start(bf16[8,4096]{1,0:T(8,128)(2,1)S(1)} %slice.99), channel_id=1, source_target_pairs={{0,6},{1,7},{2,0},{3,1},{4,2},{5,3},{6,4},{7,5},{8,14},{9,15},{10,... | collective-permute-start | bytes 196616 | tf_op jit(solution)/shard_map/ppermute | solution.py:274
  165.8 4.5 %collective-permute-done.24 = bf16[32,4096]{1,0:T(8,128)(2,1)S(1)} collective-permute-done((bf16[32,4096]{1,0:T(8,128)(2,1)S(1)}, bf16[32,4096]{1,0:T(8,128)(2,1)S(1)}, u32[]{:S(2)}, u32[]{:S(2)}) %collective-permute-start.24) | collective-permute-done | bytes 262176 | tf_op jit(solution)/shard_map/ppermute | solution.py:274
  170.9 2.3 collective-permute-start.26
  173.3 2.2 collective-permute-done.25
  176.1 1.7 shard_map.107
  177.8 2.0 copy-done
  179.8 12.6 %collective-permute-start.33 = (f32[8,512]{1,0:T(8,128)S(1)}, f32[8,512]{1,0:T(8,128)S(1)}, u32[]{:S(2)}, u32[]{:S(2)}) collective-permute-start(f32[8,512]{1,0:T(8,128)S(1)} %get-tuple-element.83), channel_id=1, source_target_pairs={{0,1},{1,0},{2,3},{3,2},{4,5},{5,4},{6,7},{7,6},{8,9},{9,8},{10,11... | collective-permute-start | bytes 49160 | tf_op jit(solution)/shard_map/ppermute | solution.py:274
  194.0 10.5 %all-to-all-start.3 = ((bf16[16,16,256]{2,1,0:T(8,128)(2,1)}), bf16[16,16,256]{2,1,0:T(8,128)(2,1)S(1)}, u32[]{:S(2)}, u32[]{:S(2)}) async-start(bf16[16,16,256]{2,1,0:T(8,128)(2,1)} %shard_map.108), calls=%async_computation.3 | async-start | bytes 262144 | tf_op jit(solution)/shard_map/all_to_all | solution.py:382
  204.6 9.9 %all-to-all-done.3.parts_ref = bf16[16,16,256]{2,1,0:T(8,128)(2,1)S(1)} async-done(((bf16[16,16,256]{2,1,0:T(8,128)(2,1)}), bf16[16,16,256]{2,1,0:T(8,128)(2,1)S(1)}, u32[]{:S(2)}, u32[]{:S(2)}) %all-to-all-start.3) | async-done | bytes 131104 | tf_op jit(solution)/shard_map/all_to_all | solution.py:382
  215.1 2.0 collective-permute-start.34
  218.0 2.2 copy-done.1
  222.0 2.7 collective-permute-start.37
  224.7 6.6 %collective-permute-done.37.off_ref = f32[16,4096]{1,0:T(8,128)S(1)} collective-permute-done((f32[16,4096]{1,0:T(8,128)S(1)}, f32[16,4096]{1,0:T(8,128)S(1)}, u32[]{:S(2)}, u32[]{:S(2)}) %collective-permute-start.37) | collective-permute-done | bytes 262176 | tf_op jit(solution)/shard_map/ppermute | solution.py:403
  231.3 1.8 shard_map.111
  234.3 14.6 %all_to_all.39.parts_ref = bf16[16,16,256]{2,1,0:T(8,128)(2,1)S(1)} all-to-all(bf16[16,16,256]{2,1,0:T(8,128)(2,1)S(1)} %shard_map.112), channel_id=1, replica_groups=mesh['dom'=16,'orb'=16] {'dom'}, dimensions={0} | all-to-all | bytes 262144 | tf_op jit(solution)/shard_map/all_to_all | solution.py:382
  249.6 2.0 collective-permute-start.39
  254.0 2.4 collective-permute-start.41
  256.6 6.6 %collective-permute-done.41.off_ref = f32[16,4096]{1,0:T(8,128)S(1)} collective-permute-done((f32[16,4096]{1,0:T(8,128)S(1)}, f32[16,4096]{1,0:T(8,128)S(1)}, u32[]{:S(2)}, u32[]{:S(2)}) %collective-permute-start.41) | collective-permute-done | bytes 262176 | tf_op jit(solution)/shard_map/ppermute | solution.py:403
  263.2 1.8 shard_map.115
  266.8 4.7 %all-to-all-start.5 = ((bf16[16,16,256]{2,1,0:T(8,128)(2,1)}), bf16[16,16,256]{2,1,0:T(8,128)(2,1)S(1)}, u32[]{:S(2)}, u32[]{:S(2)}) async-start(bf16[16,16,256]{2,1,0:T(8,128)(2,1)} %shard_map.116), calls=%async_computation.5 | async-start | bytes 262144 | tf_op jit(solution)/shard_map/all_to_all | solution.py:382
  271.6 10.3 %all-to-all-done.5.parts_ref = bf16[16,16,256]{2,1,0:T(8,128)(2,1)S(1)} async-done(((bf16[16,16,256]{2,1,0:T(8,128)(2,1)}), bf16[16,16,256]{2,1,0:T(8,128)(2,1)S(1)}, u32[]{:S(2)}, u32[]{:S(2)}) %all-to-all-start.5) | async-done | bytes 131104 | tf_op jit(solution)/shard_map/all_to_all | solution.py:382
  281.9 1.8 collective-permute-start.43
  284.6 2.2 copy-done.3
  289.0 5.8 %all-to-all-start.6 = ((f32[256,1,256]{2,1,0:T(1,128)}), f32[256,1,256]{2,1,0:T(1,128)S(1)}, u32[]{:S(2)}, u32[]{:S(2)}) async-start(f32[256,1,256]{2,1,0:T(1,128)} %copy.28), calls=%async_computation.6 | async-start | bytes 524288 | tf_op jit(solution)/shard_map/all_to_all | solution.py:426
  294.8 2.2 collective-permute-start.45
  299.3 10.7 %all-to-all-done.6 = f32[256,1,256]{2,1,0:T(1,128)S(1)} async-done(((f32[256,1,256]{2,1,0:T(1,128)}), f32[256,1,256]{2,1,0:T(1,128)S(1)}, u32[]{:S(2)}, u32[]{:S(2)}) %all-to-all-start.6) | async-done | bytes 262176 | tf_op jit(solution)/shard_map/all_to_all | solution.py:426
  (166 shorter events, 44.9 us)
Async XLA Ops:
  36.0 8.4 %collective-permute-start.2 = (bf16[128,32,128]{2,1,0:T(8,128)(2,1)}, bf16[128,32,128]{2,1,0:T(8,128)(2,1)S(1)}, u32[]{:S(2)}, u32[]{:S(2)}) collective-permute-start(bf16[128,32,128]{2,1,0:T(8,128)(2,1)} %get-tuple-element.65), channel_id=1, source_target_pairs={{0,1},{15,14},{16,17},{31,30},{32,33},{47,46},{48,49},{63,62},{64,... | collective-permute-start | bytes 3145736 | tf_op jit(solution)/shard_map/ppermute | solution.py:274
  37.3 7.2 %collective-permute-start.3 = (bf16[128,32,128]{2,1,0:T(8,128)(2,1)S(1)}, bf16[128,32,128]{2,1,0:T(8,128)(2,1)S(1)}, u32[]{:S(2)}, u32[]{:S(2)}) collective-permute-start(bf16[128,32,128]{2,1,0:T(8,128)(2,1)S(1)} %get-tuple-element.66), channel_id=1, source_target_pairs={{0,1},{1,0},{2,3},{3,2},{4,5},{5,4},{6,7},{7,6},{8,9},{9,8},{10,11... | collective-permute-start | bytes 3145736 | tf_op jit(solution)/shard_map/ppermute | solution.py:274
  40.8 3.6 %collective-permute-start.1 = (f32[8,4096]{1,0:T(8,128)S(1)}, f32[8,4096]{1,0:T(8,128)S(1)}, u32[]{:S(2)}, u32[]{:S(2)}) collective-permute-start(f32[8,4096]{1,0:T(8,128)S(1)} %bitcast.112), channel_id=1, source_target_pairs={{0,1},{1,0},{2,3},{3,2},{4,5},{5,4},{6,7},{7,6},{8,9},{9,8},{10,11... | collective-permute-start | bytes 393224 | tf_op jit(solution)/shard_map/ppermute | solution.py:274
  47.6 28.4 %collective-permute-start.4 = (bf16[16,32,128]{2,1,0:T(8,128)(2,1)S(1)}, bf16[16,32,128]{2,1,0:T(8,128)(2,1)S(1)}, u32[]{:S(2)}, u32[]{:S(2)}) collective-permute-start(bf16[16,32,128]{2,1,0:T(8,128)(2,1)S(1)} %get-tuple-element.68), channel_id=1, source_target_pairs={{0,2},{1,3},{14,12},{15,13},{16,18},{17,19},{30,28},{31,29},{32,34... | collective-permute-start | bytes 393224 | tf_op jit(solution)/shard_map/ppermute | solution.py:274
  48.9 28.4 %collective-permute-start.5 = (bf16[16,32,128]{2,1,0:T(8,128)(2,1)S(1)}, bf16[16,32,128]{2,1,0:T(8,128)(2,1)S(1)}, u32[]{:S(2)}, u32[]{:S(2)}) collective-permute-start(bf16[16,32,128]{2,1,0:T(8,128)(2,1)S(1)} %get-tuple-element.69), channel_id=1, source_target_pairs={{0,4},{1,5},{14,10},{15,11},{16,20},{17,21},{30,26},{31,27},{32,36... | collective-permute-start | bytes 393224 | tf_op jit(solution)/shard_map/ppermute | solution.py:274
  50.2 13.7 %all-to-all-start = ((bf16[8,16,32,128]{3,2,1,0:T(8,128)(2,1)}), bf16[8,16,32,128]{3,2,1,0:T(8,128)(2,1)}, u32[]{:S(2)}, u32[]{:S(2)}) async-start(bf16[8,16,32,128]{3,2,1,0:T(8,128)(2,1)} %bitcast), calls=%async_computation | async-start | bytes 2097152 | tf_op jit(solution)/shard_map/cond/branch_0_fun/all_to_all | solution.py:317
  69.7 13.4 %collective-permute-start.6 = (bf16[16,32,128]{2,1,0:T(8,128)(2,1)S(1)}, bf16[16,32,128]{2,1,0:T(8,128)(2,1)S(1)}, u32[]{:S(2)}, u32[]{:S(2)}) collective-permute-start(bf16[16,32,128]{2,1,0:T(8,128)(2,1)S(1)} %get-tuple-element.70), channel_id=1, source_target_pairs={{0,6},{1,7},{14,8},{15,9},{16,22},{17,23},{30,24},{31,25},{32,38},... | collective-permute-start | bytes 393224 | tf_op jit(solution)/shard_map/ppermute | solution.py:274
  73.3 44.0 %collective-permute-start.7 = (bf16[16,32,128]{2,1,0:T(8,128)(2,1)S(1)}, bf16[16,32,128]{2,1,0:T(8,128)(2,1)S(1)}, u32[]{:S(2)}, u32[]{:S(2)}) collective-permute-start(bf16[16,32,128]{2,1,0:T(8,128)(2,1)S(1)} %get-tuple-element.71), channel_id=1, source_target_pairs={{0,8},{1,9},{14,6},{15,7},{16,24},{17,25},{30,22},{31,23},{32,40},... | collective-permute-start | bytes 393224 | tf_op jit(solution)/shard_map/ppermute | solution.py:274
  74.6 42.7 %collective-permute-start.8 = (bf16[16,32,128]{2,1,0:T(8,128)(2,1)S(1)}, bf16[16,32,128]{2,1,0:T(8,128)(2,1)S(1)}, u32[]{:S(2)}, u32[]{:S(2)}) collective-permute-start(bf16[16,32,128]{2,1,0:T(8,128)(2,1)S(1)} %get-tuple-element.72), channel_id=1, source_target_pairs={{0,10},{1,11},{14,4},{15,5},{16,26},{17,27},{30,20},{31,21},{32,42... | collective-permute-start | bytes 393224 | tf_op jit(solution)/shard_map/ppermute | solution.py:274
  75.9 44.0 %collective-permute-start.9 = (bf16[16,32,128]{2,1,0:T(8,128)(2,1)S(1)}, bf16[16,32,128]{2,1,0:T(8,128)(2,1)S(1)}, u32[]{:S(2)}, u32[]{:S(2)}) collective-permute-start(bf16[16,32,128]{2,1,0:T(8,128)(2,1)S(1)} %get-tuple-element.73), channel_id=1, source_target_pairs={{0,12},{1,13},{14,2},{15,3},{16,28},{17,29},{30,18},{31,19},{32,44... | collective-permute-start | bytes 393224 | tf_op jit(solution)/shard_map/ppermute | solution.py:274
  77.2 42.7 %collective-permute-start.10 = (bf16[16,32,128]{2,1,0:T(8,128)(2,1)S(1)}, bf16[16,32,128]{2,1,0:T(8,128)(2,1)S(1)}, u32[]{:S(2)}, u32[]{:S(2)}) collective-permute-start(bf16[16,32,128]{2,1,0:T(8,128)(2,1)S(1)} %get-tuple-element.74), channel_id=1, source_target_pairs={{0,14},{1,15},{14,0},{15,1},{16,30},{17,31},{30,16},{31,17},{32,46... | collective-permute-start | bytes 393224 | tf_op jit(solution)/shard_map/ppermute | solution.py:274
  83.1 121.3 %collective-permute-start.35 = (f32[8,1]{0,1:T(1,128)S(1)}, f32[8,1]{0,1:T(1,128)S(1)}, u32[]{:S(2)}, u32[]{:S(2)}) collective-permute-start(f32[8,1]{0,1:T(1,128)S(1)} %bitcast.115), channel_id=1, source_target_pairs={{0,1},{1,0},{2,3},{3,2},{4,5},{5,4},{6,7},{7,6},{8,9},{9,8},{10,11... | collective-permute-start | bytes 104 | tf_op jit(solution)/shard_map/ppermute | solution.py:274
  117.2 6.3 %collective-permute-start.28 = (bf16[16,4096]{1,0:T(8,128)(2,1)S(1)}, bf16[16,4096]{1,0:T(8,128)(2,1)S(1)}, u32[]{:S(2)}, u32[]{:S(2)}) collective-permute-start(bf16[16,4096]{1,0:T(8,128)(2,1)S(1)} %bitcast.103), channel_id=1, source_target_pairs={{0,2},{1,3},{2,4},{3,5},{4,6},{5,7},{6,0},{7,1},{8,10},{9,11},{10,... | collective-permute-start | bytes 393224 | tf_op jit(solution)/shard_map/ppermute | solution.py:274
  117.3 6.6 %collective-permute-start.27 = (bf16[16,4096]{1,0:T(8,128)(2,1)S(1)}, bf16[16,4096]{1,0:T(8,128)(2,1)S(1)}, u32[]{:S(2)}, u32[]{:S(2)}) collective-permute-start(bf16[16,4096]{1,0:T(8,128)(2,1)S(1)} %bitcast.104), channel_id=1, source_target_pairs={{0,6},{1,7},{2,0},{3,1},{4,2},{5,3},{6,4},{7,5},{8,14},{9,15},{10,... | collective-permute-start | bytes 393224 | tf_op jit(solution)/shard_map/ppermute | solution.py:274
  120.0 43.8 %collective-permute-start.22 = (bf16[16,4096]{1,0:T(8,128)(2,1)S(1)}, bf16[16,4096]{1,0:T(8,128)(2,1)S(1)}, u32[]{:S(2)}, u32[]{:S(2)}) collective-permute-start(bf16[16,4096]{1,0:T(8,128)(2,1)S(1)} %bitcast.110), channel_id=1, source_target_pairs={{0,8},{1,9},{2,10},{3,11},{4,12},{5,13},{6,14},{7,15},{8,0},{9,1},... | collective-permute-start | bytes 393224 | tf_op jit(solution)/shard_map/ppermute | solution.py:274
  121.1 5.7 %collective-permute-start.17 = (bf16[16,4096]{1,0:T(8,128)(2,1)S(1)}, bf16[16,4096]{1,0:T(8,128)(2,1)S(1)}, u32[]{:S(2)}, u32[]{:S(2)}) collective-permute-start(bf16[16,4096]{1,0:T(8,128)(2,1)S(1)} %bitcast.106), channel_id=1, source_target_pairs={{0,2},{1,3},{2,4},{3,5},{4,6},{5,7},{6,0},{7,1},{8,10},{9,11},{10,... | collective-permute-start | bytes 393224 | tf_op jit(solution)/shard_map/ppermute | solution.py:274
  123.5 4.2 %collective-permute-start.16 = (bf16[16,4096]{1,0:T(8,128)(2,1)S(1)}, bf16[16,4096]{1,0:T(8,128)(2,1)S(1)}, u32[]{:S(2)}, u32[]{:S(2)}) collective-permute-start(bf16[16,4096]{1,0:T(8,128)(2,1)S(1)} %bitcast.107), channel_id=1, source_target_pairs={{0,6},{1,7},{2,0},{3,1},{4,2},{5,3},{6,4},{7,5},{8,14},{9,15},{10,... | collective-permute-start | bytes 393224 | tf_op jit(solution)/shard_map/ppermute | solution.py:274
  123.9 4.1 %collective-permute-start.11 = (bf16[16,4096]{1,0:T(8,128)(2,1)S(1)}, bf16[16,4096]{1,0:T(8,128)(2,1)S(1)}, u32[]{:S(2)}, u32[]{:S(2)}) collective-permute-start(bf16[16,4096]{1,0:T(8,128)(2,1)S(1)} %bitcast.111), channel_id=1, source_target_pairs={{0,8},{1,9},{2,10},{3,11},{4,12},{5,13},{6,14},{7,15},{8,0},{9,1},... | collective-permute-start | bytes 393224 | tf_op jit(solution)/shard_map/ppermute | solution.py:274
  126.8 49.1 %collective-permute-start.29 = (bf16[48,4096]{1,0:T(8,128)(2,1)S(1)}, bf16[48,4096]{1,0:T(8,128)(2,1)S(1)}, u32[]{:S(2)}, u32[]{:S(2)}) collective-permute-start(bf16[48,4096]{1,0:T(8,128)(2,1)S(1)} %pad_maximum_fusion.1), channel_id=1, source_target_pairs={{0,8},{1,9},{2,10},{3,11},{4,12},{5,13},{6,14},{7,15},{8,0},{9,1},... | collective-permute-start | bytes 1179656 | tf_op jit(solution)/shard_map/ppermute | solution.py:274
  127.7 4.4 %collective-permute-start.19 = (bf16[8,4096]{1,0:T(8,128)(2,1)S(1)}, bf16[8,4096]{1,0:T(8,128)(2,1)S(1)}, u32[]{:S(2)}, u32[]{:S(2)}) collective-permute-start(bf16[8,4096]{1,0:T(8,128)(2,1)S(1)} %slice.91), channel_id=1, source_target_pairs={{0,2},{1,3},{2,4},{3,5},{4,6},{5,7},{6,0},{7,1},{8,10},{9,11},{10,... | collective-permute-start | bytes 196616 | tf_op jit(solution)/shard_map/ppermute | solution.py:274
  128.0 4.3 %collective-permute-start.20 = (bf16[8,4096]{1,0:T(8,128)(2,1)S(1)}, bf16[8,4096]{1,0:T(8,128)(2,1)S(1)}, u32[]{:S(2)}, u32[]{:S(2)}) collective-permute-start(bf16[8,4096]{1,0:T(8,128)(2,1)S(1)} %slice.92), channel_id=1, source_target_pairs={{0,6},{1,7},{2,0},{3,1},{4,2},{5,3},{6,4},{7,5},{8,14},{9,15},{10,... | collective-permute-start | bytes 196616 | tf_op jit(solution)/shard_map/ppermute | solution.py:274
  132.1 7.0 %collective-permute-start.12 = (bf16[32,4096]{1,0:T(8,128)(2,1)S(1)}, bf16[32,4096]{1,0:T(8,128)(2,1)S(1)}, u32[]{:S(2)}, u32[]{:S(2)}) collective-permute-start(bf16[32,4096]{1,0:T(8,128)(2,1)S(1)} %get-tuple-element.131), channel_id=1, source_target_pairs={{0,6},{1,7},{2,0},{3,1},{4,2},{5,3},{6,4},{7,5},{8,14},{9,15},{10,... | collective-permute-start | bytes 786440 | tf_op jit(solution)/shard_map/ppermute | solution.py:274
  132.3 6.4 %collective-permute-start.13 = (bf16[32,4096]{1,0:T(8,128)(2,1)S(1)}, bf16[32,4096]{1,0:T(8,128)(2,1)S(1)}, u32[]{:S(2)}, u32[]{:S(2)}) collective-permute-start(bf16[32,4096]{1,0:T(8,128)(2,1)S(1)} %get-tuple-element.131), channel_id=1, source_target_pairs={{0,2},{1,3},{2,4},{3,5},{4,6},{5,7},{6,0},{7,1},{8,10},{9,11},{10,... | collective-permute-start | bytes 786440 | tf_op jit(solution)/shard_map/ppermute | solution.py:274
  138.8 25.1 %collective-permute-start.30 = (bf16[8,4096]{1,0:T(8,128)(2,1)S(1)}, bf16[8,4096]{1,0:T(8,128)(2,1)S(1)}, u32[]{:S(2)}, u32[]{:S(2)}) collective-permute-start(bf16[8,4096]{1,0:T(8,128)(2,1)S(1)} %slice.98), channel_id=1, source_target_pairs={{0,2},{1,3},{2,4},{3,5},{4,6},{5,7},{6,0},{7,1},{8,10},{9,11},{10,... | collective-permute-start | bytes 196616 | tf_op jit(solution)/shard_map/ppermute | solution.py:274
  139.1 6.7 %collective-permute-start.14 = (bf16[16,4096]{1,0:T(8,128)(2,1)S(1)}, bf16[16,4096]{1,0:T(8,128)(2,1)S(1)}, u32[]{:S(2)}, u32[]{:S(2)}) collective-permute-start(bf16[16,4096]{1,0:T(8,128)(2,1)S(1)} %slice.86), channel_id=1, source_target_pairs={{0,2},{1,3},{2,4},{3,5},{4,6},{5,7},{6,0},{7,1},{8,10},{9,11},{10,... | collective-permute-start | bytes 393224 | tf_op jit(solution)/shard_map/ppermute | solution.py:274
  145.8 3.8 %collective-permute-start.15 = (bf16[16,4096]{1,0:T(8,128)(2,1)S(1)}, bf16[16,4096]{1,0:T(8,128)(2,1)S(1)}, u32[]{:S(2)}, u32[]{:S(2)}) collective-permute-start(bf16[16,4096]{1,0:T(8,128)(2,1)S(1)} %slice.87), channel_id=1, source_target_pairs={{0,6},{1,7},{2,0},{3,1},{4,2},{5,3},{6,4},{7,5},{8,14},{9,15},{10,... | collective-permute-start | bytes 393224 | tf_op jit(solution)/shard_map/ppermute | solution.py:274
  149.6 6.9 %collective-permute-start.18 = (bf16[48,4096]{1,0:T(8,128)(2,1)S(1)}, bf16[48,4096]{1,0:T(8,128)(2,1)S(1)}, u32[]{:S(2)}, u32[]{:S(2)}) collective-permute-start(bf16[48,4096]{1,0:T(8,128)(2,1)S(1)} %pad_maximum_fusion), channel_id=1, source_target_pairs={{0,8},{1,9},{2,10},{3,11},{4,12},{5,13},{6,14},{7,15},{8,0},{9,1},... | collective-permute-start | bytes 1179656 | tf_op jit(solution)/shard_map/ppermute | solution.py:274
  156.5 3.8 %collective-permute-start.21 = (bf16[16,4096]{1,0:T(8,128)(2,1)S(1)}, bf16[16,4096]{1,0:T(8,128)(2,1)S(1)}, u32[]{:S(2)}, u32[]{:S(2)}) collective-permute-start(bf16[16,4096]{1,0:T(8,128)(2,1)S(1)} %pad_maximum_fusion.4), channel_id=1, source_target_pairs={{0,8},{1,9},{2,10},{3,11},{4,12},{5,13},{6,14},{7,15},{8,0},{9,1},... | collective-permute-start | bytes 393224 | tf_op jit(solution)/shard_map/ppermute | solution.py:274
  160.4 4.9 %collective-permute-start.31 = (bf16[8,4096]{1,0:T(8,128)(2,1)S(1)}, bf16[8,4096]{1,0:T(8,128)(2,1)S(1)}, u32[]{:S(2)}, u32[]{:S(2)}) collective-permute-start(bf16[8,4096]{1,0:T(8,128)(2,1)S(1)} %slice.99), channel_id=1, source_target_pairs={{0,6},{1,7},{2,0},{3,1},{4,2},{5,3},{6,4},{7,5},{8,14},{9,15},{10,... | collective-permute-start | bytes 196616 | tf_op jit(solution)/shard_map/ppermute | solution.py:274
  163.8 7.2 %collective-permute-start.23 = (bf16[32,4096]{1,0:T(8,128)(2,1)S(1)}, bf16[32,4096]{1,0:T(8,128)(2,1)S(1)}, u32[]{:S(2)}, u32[]{:S(2)}) collective-permute-start(bf16[32,4096]{1,0:T(8,128)(2,1)S(1)} %get-tuple-element.127), channel_id=1, source_target_pairs={{0,6},{1,7},{2,0},{3,1},{4,2},{5,3},{6,4},{7,5},{8,14},{9,15},{10,... | collective-permute-start | bytes 786440 | tf_op jit(solution)/shard_map/ppermute | solution.py:274
  163.9 6.5 %collective-permute-start.24 = (bf16[32,4096]{1,0:T(8,128)(2,1)S(1)}, bf16[32,4096]{1,0:T(8,128)(2,1)S(1)}, u32[]{:S(2)}, u32[]{:S(2)}) collective-permute-start(bf16[32,4096]{1,0:T(8,128)(2,1)S(1)} %get-tuple-element.127), channel_id=1, source_target_pairs={{0,2},{1,3},{2,4},{3,5},{4,6},{5,7},{6,0},{7,1},{8,10},{9,11},{10,... | collective-permute-start | bytes 786440 | tf_op jit(solution)/shard_map/ppermute | solution.py:274
  165.3 10.7 %collective-permute-start.32 = (bf16[16,4096]{1,0:T(8,128)(2,1)S(1)}, bf16[16,4096]{1,0:T(8,128)(2,1)S(1)}, u32[]{:S(2)}, u32[]{:S(2)}) collective-permute-start(bf16[16,4096]{1,0:T(8,128)(2,1)S(1)} %pad_maximum_fusion.5), channel_id=1, source_target_pairs={{0,8},{1,9},{2,10},{3,11},{4,12},{5,13},{6,14},{7,15},{8,0},{9,1},... | collective-permute-start | bytes 393224 | tf_op jit(solution)/shard_map/ppermute | solution.py:274
  170.4 5.1 %collective-permute-start.25 = (bf16[16,4096]{1,0:T(8,128)(2,1)S(1)}, bf16[16,4096]{1,0:T(8,128)(2,1)S(1)}, u32[]{:S(2)}, u32[]{:S(2)}) collective-permute-start(bf16[16,4096]{1,0:T(8,128)(2,1)S(1)} %slice.94), channel_id=1, source_target_pairs={{0,2},{1,3},{2,4},{3,5},{4,6},{5,7},{6,0},{7,1},{8,10},{9,11},{10,... | collective-permute-start | bytes 393224 | tf_op jit(solution)/shard_map/ppermute | solution.py:274
  170.9 4.9 %collective-permute-start.26 = (bf16[16,4096]{1,0:T(8,128)(2,1)S(1)}, bf16[16,4096]{1,0:T(8,128)(2,1)S(1)}, u32[]{:S(2)}, u32[]{:S(2)}) collective-permute-start(bf16[16,4096]{1,0:T(8,128)(2,1)S(1)} %slice.95), channel_id=1, source_target_pairs={{0,6},{1,7},{2,0},{3,1},{4,2},{5,3},{6,4},{7,5},{8,14},{9,15},{10,... | collective-permute-start | bytes 393224 | tf_op jit(solution)/shard_map/ppermute | solution.py:274
  179.8 13.5 %collective-permute-start.33 = (f32[8,512]{1,0:T(8,128)S(1)}, f32[8,512]{1,0:T(8,128)S(1)}, u32[]{:S(2)}, u32[]{:S(2)}) collective-permute-start(f32[8,512]{1,0:T(8,128)S(1)} %get-tuple-element.83), channel_id=1, source_target_pairs={{0,1},{1,0},{2,3},{3,2},{4,5},{5,4},{6,7},{7,6},{8,9},{9,8},{10,11... | collective-permute-start | bytes 49160 | tf_op jit(solution)/shard_map/ppermute | solution.py:274
  194.0 20.5 %all-to-all-start.3 = ((bf16[16,16,256]{2,1,0:T(8,128)(2,1)}), bf16[16,16,256]{2,1,0:T(8,128)(2,1)S(1)}, u32[]{:S(2)}, u32[]{:S(2)}) async-start(bf16[16,16,256]{2,1,0:T(8,128)(2,1)} %shard_map.108), calls=%async_computation.3 | async-start | bytes 262144 | tf_op jit(solution)/shard_map/all_to_all | solution.py:382
  215.1 2.9 collective-permute-start.34
  221.4 3.3 %collective-permute-start.36 = (f32[16,4096]{1,0:T(8,128)S(1)}, f32[16,4096]{1,0:T(8,128)S(1)}, u32[]{:S(2)}, u32[]{:S(2)}) collective-permute-start(f32[16,4096]{1,0:T(8,128)S(1)} %shard_map.110.x_ref.refs_0_), channel_id=1, source_target_pairs={{0,1},{1,0},{2,3},{3,2},{4,5},{5,4},{6,7},{7,6},{8,9},{9,8},{10,11... | collective-permute-start | bytes 786440 | tf_op jit(solution)/shard_map/ppermute | solution.py:274
  222.0 9.3 %collective-permute-start.37 = (f32[16,4096]{1,0:T(8,128)S(1)}, f32[16,4096]{1,0:T(8,128)S(1)}, u32[]{:S(2)}, u32[]{:S(2)}) collective-permute-start(f32[16,4096]{1,0:T(8,128)S(1)} %shard_map.110.x_ref.refs_0_), channel_id=1, source_target_pairs={{1,16},{16,1},{3,18},{18,3},{5,20},{20,5},{7,22},{22,7},{9,24},{24... | collective-permute-start | bytes 786440 | tf_op jit(solution)/shard_map/ppermute | solution.py:403
  249.6 2.8 collective-permute-start.39
  253.6 3.0 collective-permute-start.40
  254.0 9.2 %collective-permute-start.41 = (f32[16,4096]{1,0:T(8,128)S(1)}, f32[16,4096]{1,0:T(8,128)S(1)}, u32[]{:S(2)}, u32[]{:S(2)}) collective-permute-start(f32[16,4096]{1,0:T(8,128)S(1)} %shard_map.114.x_ref.refs_0_), channel_id=1, source_target_pairs={{1,16},{16,1},{3,18},{18,3},{5,20},{20,5},{7,22},{22,7},{9,24},{24... | collective-permute-start | bytes 786440 | tf_op jit(solution)/shard_map/ppermute | solution.py:403
  256.5 15.1 %collective-permute-start.44 = (bf16[8,4096]{1,0:T(8,128)(2,1)S(1)}, bf16[8,4096]{1,0:T(8,128)(2,1)S(1)}, u32[]{:S(2)}, u32[]{:S(2)}) collective-permute-start(bf16[8,4096]{1,0:T(8,128)(2,1)S(1)} %bitcast.114), channel_id=1, source_target_pairs={{0,1},{1,0},{2,3},{3,2},{4,5},{5,4},{6,7},{7,6},{8,9},{9,8},{10,11... | collective-permute-start | bytes 196616 | tf_op jit(solution)/shard_map/ppermute | solution.py:274
  264.9 1.2 collective-permute-start.42
  266.8 15.1 %all-to-all-start.5 = ((bf16[16,16,256]{2,1,0:T(8,128)(2,1)}), bf16[16,16,256]{2,1,0:T(8,128)(2,1)S(1)}, u32[]{:S(2)}, u32[]{:S(2)}) async-start(bf16[16,16,256]{2,1,0:T(8,128)(2,1)} %shard_map.116), calls=%async_computation.5 | async-start | bytes 262144 | tf_op jit(solution)/shard_map/all_to_all | solution.py:382
  281.9 2.6 collective-permute-start.43
  289.0 21.0 %all-to-all-start.6 = ((f32[256,1,256]{2,1,0:T(1,128)}), f32[256,1,256]{2,1,0:T(1,128)S(1)}, u32[]{:S(2)}, u32[]{:S(2)}) async-start(f32[256,1,256]{2,1,0:T(1,128)} %copy.28), calls=%async_computation.6 | async-start | bytes 524288 | tf_op jit(solution)/shard_map/all_to_all | solution.py:426
  294.8 3.7 %collective-permute-start.45 = (f32[8,4096]{1,0:T(8,128)S(1)}, f32[8,4096]{1,0:T(8,128)S(1)}, u32[]{:S(2)}, u32[]{:S(2)}) collective-permute-start(f32[8,4096]{1,0:T(8,128)S(1)} %get-tuple-element.94), channel_id=1, source_target_pairs={{0,1},{1,0},{2,3},{3,2},{4,5},{5,4},{6,7},{7,6},{8,9},{9,8},{10,11... | collective-permute-start | bytes 393224 | tf_op jit(solution)/shard_map/ppermute | solution.py:274
  (11 other events, 197.7 us)

commit v3 on v2

--- a/solution.py
+++ b/solution.py
@@ -9,7 +9,7 @@
 from jax.sharding import PartitionSpec as P
 
 ITERS = 3
-VMEM_LIMIT = 24 * 1024 * 1024
+VMEM_LIMIT = 16 * 1024 * 1024
 NT = (((1,), (1,)), ((), ()))
 SMEM = pl.BlockSpec(memory_space=pltpu.SMEM)
 ANY = pl.BlockSpec(memory_space=pl.ANY)
@@ -53,7 +53,10 @@
         for q in range(chips):
             down = (q % ring + ring - y) % ring
             side = (q // ring + x) % 2
-            out_ref[TABLE + j * chips + q] = order[j] * chips + down * 2 + side
+            first = jnp.where(down == 1, 4, jnp.where(down == 3, 8, jnp.where(down == 2, 12, 0))) + side * 2
+            second = jnp.where(down == 1, 4, jnp.where(down == 3, 2, 0)) + side * 6
+            second = 16 + jnp.where(down == 2, 12 + side * 2, second)
+            out_ref[TABLE + j * chips + q] = jnp.where(order[j] % 2 == 0, first, second) + order[j] // 2
 
 
 def offer_kernel(plan_ref, occupied_ref, fixed_ref, offer_ref, sem):
@@ -74,56 +77,52 @@
     chip = dev // 2
     last = occupied_ref.shape[0] - 1
     rows = piece_refs[0].shape[0]
-    ends = jnp.logical_or(dev == 0, dev == 2 * chips - 1)
-
-    def run(copies):
+
+    def at(s):
+        return pl.ds(jnp.where(chip == 0, s, chips - 1 - s) * rows, rows)
+
+    @pl.when(plan_ref[CORE] == core)
+    def _():
+        copy = pltpu.make_async_copy(occupied_ref.at[plan_ref[SLOT], :, core], out_ref, sem.at[chips])
+        copy.start()
+        copy.wait()
+
+    @pl.when(plan_ref[CORE] != core)
+    def _():
+        @pl.loop(0, chips)
+        def _(k):
+            here = pl.ds(k * rows, rows)
+            out_ref[here] = offer_ref[here]
+
+    @pl.when(jnp.logical_or(dev == 0, dev == 2 * chips - 1))
+    def _():
+        copies = [
+            pltpu.make_async_copy(occupied_ref.at[core * last, at(s), core], ref, sem.at[s])
+            for s, ref in enumerate(piece_refs)
+        ]
         for copy in copies:
             copy.start()
         for copy in copies:
             copy.wait()
 
-    def pieces(source):
-        copies = []
+    @pl.when(jnp.logical_or(dev == 1, dev == 2 * chips - 2))
+    def _():
         for s, ref in enumerate(piece_refs):
-            at = jnp.where(chip == 0, s, chips - 1 - s) * rows
-            copies.append(pltpu.make_async_copy(source(pl.ds(at, rows)), ref, sem.at[s]))
-        return copies
-
-    mine = plan_ref[CORE] == core
-
-    @pl.when(mine)
-    def _():
-        run([pltpu.make_async_copy(occupied_ref.at[plan_ref[SLOT], :, core], out_ref, sem.at[chips])])
-
-    @pl.when(jnp.logical_not(mine))
-    def _():
-        run([pltpu.make_async_copy(offer_ref, out_ref, sem.at[chips])])
-
-    @pl.when(ends)
-    def _():
-        run(pieces(lambda at: occupied_ref.at[core * last, at, core]))
-
-    @pl.when(jnp.logical_not(ends))
-    def _():
-        run(pieces(lambda at: fixed_ref.at[at]))
+            ref[...] = fixed_ref[at(s)]
 
 
 def share_kernel(chips, plan_ref, *refs):
-    *piece_refs, out_ref, sem = refs
+    *piece_refs, zero_ref, last_ref = refs
     chip = plan_ref[DEV] // 2
     for s, ref in enumerate(piece_refs):
 
         @pl.when(chip == s)
         def _(ref=ref):
-            copy = pltpu.make_async_copy(ref, out_ref.at[0], sem.at[0])
-            copy.start()
-            copy.wait()
+            zero_ref[...] = ref[...]
 
         @pl.when(chip == chips - 1 - s)
         def _(ref=ref):
-            copy = pltpu.make_async_copy(ref, out_ref.at[1], sem.at[1])
-            copy.start()
-            copy.wait()
+            last_ref[...] = ref[...]
 
 
 def split(plan_ref, value, mine_ref, other_ref):
@@ -134,17 +133,20 @@
     other_ref[...] = jnp.where(low, second, first)
 
 
-def project(scale, plan_ref, resid_b, blocks_ref, mine_ref, other_ref):
-    part = lax.dot_general(resid_b, blocks_ref[...], NT, preferred_element_type=jnp.float32)
-    split(plan_ref, part * scale, mine_ref, other_ref)
-
-
-def first_kernel(scale, plan_ref, rhs_ref, blocks_ref, mine_ref, other_ref):
-    project(scale, plan_ref, rhs_ref[...].astype(jnp.bfloat16), blocks_ref, mine_ref, other_ref)
+def project(scale, plan_ref, resid_b, block_refs, mine_ref, other_ref):
+    parts = [
+        lax.dot_general(resid_b, ref[...], NT, preferred_element_type=jnp.float32) for ref in block_refs
+    ]
+    split(plan_ref, jnp.concatenate(parts, axis=1) * scale, mine_ref, other_ref)
+
+
+def first_kernel(scale, plan_ref, rhs_ref, first_ref, second_ref, mine_ref, other_ref):
+    blocks = (first_ref, second_ref)
+    project(scale, plan_ref, rhs_ref[...].astype(jnp.bfloat16), blocks, mine_ref, other_ref)
 
 
 def resid_kernel(
-    scale, row, plan_ref, x_ref, sib_ref, off_ref, rhs_ref, diag_ref, blocks_ref,
+    scale, row, plan_ref, x_ref, sib_ref, off_ref, rhs_ref, diag_ref, first_ref, second_ref,
     resid_ref, mine_ref, other_ref, rb_ref,
 ):
     cells = x_ref.shape[1]
@@ -162,7 +164,7 @@
         resid = rhs_ref[:, here] - (diag_ref[:, here] * x - 0.5 * beside)
         resid_ref[:, here] = resid
         rb_ref[:, here] = resid.astype(jnp.bfloat16)
-    project(scale, plan_ref, rb_ref[...], blocks_ref, mine_ref, other_ref)
+    project(scale, plan_ref, rb_ref[...], (first_ref, second_ref), mine_ref, other_ref)
 
 
 def stacked(value):
@@ -176,24 +178,24 @@
 
 
 def spread_kernel(mine_ref, other_ref, out_ref):
-    total = stacked(mine_ref[...] + other_ref[...]).astype(jnp.bfloat16)
+    total = mine_ref[...] + other_ref[...]
     for d in range(out_ref.shape[0]):
         out_ref[d] = total
 
 
 def total_kernel(parts_ref, coeff_ref, coeff_b_ref):
-    total = parts_ref[0].astype(jnp.float32)
+    total = parts_ref[0]
     for d in range(1, parts_ref.shape[0]):
-        total = total + parts_ref[d].astype(jnp.float32)
-    coeff_ref[...] = unstacked(total)
-    coeff_b_ref[...] = total.astype(jnp.bfloat16)
+        total = total + parts_ref[d]
+    coeff_ref[...] = total
+    coeff_b_ref[...] = stacked(total).astype(jnp.bfloat16)
 
 
 def update_kernel(scale, tile, has_x, last, root, plan_ref, mine_ref, other_ref, resid_ref, diag_ref, *refs):
     refs = list(refs)
     x_ref = refs.pop(0) if has_x else None
     psi_ref = refs.pop(0) if last else None
-    blocks_ref, *outs = refs
+    first_ref, second_ref, *outs = refs
     low = plan_ref[DEV] % 2 == 0
     mine = unstacked(mine_ref[...].astype(jnp.float32))
     other = unstacked(other_ref[...].astype(jnp.float32))
@@ -202,7 +204,13 @@
     cells = resid_ref.shape[1]
     for at in range(0, cells, tile):
         here = slice(at, at + tile)
-        corr = jnp.dot(coeff, blocks_ref[:, here], preferred_element_type=jnp.float32)
+        corr = 0.0
+        start = 0
+        for ref in (first_ref, second_ref):
+            rows = ref.shape[0]
+            some = coeff[:, start : start + rows]
+            corr = corr + jnp.dot(some, ref[:, here], preferred_element_type=jnp.float32)
+            start += rows
         x = (resid_ref[:, here] - corr * scale) / diag_ref[:, here]
         if has_x:
             x = x + x_ref[:, here]
@@ -211,10 +219,11 @@
             outs[0][:, here] = jnp.where(low, x[:half], x[half:])
             outs[1][:, here] = jnp.where(low, x[half:], x[:half])
             raw = jnp.sum(x * psi_ref[:, here].astype(jnp.float32), axis=0, keepdims=True) / root
-            wide = outs[2].shape[2]
+            rows, wide = outs[2].shape[2:]
             for k in range(tile // wide):
                 row = raw[:, k * wide : (k + 1) * wide]
-                outs[2][at // wide + k] = jnp.broadcast_to(row, outs[2].shape[1:])
+                spot = at // wide + k
+                outs[2][spot // rows, :, spot % rows, :] = jnp.broadcast_to(row, (outs[2].shape[1], wide))
         else:
             outs[0][:, here] = x
 
@@ -225,6 +234,17 @@
     for j in range(out_ref.shape[0] // share):
         at = pl.multiple_of(plan_ref[TABLE + j] * share, share)
         out_ref[j * share : (j + 1) * share] = rows_ref[pl.ds(at, share)]
+
+
+def finish_kernel(z_part, plan_ref, weights_ref, terms_ref, out_ref):
+    width = terms_ref.shape[2]
+    shift = lax.rem(width - plan_ref[DEV] * z_part, width)
+    for k in range(terms_ref.shape[1]):
+        rows = lax.dot_general(
+            weights_ref[...], terms_ref[:, k, :], (((1,), (0,)), ((), ())),
+            precision=lax.Precision.HIGHEST, preferred_element_type=jnp.float32,
+        )
+        out_ref[:, k, :] = pltpu.roll(rows, shift, 1)[:, :z_part]
 
 
 def call(kernel, out_shape, in_specs=None, out_specs=None, scratch=()):
@@ -286,7 +306,7 @@
     plane_shape = shape((blk_rows, rows_y, rows_z), jnp.bfloat16)
     piece_shape = shape((share, rows_y, rows_z), jnp.bfloat16)
     fixed, offer = call(
-        offer_kernel, (plane_shape, plane_shape), [SMEM, ANY], (ANY, ANY),
+        offer_kernel, (plane_shape, plane_shape), [SMEM, ANY], (VMEM, VMEM),
         (pltpu.SemaphoreType.DMA((2,)),),
     )(plan, occupied)
     fixed = permute(fixed, [(0, 1), (n_orb - 1, n_orb - 2)])
@@ -294,8 +314,8 @@
     *pieces, offer = call(
         functools.partial(pick_kernel, chips),
         [piece_shape] * chips + [plane_shape],
-        [SMEM, ANY, ANY, ANY],
-        [ANY] * (chips + 1),
+        [SMEM, ANY, VMEM, VMEM],
+        [VMEM] * (chips + 1),
         (pltpu.SemaphoreType.DMA((chips + 1,)),),
     )(plan, occupied, fixed, offer)
 
@@ -306,58 +326,65 @@
         got.append(permute(pieces[s], pairs))
     fixed_shares = call(
         functools.partial(share_kernel, chips),
-        shape((2, share, rows_y, rows_z), jnp.bfloat16),
-        [SMEM] + [ANY] * chips,
-        ANY,
-        (pltpu.SemaphoreType.DMA((2,)),),
-    )(plan, *got).reshape(2, share, cells)
+        (piece_shape, piece_shape),
+        [SMEM] + [VMEM] * chips,
+    )(plan, *got)
 
     def scatter(value):
         value = value.reshape(chips, share, rows_y, rows_z)
         return lax.all_to_all(value, "orb", 0, 0, axis_index_groups=groups, tiled=True)
 
     def take(value, owner):
-        return lax.dynamic_index_in_dim(value, owner, 0, keepdims=False).reshape(share, cells)
-
-    def apart(plan, occupied, offer):
-        offered = scatter(offer)
-        return tuple(take(offered, plan[CHIP + k]) for k in range(nproj - 2))
-
-    def together(plan, occupied, offer):
+        return lax.dynamic_index_in_dim(value, owner, 0, keepdims=False)
+
+    def apart(plan, occupied, offered):
+        return take(offered, plan[CHIP + 1])
+
+    def together(plan, occupied, offered):
         def plane_of(slot, plane):
             dims = (1, blk_rows, 1, rows_y, rows_z)
-            return lax.dynamic_slice(occupied, (slot, 0, plane, 0, 0), dims).reshape(offer.shape)
-
-        out = [take(scatter(offer), plan[CHIP])]
-        for k in range(1, nproj - 2):
-            mid = plan[MID + k]
-            other = permute(plane_of(mid % per_dev, 1 - core), swap_core)
-            here = (mid // per_dev) % 2 == core
-            again = jnp.where(here, plane_of(mid % per_dev, core), other)
-            out.append(take(scatter(again), plan[CHIP + k]))
-        return tuple(out)
-
-    mid_shares = lax.cond(plan[SAME] == 1, together, apart, plan, occupied, offer)
-
-    def gather(one, two):
-        own = jnp.concatenate([one, permute(one, swap_x)], axis=0)
-        above = permute(own, up_y)
-        below = permute(own, down_y)
-        near_y = permute(two, up_y)
-        back_y = permute(two, down_y)
-        far0 = permute(above[:share], up_y)
-        far1 = permute(below[share:], down_y)
-        half = share // 2
-        line = jnp.concatenate([two, back_y, near_y], axis=0)
-        line_x = permute(line, swap_x)
-        far = jnp.concatenate([permute(near_y[:half], up_y), permute(back_y[half:], down_y)], axis=0)
-        far_x = permute(far, swap_x)
-        first = [own, below, far0, far1, above]
-        second = [two, line_x[:share], back_y, line_x[share : 2 * share], far, far_x, near_y, line_x[2 * share :]]
-        return first, second
-
-    held = gather(fixed_shares[0], fixed_shares[1]) + gather(*mid_shares)
-    blocks = jnp.concatenate([piece for part in held for piece in part], axis=0)
+            return lax.dynamic_slice(occupied, (slot, 0, plane, 0, 0), dims).reshape(plane_shape.shape)
+
+        mid = plan[MID + 1]
+        other = permute(plane_of(mid % per_dev, 1 - core), swap_core)
+        here = (mid // per_dev) % 2 == core
+        again = scatter(jnp.where(here, plane_of(mid % per_dev, core), other))
+        return take(again, plan[CHIP + 1])
+
+    offered = scatter(offer)
+    mid_shares = [
+        take(offered, plan[CHIP]),
+        lax.cond(plan[SAME] == 1, together, apart, plan, occupied, offered),
+    ]
+
+    def flat(one, two):
+        return jnp.concatenate([one, two], axis=0).reshape(2 * share, cells)
+
+    xs = flat(fixed_shares[0], mid_shares[0])
+    ys = flat(fixed_shares[1], mid_shares[1])
+    xs, ys = lax.optimization_barrier((xs, ys))
+    xs_x = permute(xs, swap_x)
+    ys_up = permute(ys, up_y)
+    ys_down = permute(ys, down_y)
+    xs_x, ys_up, ys_down = lax.optimization_barrier((xs_x, ys_up, ys_down))
+    own = jnp.concatenate([xs, xs_x], axis=0)
+    line = jnp.concatenate([ys, ys_up, ys_down], axis=0)
+    line_x = permute(line, swap_x)
+    above = permute(own, up_y)
+    below = permute(own, down_y)
+    far_up = permute(ys_up[:share], up_y)
+    far_down = permute(ys_down[share:], down_y)
+    line_x, above, below, far_up, far_down = lax.optimization_barrier(
+        (line_x, above, below, far_up, far_down)
+    )
+    far = jnp.concatenate([far_up, far_down], axis=0)
+    far_x = permute(far, swap_x)
+    own_up = permute(above[: 2 * share], up_y)
+    own_down = permute(below[2 * share :], down_y)
+    blocks = [
+        jnp.concatenate([own, below, above, own_up, own_down], axis=0),
+        jnp.concatenate([line, line_x, far, far_x], axis=0),
+    ]
 
     def both(field):
         mine = lax.dynamic_index_in_dim(field, core, 1, keepdims=False).reshape(local_orbs, cells)
@@ -378,7 +405,7 @@
 
     def total(mine, other):
         other = permute(other, swap_core)
-        spread = call(spread_kernel, shape((n_dom,) + flat_shape, jnp.bfloat16))(mine, other)
+        spread = call(spread_kernel, shape((n_dom,) + half_shape.shape))(mine, other)
         parts = lax.all_to_all(spread, "dom", 0, 0, tiled=True)
         coeff, coeff_b = call(total_kernel, (half_shape, shape(flat_shape, jnp.bfloat16)))(parts)
         return coeff, coeff_b, permute(coeff_b, swap_core)
@@ -396,38 +423,42 @@
             mine, other = call(
                 functools.partial(first_kernel, scale),
                 (half_shape, half_shape),
-                [SMEM, VMEM, VMEM],
-            )(plan, rhs_wide, blocks)
+                [SMEM] + [VMEM] * 3,
+            )(plan, rhs_wide, *blocks)
         else:
             sib = permute(x, swap_core)
             off = lax.ppermute(x, ("dom", "orb"), across)
             resid, mine, other = call(
                 functools.partial(resid_kernel, scale, rows_z),
                 (field_shape, half_shape, half_shape),
-                [SMEM] + [VMEM] * 6,
+                [SMEM] + [VMEM] * 7,
                 scratch=(pltpu.VMEM((wide, cells), jnp.bfloat16),),
-            )(plan, x, sib, off, rhs_wide, diag, blocks)
+            )(plan, x, sib, off, rhs_wide, diag, *blocks)
         coeff, coeff_b, coeff_o = total(mine, other)
         final = step == ITERS - 1
         extra = ([x] if step else []) + ([psi_wide] if final else [])
         outs = [field_shape]
         if final:
-            outs = [shape((local_orbs, cells))] * 2 + [shape((n_dom, n_orb, cells // n_dom))]
+            outs = [shape((local_orbs, cells))] * 2 + [shape((n_dom, n_orb, rows_y // n_dom, rows_z))]
         x, *rest = call(
             functools.partial(update_kernel, scale, 512, step > 0, final, math.sqrt(width)),
             outs,
-            [SMEM] + [VMEM] * (5 + len(extra)),
-        )(plan, coeff_b, coeff_o, resid, diag, *extra, blocks)
+            [SMEM] + [VMEM] * (6 + len(extra)),
+        )(plan, coeff_b, coeff_o, resid, diag, *extra, *blocks)
     other, raw = rest
 
     weights = jnp.broadcast_to(
         smoother.reshape(2 * n_dom, n_dom, 1, 2), (2 * n_dom, n_dom, chips, 2)
     ).reshape(2 * n_dom, n_dom * n_orb)
-    terms = lax.all_to_all(raw.reshape(n_dom * n_orb, -1), ("dom", "orb"), 0, 0, tiled=True)
-    smoothed = jnp.dot(weights, terms, precision=lax.Precision.HIGHEST)
-    smoothed = smoothed.reshape(2 * n_dom, rows_y // n_dom, rows_z)
+    terms = lax.all_to_all(
+        raw.reshape((n_dom * n_orb,) + raw.shape[2:]), ("dom", "orb"), 0, 0, tiled=True
+    )
     z_part = rows_z // n_orb
-    gradient = lax.dynamic_slice_in_dim(smoothed, o * z_part, z_part, axis=2)
+    gradient = call(
+        functools.partial(finish_kernel, z_part),
+        shape((2 * n_dom, rows_y // n_dom, z_part)),
+        [SMEM, VMEM, VMEM],
+    )(plan, weights, terms)
 
     other = permute(other, swap_core)
     solution = jnp.stack([jnp.where(low, x, other), jnp.where(low, other, x)], axis=1)

time: 312 us -> 225 us (0.72)
  starting transfers between devices: 127 us -> 83.7 us
  Pallas kernels: 50.9 us -> 21.1 us
  waiting for transfers between devices: 94.3 us -> 83.9 us
  local copies, waits for them, and re-layouts: 18.2 us -> 9.01 us
  blocking collectives: 14.6 us -> 17.8 us
    ppermute x43 -> x32, starting transfers between devices: 96.9 us -> 52.2 us  [permute(): return lax.ppermute(value, 'orb', pairs)]
    pallas_call x5 -> x6, Pallas kernels: 35.7 us -> 6.41 us  [the longest x1 3.34 us: per_device(): call(offer_kernel, (plane_shape, plane_shape), [SMEM, ANY], (VMEM, VMEM),...]
    all_to_all x1, waiting for transfers between devices: 8.78 us -> 0.01 us  [scatter(): lax.all_to_all(value, 'orb', 0, 0, axis_index_groups=groups, tiled=True)]
    cond x2 -> x0, local copies, waits for them, and re-layouts: 4.56 us -> none
    ppermute x43 -> x32, waiting for transfers between devices: 41.4 us -> 37 us  [permute(): return lax.ppermute(value, 'orb', pairs)]
    all_to_all x1, blocking collectives: 14.6 us -> 17.8 us  [total(): parts = lax.all_to_all(spread, 'dom', 0, 0, tiled=True)]
    unnamed x57 -> x38, local copies, waits for them, and re-layouts: 8.7 us -> 7.45 us
  transfers between devices with their start and end apart: 49 -> 38, of which waited for: 25 -> 21; matrix products, arithmetic and copies ran while one was open for 4% -> 3% of each run, Pallas kernels for 2% -> 3%
where the time goes in v3:
time: 225 us; the launch traced here: 224 us
  waiting for transfers between devices  83.9 us (37%)
  starting transfers between devices  83.7 us (37%)
  Pallas kernels  21.1 us (9%)
  blocking collectives  17.8 us (8%)
  local copies, waits for them, and re-layouts  9.01 us (4%)
  between operations  3.63 us (2%)
  other arithmetic  3.14 us (1%)
    ppermute x32, starting transfers between devices, permute(): return lax.ppermute(value, 'orb', pairs)  52.2 us
    ppermute x32, waiting for transfers between devices, permute(): return lax.ppermute(value, 'orb', pairs)  37 us
    all_to_all x2, waiting for transfers between devices, total(): parts = lax.all_to_all(spread, 'dom', 0, 0, tiled=True)  22.6 us
    all_to_all x1, blocking collectives, total(): parts = lax.all_to_all(spread, 'dom', 0, 0, tiled=True)  17.8 us
    all_to_all x2, starting transfers between devices, total(): parts = lax.all_to_all(spread, 'dom', 0, 0, tiled=True)  15.8 us
    ppermute x2, waiting for transfers between devices, per_device(): off = lax.ppermute(x, ('dom', 'orb'), across)  13.7 us
    all_to_all x1, waiting for transfers between devices, per_device(): lax.all_to_all(raw.reshape((n_dom * n_orb,) + raw.shape[2:]), ('dom', 'or...  10.6 us
    unnamed x38, local copies, waits for them, and re-layouts  7.45 us
  transfers between devices with their start and end apart: 38, of which 21 were waited for; matrix products, arithmetic and copies ran while one was open for 3% of the time, Pallas kernels for 3%

profile of v3, /device:TPU:1, one launch (start us, length us, event | category | flops | bytes accessed | tf_op | source)
XLA Modules:
  0.0 224.3 jit_solution(3852662760462151662)
XLA Ops:
  1.3 1.3 shard_map.103.plan_ref
  2.6 3.3 %shard_map.104 = (bf16[128,32,128]{2,1,0:T(8,128)(2,1)}, bf16[128,32,128]{2,1,0:T(8,128)(2,1)S(1)}) custom-call(s32[40]{0:T(128)S(1)} %shard_map.103.plan_ref, bf16[2,128,2,32,128]{4,3,2,1,0:T(8,128)(2,1)} %occupied_ref.3), custom_call_target="tpu_custom_call" | custom-call | tf_op jit(solution)/shard_map/pallas_call | solution.py:308
  5.9 1.3 collective-permute-start.2
  7.2 3.2 %collective-permute-start.3 = (bf16[128,32,128]{2,1,0:T(8,128)(2,1)S(1)}, bf16[128,32,128]{2,1,0:T(8,128)(2,1)S(1)}, u32[]{:S(2)}, u32[]{:S(2)}) collective-permute-start(bf16[128,32,128]{2,1,0:T(8,128)(2,1)S(1)} %get-tuple-element.61), channel_id=1, source_target_pairs={{0,1},{1,0},{2,3},{3,2},{4,5},{5,4},{6,7},{7,6},{8,9},{9,8},{10,11... | collective-permute-start | bytes 3145736 | tf_op jit(solution)/shard_map/ppermute | solution.py:294
  15.1 1.8 shard_map.105
  16.9 5.5 %all-to-all-start.1 = ((bf16[8,16,32,128]{3,2,1,0:T(8,128)(2,1)}), bf16[8,16,32,128]{3,2,1,0:T(8,128)(2,1)S(1)}, u32[]{:S(2)}, u32[]{:S(2)}) async-start(bf16[8,16,32,128]{3,2,1,0:T(8,128)(2,1)} %bitcast.9), calls=%async_computation.1 | async-start | bytes 2097152 | tf_op jit(solution)/shard_map/all_to_all | solution.py:335
  22.4 3.4 %collective-permute-start.4 = (bf16[16,32,128]{2,1,0:T(8,128)(2,1)S(1)}, bf16[16,32,128]{2,1,0:T(8,128)(2,1)S(1)}, u32[]{:S(2)}, u32[]{:S(2)}) collective-permute-start(bf16[16,32,128]{2,1,0:T(8,128)(2,1)S(1)} %get-tuple-element.63), channel_id=1, source_target_pairs={{0,2},{1,3},{14,12},{15,13},{16,18},{17,19},{30,28},{31,29},{32,34... | collective-permute-start | bytes 393224 | tf_op jit(solution)/shard_map/ppermute | solution.py:294
  25.8 2.2 collective-permute-start.5
  29.0 1.3 collective-permute-start.6
  30.3 1.3 collective-permute-start.7
  31.6 1.3 collective-permute-start.8
  32.9 3.3 %collective-permute-done.4.refs_1_ = bf16[16,32,128]{2,1,0:T(8,128)(2,1)S(1)} collective-permute-done((bf16[16,32,128]{2,1,0:T(8,128)(2,1)S(1)}, bf16[16,32,128]{2,1,0:T(8,128)(2,1)S(1)}, u32[]{:S(2)}, u32[]{:S(2)}) %collective-permute-start.4) | collective-permute-done | bytes 131104 | tf_op jit(solution)/shard_map/ppermute | solution.py:294
  36.2 8.3 %collective-permute-start.9 = (bf16[16,32,128]{2,1,0:T(8,128)(2,1)S(1)}, bf16[16,32,128]{2,1,0:T(8,128)(2,1)S(1)}, u32[]{:S(2)}, u32[]{:S(2)}) collective-permute-start(bf16[16,32,128]{2,1,0:T(8,128)(2,1)S(1)} %get-tuple-element.68), channel_id=1, source_target_pairs={{0,12},{1,13},{14,2},{15,3},{16,28},{17,29},{30,18},{31,19},{32,44... | collective-permute-start | bytes 393224 | tf_op jit(solution)/shard_map/ppermute | solution.py:294
  44.5 1.9 collective-permute-start.10
  46.7 5.9 %collective-permute-done.10.refs_7_ = bf16[16,32,128]{2,1,0:T(8,128)(2,1)S(1)} collective-permute-done((bf16[16,32,128]{2,1,0:T(8,128)(2,1)S(1)}, bf16[16,32,128]{2,1,0:T(8,128)(2,1)S(1)}, u32[]{:S(2)}, u32[]{:S(2)}) %collective-permute-start.10) | collective-permute-done | bytes 131104 | tf_op jit(solution)/shard_map/ppermute | solution.py:294
  53.3 2.6 %conditional.1 = (bf16[16,32,128]{2,1,0:T(8,128)(2,1)S(1)}) conditional(s32[]{:T(128)} %bitcast.11, (s32[40]{0:T(128)S(1)}, bf16[8,16,32,128]{3,2,1,0:T(8,128)(2,1)S(1)}) %tuple.18, (s32[40]{0:T(128)S(1)}, s32[]{:T(128)}, bf16[2,128,2,32,128]{4,3,2,1,0:T(8,128)(2,1)}) %tuple.19), branch_computations={%region_0.1_spmd, %region_1.2_spmd} | conditional | flops 524332 | bytes 12845626 | solution.py:357
  56.4 2.7 %collective-permute-start.13 = (bf16[32,4096]{1,0:T(8,128)(2,1)S(1)}, bf16[32,4096]{1,0:T(8,128)(2,1)S(1)}, u32[]{:S(2)}, u32[]{:S(2)}) collective-permute-start(bf16[32,4096]{1,0:T(8,128)(2,1)S(1)} %bitcast.69), channel_id=1, source_target_pairs={{0,6},{1,7},{2,0},{3,1},{4,2},{5,3},{6,4},{7,5},{8,14},{9,15},{10,... | collective-permute-start | bytes 786440 | tf_op jit(solution)/shard_map/ppermute | solution.py:294
  59.1 3.2 %collective-permute-done.11 = bf16[32,4096]{1,0:T(8,128)(2,1)S(1)} collective-permute-done((bf16[32,4096]{1,0:T(8,128)(2,1)S(1)}, bf16[32,4096]{1,0:T(8,128)(2,1)S(1)}, u32[]{:S(2)}, u32[]{:S(2)}) %collective-permute-start.11) | collective-permute-done | bytes 262176 | tf_op jit(solution)/shard_map/ppermute | solution.py:294
  62.3 1.3 collective-permute-done.12
  63.7 2.7 %collective-permute-start.16 = (bf16[64,4096]{1,0:T(8,128)(2,1)S(1)}, bf16[64,4096]{1,0:T(8,128)(2,1)S(1)}, u32[]{:S(2)}, u32[]{:S(2)}) collective-permute-start(bf16[64,4096]{1,0:T(8,128)(2,1)S(1)} %get-tuple-element.112), channel_id=1, source_target_pairs={{0,6},{1,7},{2,0},{3,1},{4,2},{5,3},{6,4},{7,5},{8,14},{9,15},{10,... | collective-permute-start | bytes 1572872 | tf_op jit(solution)/shard_map/ppermute | solution.py:294
  67.7 2.7 %collective-permute-start.18 = (bf16[16,4096]{1,0:T(8,128)(2,1)S(1)}, bf16[16,4096]{1,0:T(8,128)(2,1)S(1)}, u32[]{:S(2)}, u32[]{:S(2)}) collective-permute-start(bf16[16,4096]{1,0:T(8,128)(2,1)S(1)} %slice.30), channel_id=1, source_target_pairs={{0,6},{1,7},{2,0},{3,1},{4,2},{5,3},{6,4},{7,5},{8,14},{9,15},{10,... | collective-permute-start | bytes 393224 | tf_op jit(solution)/shard_map/ppermute | solution.py:294
  70.4 8.1 %collective-permute-done.17 = bf16[16,4096]{1,0:T(8,128)(2,1)S(1)} collective-permute-done((bf16[16,4096]{1,0:T(8,128)(2,1)S(1)}, bf16[16,4096]{1,0:T(8,128)(2,1)S(1)}, u32[]{:S(2)}, u32[]{:S(2)}) %collective-permute-start.17) | collective-permute-done | bytes 131104 | tf_op jit(solution)/shard_map/ppermute | solution.py:294
  78.5 3.9 %collective-permute-done.14 = bf16[96,4096]{1,0:T(8,128)(2,1)S(1)} collective-permute-done((bf16[96,4096]{1,0:T(8,128)(2,1)S(1)}, bf16[96,4096]{1,0:T(8,128)(2,1)S(1)}, u32[]{:S(2)}, u32[]{:S(2)}) %collective-permute-start.14) | collective-permute-done | bytes 786464 | tf_op jit(solution)/shard_map/ppermute | solution.py:294
  82.6 2.7 %collective-permute-start.20 = (bf16[32,4096]{1,0:T(8,128)(2,1)S(1)}, bf16[32,4096]{1,0:T(8,128)(2,1)S(1)}, u32[]{:S(2)}, u32[]{:S(2)}) collective-permute-start(bf16[32,4096]{1,0:T(8,128)(2,1)S(1)} %slice.32), channel_id=1, source_target_pairs={{0,6},{1,7},{2,0},{3,1},{4,2},{5,3},{6,4},{7,5},{8,14},{9,15},{10,... | collective-permute-start | bytes 786440 | tf_op jit(solution)/shard_map/ppermute | solution.py:294
  86.5 2.6 %collective-permute-done.19 = bf16[32,4096]{1,0:T(8,128)(2,1)S(1)} collective-permute-done((bf16[32,4096]{1,0:T(8,128)(2,1)S(1)}, bf16[32,4096]{1,0:T(8,128)(2,1)S(1)}, u32[]{:S(2)}, u32[]{:S(2)}) %collective-permute-start.19) | collective-permute-done | bytes 262176 | tf_op jit(solution)/shard_map/ppermute | solution.py:294
  89.1 2.1 collective-permute-done.21
  91.2 1.7 shard_map.107
  92.9 5.6 %collective-permute-start.22 = (f32[8,512]{1,0:T(8,128)S(1)}, f32[8,512]{1,0:T(8,128)S(1)}, u32[]{:S(2)}, u32[]{:S(2)}) collective-permute-start(f32[8,512]{1,0:T(8,128)S(1)} %get-tuple-element.84), channel_id=1, source_target_pairs={{0,1},{1,0},{2,3},{3,2},{4,5},{5,4},{6,7},{7,6},{8,9},{9,8},{10,11... | collective-permute-start | bytes 49160 | tf_op jit(solution)/shard_map/ppermute | solution.py:294
  100.1 10.6 %all-to-all-start.2 = ((f32[16,8,512]{2,1,0:T(8,128)}), f32[16,8,512]{2,1,0:T(8,128)S(1)}, u32[]{:S(2)}, u32[]{:S(2)}) async-start(f32[16,8,512]{2,1,0:T(8,128)} %shard_map.108), calls=%async_computation.2 | async-start | bytes 524288 | tf_op jit(solution)/shard_map/all_to_all | solution.py:409
  112.6 10.7 %all-to-all-done.2.parts_ref = f32[16,8,512]{2,1,0:T(8,128)S(1)} async-done(((f32[16,8,512]{2,1,0:T(8,128)}), f32[16,8,512]{2,1,0:T(8,128)S(1)}, u32[]{:S(2)}, u32[]{:S(2)}) %all-to-all-start.2) | async-done | bytes 262176 | tf_op jit(solution)/shard_map/all_to_all | solution.py:409
  124.0 1.9 collective-permute-start.23
  126.7 1.6 copy-done.1
  129.9 2.3 %collective-permute-start.26 = (f32[16,4096]{1,0:T(8,128)S(1)}, f32[16,4096]{1,0:T(8,128)S(1)}, u32[]{:S(2)}, u32[]{:S(2)}) collective-permute-start(f32[16,4096]{1,0:T(8,128)S(1)} %shard_map.110.x_ref.refs_0_), channel_id=1, source_target_pairs={{1,16},{16,1},{3,18},{18,3},{5,20},{20,5},{7,22},{22,7},{9,24},{24... | collective-permute-start | bytes 786440 | tf_op jit(solution)/shard_map/ppermute | solution.py:430
  132.2 7.0 %collective-permute-done.26.off_ref = f32[16,4096]{1,0:T(8,128)S(1)} collective-permute-done((f32[16,4096]{1,0:T(8,128)S(1)}, f32[16,4096]{1,0:T(8,128)S(1)}, u32[]{:S(2)}, u32[]{:S(2)}) %collective-permute-start.26) | collective-permute-done | bytes 262176 | tf_op jit(solution)/shard_map/ppermute | solution.py:430
  139.2 1.8 shard_map.111
  142.2 17.8 %all_to_all.29.parts_ref = f32[16,8,512]{2,1,0:T(8,128)S(1)} all-to-all(f32[16,8,512]{2,1,0:T(8,128)S(1)} %shard_map.112), channel_id=1, replica_groups=mesh['dom'=16,'orb'=16] {'dom'}, dimensions={0} | all-to-all | bytes 524288 | tf_op jit(solution)/shard_map/all_to_all | solution.py:409
  160.7 1.6 collective-permute-start.28
  164.7 2.3 %collective-permute-start.30 = (f32[16,4096]{1,0:T(8,128)S(1)}, f32[16,4096]{1,0:T(8,128)S(1)}, u32[]{:S(2)}, u32[]{:S(2)}) collective-permute-start(f32[16,4096]{1,0:T(8,128)S(1)} %shard_map.114.x_ref.refs_0_), channel_id=1, source_target_pairs={{1,16},{16,1},{3,18},{18,3},{5,20},{20,5},{7,22},{22,7},{9,24},{24... | collective-permute-start | bytes 786440 | tf_op jit(solution)/shard_map/ppermute | solution.py:430
  167.2 6.7 %collective-permute-done.30.off_ref = f32[16,4096]{1,0:T(8,128)S(1)} collective-permute-done((f32[16,4096]{1,0:T(8,128)S(1)}, f32[16,4096]{1,0:T(8,128)S(1)}, u32[]{:S(2)}, u32[]{:S(2)}) %collective-permute-start.30) | collective-permute-done | bytes 262176 | tf_op jit(solution)/shard_map/ppermute | solution.py:430
  173.9 1.8 shard_map.115
  177.6 5.2 %all-to-all-start.4 = ((f32[16,8,512]{2,1,0:T(8,128)}), f32[16,8,512]{2,1,0:T(8,128)S(1)}, u32[]{:S(2)}, u32[]{:S(2)}) async-start(f32[16,8,512]{2,1,0:T(8,128)} %shard_map.116), calls=%async_computation.4 | async-start | bytes 524288 | tf_op jit(solution)/shard_map/all_to_all | solution.py:409
  183.6 11.9 %all-to-all-done.4.parts_ref = f32[16,8,512]{2,1,0:T(8,128)S(1)} async-done(((f32[16,8,512]{2,1,0:T(8,128)}), f32[16,8,512]{2,1,0:T(8,128)S(1)}, u32[]{:S(2)}, u32[]{:S(2)}) %all-to-all-start.4) | async-done | bytes 262176 | tf_op jit(solution)/shard_map/all_to_all | solution.py:409
  195.6 1.7 collective-permute-start.32
  198.1 1.6 copy-done.3
  199.7 2.0 shard_map.118
  201.7 5.6 %all-to-all-start.5 = ((f32[256,2,128]{2,1,0:T(2,128)}), f32[256,2,128]{2,1,0:T(2,128)S(1)}, u32[]{:S(2)}, u32[]{:S(2)}) async-start(f32[256,2,128]{2,1,0:T(2,128)} %bitcast.20), calls=%async_computation.5 | async-start | bytes 524288 | tf_op jit(solution)/shard_map/all_to_all | solution.py:453
  207.3 2.4 %collective-permute-start.34 = (f32[8,4096]{1,0:T(8,128)S(1)}, f32[8,4096]{1,0:T(8,128)S(1)}, u32[]{:S(2)}, u32[]{:S(2)}) collective-permute-start(f32[8,4096]{1,0:T(8,128)S(1)} %get-tuple-element.95), channel_id=1, source_target_pairs={{0,1},{1,0},{2,3},{3,2},{4,5},{5,4},{6,7},{7,6},{8,9},{9,8},{10,11... | collective-permute-start | bytes 393224 | tf_op jit(solution)/shard_map/ppermute | solution.py:294
  212.1 10.6 %all-to-all-done.5.terms_ref = f32[256,2,128]{2,1,0:T(2,128)S(1)} async-done(((f32[256,2,128]{2,1,0:T(2,128)}), f32[256,2,128]{2,1,0:T(2,128)S(1)}, u32[]{:S(2)}, u32[]{:S(2)}) %all-to-all-start.5) | async-done | bytes 262176 | tf_op jit(solution)/shard_map/all_to_all | solution.py:453
  (117 shorter events, 27.4 us)
Async XLA Ops:
  0.6 0.7 copy-start.4
  5.9 9.2 %collective-permute-start.2 = (bf16[128,32,128]{2,1,0:T(8,128)(2,1)}, bf16[128,32,128]{2,1,0:T(8,128)(2,1)S(1)}, u32[]{:S(2)}, u32[]{:S(2)}) collective-permute-start(bf16[128,32,128]{2,1,0:T(8,128)(2,1)} %get-tuple-element.60), channel_id=1, source_target_pairs={{0,1},{15,14},{16,17},{31,30},{32,33},{47,46},{48,49},{63,62},{64,... | collective-permute-start | bytes 3145736 | tf_op jit(solution)/shard_map/ppermute | solution.py:294
  7.2 7.9 %collective-permute-start.3 = (bf16[128,32,128]{2,1,0:T(8,128)(2,1)S(1)}, bf16[128,32,128]{2,1,0:T(8,128)(2,1)S(1)}, u32[]{:S(2)}, u32[]{:S(2)}) collective-permute-start(bf16[128,32,128]{2,1,0:T(8,128)(2,1)S(1)} %get-tuple-element.61), channel_id=1, source_target_pairs={{0,1},{1,0},{2,3},{3,2},{4,5},{5,4},{6,7},{7,6},{8,9},{9,8},{10,11... | collective-permute-start | bytes 3145736 | tf_op jit(solution)/shard_map/ppermute | solution.py:294
  12.1 15.9 %collective-permute-start.1 = (f32[8,4096]{1,0:T(8,128)}, f32[8,4096]{1,0:T(8,128)}, u32[]{:S(2)}, u32[]{:S(2)}) collective-permute-start(f32[8,4096]{1,0:T(8,128)} %bitcast.64), channel_id=1, source_target_pairs={{0,1},{1,0},{2,3},{3,2},{4,5},{5,4},{6,7},{7,6},{8,9},{9,8},{10,11... | collective-permute-start | bytes 393224 | tf_op jit(solution)/shard_map/ppermute | solution.py:294
  16.9 36.3 %all-to-all-start.1 = ((bf16[8,16,32,128]{3,2,1,0:T(8,128)(2,1)}), bf16[8,16,32,128]{3,2,1,0:T(8,128)(2,1)S(1)}, u32[]{:S(2)}, u32[]{:S(2)}) async-start(bf16[8,16,32,128]{3,2,1,0:T(8,128)(2,1)} %bitcast.9), calls=%async_computation.1 | async-start | bytes 2097152 | tf_op jit(solution)/shard_map/all_to_all | solution.py:335
  22.4 13.7 %collective-permute-start.4 = (bf16[16,32,128]{2,1,0:T(8,128)(2,1)S(1)}, bf16[16,32,128]{2,1,0:T(8,128)(2,1)S(1)}, u32[]{:S(2)}, u32[]{:S(2)}) collective-permute-start(bf16[16,32,128]{2,1,0:T(8,128)(2,1)S(1)} %get-tuple-element.63), channel_id=1, source_target_pairs={{0,2},{1,3},{14,12},{15,13},{16,18},{17,19},{30,28},{31,29},{32,34... | collective-permute-start | bytes 393224 | tf_op jit(solution)/shard_map/ppermute | solution.py:294
  25.8 18.7 %collective-permute-start.5 = (bf16[16,32,128]{2,1,0:T(8,128)(2,1)S(1)}, bf16[16,32,128]{2,1,0:T(8,128)(2,1)S(1)}, u32[]{:S(2)}, u32[]{:S(2)}) collective-permute-start(bf16[16,32,128]{2,1,0:T(8,128)(2,1)S(1)} %get-tuple-element.64), channel_id=1, source_target_pairs={{0,4},{1,5},{14,10},{15,11},{16,20},{17,21},{30,26},{31,27},{32,36... | collective-permute-start | bytes 393224 | tf_op jit(solution)/shard_map/ppermute | solution.py:294
  29.0 17.5 %collective-permute-start.6 = (bf16[16,32,128]{2,1,0:T(8,128)(2,1)S(1)}, bf16[16,32,128]{2,1,0:T(8,128)(2,1)S(1)}, u32[]{:S(2)}, u32[]{:S(2)}) collective-permute-start(bf16[16,32,128]{2,1,0:T(8,128)(2,1)S(1)} %get-tuple-element.65), channel_id=1, source_target_pairs={{0,6},{1,7},{14,8},{15,9},{16,22},{17,23},{30,24},{31,25},{32,38},... | collective-permute-start | bytes 393224 | tf_op jit(solution)/shard_map/ppermute | solution.py:294
  30.3 16.2 %collective-permute-start.7 = (bf16[16,32,128]{2,1,0:T(8,128)(2,1)S(1)}, bf16[16,32,128]{2,1,0:T(8,128)(2,1)S(1)}, u32[]{:S(2)}, u32[]{:S(2)}) collective-permute-start(bf16[16,32,128]{2,1,0:T(8,128)(2,1)S(1)} %get-tuple-element.66), channel_id=1, source_target_pairs={{0,8},{1,9},{14,6},{15,7},{16,24},{17,25},{30,22},{31,23},{32,40},... | collective-permute-start | bytes 393224 | tf_op jit(solution)/shard_map/ppermute | solution.py:294
  31.6 14.9 %collective-permute-start.8 = (bf16[16,32,128]{2,1,0:T(8,128)(2,1)S(1)}, bf16[16,32,128]{2,1,0:T(8,128)(2,1)S(1)}, u32[]{:S(2)}, u32[]{:S(2)}) collective-permute-start(bf16[16,32,128]{2,1,0:T(8,128)(2,1)S(1)} %get-tuple-element.67), channel_id=1, source_target_pairs={{0,10},{1,11},{14,4},{15,5},{16,26},{17,27},{30,20},{31,21},{32,42... | collective-permute-start | bytes 393224 | tf_op jit(solution)/shard_map/ppermute | solution.py:294
  36.2 10.6 %collective-permute-start.9 = (bf16[16,32,128]{2,1,0:T(8,128)(2,1)S(1)}, bf16[16,32,128]{2,1,0:T(8,128)(2,1)S(1)}, u32[]{:S(2)}, u32[]{:S(2)}) collective-permute-start(bf16[16,32,128]{2,1,0:T(8,128)(2,1)S(1)} %get-tuple-element.68), channel_id=1, source_target_pairs={{0,12},{1,13},{14,2},{15,3},{16,28},{17,29},{30,18},{31,19},{32,44... | collective-permute-start | bytes 393224 | tf_op jit(solution)/shard_map/ppermute | solution.py:294
  44.5 8.1 %collective-permute-start.10 = (bf16[16,32,128]{2,1,0:T(8,128)(2,1)S(1)}, bf16[16,32,128]{2,1,0:T(8,128)(2,1)S(1)}, u32[]{:S(2)}, u32[]{:S(2)}) collective-permute-start(bf16[16,32,128]{2,1,0:T(8,128)(2,1)S(1)} %get-tuple-element.69), channel_id=1, source_target_pairs={{0,14},{1,15},{14,0},{15,1},{16,30},{17,31},{30,16},{31,17},{32,46... | collective-permute-start | bytes 393224 | tf_op jit(solution)/shard_map/ppermute | solution.py:294
  56.2 6.1 %collective-permute-start.11 = (bf16[32,4096]{1,0:T(8,128)(2,1)S(1)}, bf16[32,4096]{1,0:T(8,128)(2,1)S(1)}, u32[]{:S(2)}, u32[]{:S(2)}) collective-permute-start(bf16[32,4096]{1,0:T(8,128)(2,1)S(1)} %pad_maximum_fusion.2), channel_id=1, source_target_pairs={{0,8},{1,9},{2,10},{3,11},{4,12},{5,13},{6,14},{7,15},{8,0},{9,1},... | collective-permute-start | bytes 786440 | tf_op jit(solution)/shard_map/ppermute | solution.py:294
  56.3 7.3 %collective-permute-start.12 = (bf16[32,4096]{1,0:T(8,128)(2,1)S(1)}, bf16[32,4096]{1,0:T(8,128)(2,1)S(1)}, u32[]{:S(2)}, u32[]{:S(2)}) collective-permute-start(bf16[32,4096]{1,0:T(8,128)(2,1)S(1)} %bitcast.68), channel_id=1, source_target_pairs={{0,2},{1,3},{2,4},{3,5},{4,6},{5,7},{6,0},{7,1},{8,10},{9,11},{10,... | collective-permute-start | bytes 786440 | tf_op jit(solution)/shard_map/ppermute | solution.py:294
  56.4 7.2 %collective-permute-start.13 = (bf16[32,4096]{1,0:T(8,128)(2,1)S(1)}, bf16[32,4096]{1,0:T(8,128)(2,1)S(1)}, u32[]{:S(2)}, u32[]{:S(2)}) collective-permute-start(bf16[32,4096]{1,0:T(8,128)(2,1)S(1)} %bitcast.69), channel_id=1, source_target_pairs={{0,6},{1,7},{2,0},{3,1},{4,2},{5,3},{6,4},{7,5},{8,14},{9,15},{10,... | collective-permute-start | bytes 786440 | tf_op jit(solution)/shard_map/ppermute | solution.py:294
  63.6 14.8 %collective-permute-start.15 = (bf16[64,4096]{1,0:T(8,128)(2,1)S(1)}, bf16[64,4096]{1,0:T(8,128)(2,1)S(1)}, u32[]{:S(2)}, u32[]{:S(2)}) collective-permute-start(bf16[64,4096]{1,0:T(8,128)(2,1)S(1)} %get-tuple-element.112), channel_id=1, source_target_pairs={{0,2},{1,3},{2,4},{3,5},{4,6},{5,7},{6,0},{7,1},{8,10},{9,11},{10,... | collective-permute-start | bytes 1572872 | tf_op jit(solution)/shard_map/ppermute | solution.py:294
  63.7 14.7 %collective-permute-start.16 = (bf16[64,4096]{1,0:T(8,128)(2,1)S(1)}, bf16[64,4096]{1,0:T(8,128)(2,1)S(1)}, u32[]{:S(2)}, u32[]{:S(2)}) collective-permute-start(bf16[64,4096]{1,0:T(8,128)(2,1)S(1)} %get-tuple-element.112), channel_id=1, source_target_pairs={{0,6},{1,7},{2,0},{3,1},{4,2},{5,3},{6,4},{7,5},{8,14},{9,15},{10,... | collective-permute-start | bytes 1572872 | tf_op jit(solution)/shard_map/ppermute | solution.py:294
  66.5 15.9 %collective-permute-start.14 = (bf16[96,4096]{1,0:T(8,128)(2,1)S(1)}, bf16[96,4096]{1,0:T(8,128)(2,1)S(1)}, u32[]{:S(2)}, u32[]{:S(2)}) collective-permute-start(bf16[96,4096]{1,0:T(8,128)(2,1)S(1)} %pad_maximum_fusion), channel_id=1, source_target_pairs={{0,8},{1,9},{2,10},{3,11},{4,12},{5,13},{6,14},{7,15},{8,0},{9,1},... | collective-permute-start | bytes 2359304 | tf_op jit(solution)/shard_map/ppermute | solution.py:294
  67.7 10.8 %collective-permute-start.17 = (bf16[16,4096]{1,0:T(8,128)(2,1)S(1)}, bf16[16,4096]{1,0:T(8,128)(2,1)S(1)}, u32[]{:S(2)}, u32[]{:S(2)}) collective-permute-start(bf16[16,4096]{1,0:T(8,128)(2,1)S(1)} %slice.29), channel_id=1, source_target_pairs={{0,2},{1,3},{2,4},{3,5},{4,6},{5,7},{6,0},{7,1},{8,10},{9,11},{10,... | collective-permute-start | bytes 393224 | tf_op jit(solution)/shard_map/ppermute | solution.py:294
  67.7 10.8 %collective-permute-start.18 = (bf16[16,4096]{1,0:T(8,128)(2,1)S(1)}, bf16[16,4096]{1,0:T(8,128)(2,1)S(1)}, u32[]{:S(2)}, u32[]{:S(2)}) collective-permute-start(bf16[16,4096]{1,0:T(8,128)(2,1)S(1)} %slice.30), channel_id=1, source_target_pairs={{0,6},{1,7},{2,0},{3,1},{4,2},{5,3},{6,4},{7,5},{8,14},{9,15},{10,... | collective-permute-start | bytes 393224 | tf_op jit(solution)/shard_map/ppermute | solution.py:294
  82.5 6.5 %collective-permute-start.19 = (bf16[32,4096]{1,0:T(8,128)(2,1)S(1)}, bf16[32,4096]{1,0:T(8,128)(2,1)S(1)}, u32[]{:S(2)}, u32[]{:S(2)}) collective-permute-start(bf16[32,4096]{1,0:T(8,128)(2,1)S(1)} %slice.31), channel_id=1, source_target_pairs={{0,2},{1,3},{2,4},{3,5},{4,6},{5,7},{6,0},{7,1},{8,10},{9,11},{10,... | collective-permute-start | bytes 786440 | tf_op jit(solution)/shard_map/ppermute | solution.py:294
  82.6 6.4 %collective-permute-start.20 = (bf16[32,4096]{1,0:T(8,128)(2,1)S(1)}, bf16[32,4096]{1,0:T(8,128)(2,1)S(1)}, u32[]{:S(2)}, u32[]{:S(2)}) collective-permute-start(bf16[32,4096]{1,0:T(8,128)(2,1)S(1)} %slice.32), channel_id=1, source_target_pairs={{0,6},{1,7},{2,0},{3,1},{4,2},{5,3},{6,4},{7,5},{8,14},{9,15},{10,... | collective-permute-start | bytes 786440 | tf_op jit(solution)/shard_map/ppermute | solution.py:294
  85.4 5.8 %collective-permute-start.21 = (bf16[32,4096]{1,0:T(8,128)(2,1)S(1)}, bf16[32,4096]{1,0:T(8,128)(2,1)S(1)}, u32[]{:S(2)}, u32[]{:S(2)}) collective-permute-start(bf16[32,4096]{1,0:T(8,128)(2,1)S(1)} %pad_maximum_fusion.4), channel_id=1, source_target_pairs={{0,8},{1,9},{2,10},{3,11},{4,12},{5,13},{6,14},{7,15},{8,0},{9,1},... | collective-permute-start | bytes 786440 | tf_op jit(solution)/shard_map/ppermute | solution.py:294
  89.1 3.9 %copy-start = (bf16[256,4096]{1,0:T(8,128)(2,1)}, bf16[256,4096]{1,0:T(8,128)(2,1)S(1)}, u32[]{:S(2)}) copy-start(bf16[256,4096]{1,0:T(8,128)(2,1)S(1)} %constant_dynamic-update-slice_fusion.2.first_ref.refs_0_.refs_1_.refs_2_) | copy-start | bytes 6291460
  91.2 19.6 %copy-start.6 = (f32[4096]{0:T(1024)S(1)}, f32[4096]{0:T(1024)}, u32[]{:S(2)}) copy-start(f32[4096]{0:T(1024)} %param.12) | copy-start | bytes 49156
  91.2 19.6 %copy-start.9 = (s32[8]{0:T(128)S(1)}, s32[8]{0:T(128)}, u32[]{:S(2)}) copy-start(s32[8]{0:T(128)} %param.13) | copy-start | bytes 100
  91.2 20.5 %copy-start.8 = (f32[2,32,128]{2,1,0:T(8,128)S(1)}, f32[2,32,128]{2,1,0:T(8,128)}, u32[]{:S(2)}) copy-start(f32[2,32,128]{2,1,0:T(8,128)} %param.11) | copy-start | bytes 98308
  92.9 6.5 %collective-permute-start.22 = (f32[8,512]{1,0:T(8,128)S(1)}, f32[8,512]{1,0:T(8,128)S(1)}, u32[]{:S(2)}, u32[]{:S(2)}) collective-permute-start(f32[8,512]{1,0:T(8,128)S(1)} %get-tuple-element.84), channel_id=1, source_target_pairs={{0,1},{1,0},{2,3},{3,2},{4,5},{5,4},{6,7},{7,6},{8,9},{9,8},{10,11... | collective-permute-start | bytes 49160 | tf_op jit(solution)/shard_map/ppermute | solution.py:294
  100.1 23.2 %all-to-all-start.2 = ((f32[16,8,512]{2,1,0:T(8,128)}), f32[16,8,512]{2,1,0:T(8,128)S(1)}, u32[]{:S(2)}, u32[]{:S(2)}) async-start(f32[16,8,512]{2,1,0:T(8,128)} %shard_map.108), calls=%async_computation.2 | async-start | bytes 524288 | tf_op jit(solution)/shard_map/all_to_all | solution.py:409
  111.0 1.5 collective-permute-start.24
  124.0 2.7 %collective-permute-start.23 = (bf16[16,256]{1,0:T(8,128)(2,1)S(1)}, bf16[16,256]{1,0:T(8,128)(2,1)S(1)}, u32[]{:S(2)}, u32[]{:S(2)}) collective-permute-start(bf16[16,256]{1,0:T(8,128)(2,1)S(1)} %get-tuple-element.85.mine_ref), channel_id=1, source_target_pairs={{0,1},{1,0},{2,3},{3,2},{4,5},{5,4},{6,7},{7,6},{8,9},{9,8},{10,11... | collective-permute-start | bytes 24584 | tf_op jit(solution)/shard_map/ppermute | solution.py:294
  126.7 1.6 copy-start.1
  129.5 33.6 %copy-start.2 = (bf16[256,4096]{1,0:T(8,128)(2,1)S(1)}, bf16[256,4096]{1,0:T(8,128)(2,1)}, u32[]{:S(2)}) copy-start(bf16[256,4096]{1,0:T(8,128)(2,1)} %copy-done) | copy-start | bytes 6291460
  129.5 2.7 %collective-permute-start.25 = (f32[16,4096]{1,0:T(8,128)S(1)}, f32[16,4096]{1,0:T(8,128)S(1)}, u32[]{:S(2)}, u32[]{:S(2)}) collective-permute-start(f32[16,4096]{1,0:T(8,128)S(1)} %shard_map.110.x_ref.refs_0_), channel_id=1, source_target_pairs={{0,1},{1,0},{2,3},{3,2},{4,5},{5,4},{6,7},{7,6},{8,9},{9,8},{10,11... | collective-permute-start | bytes 786440 | tf_op jit(solution)/shard_map/ppermute | solution.py:294
  129.9 9.3 %collective-permute-start.26 = (f32[16,4096]{1,0:T(8,128)S(1)}, f32[16,4096]{1,0:T(8,128)S(1)}, u32[]{:S(2)}, u32[]{:S(2)}) collective-permute-start(f32[16,4096]{1,0:T(8,128)S(1)} %shard_map.110.x_ref.refs_0_), channel_id=1, source_target_pairs={{1,16},{16,1},{3,18},{18,3},{5,20},{20,5},{7,22},{22,7},{9,24},{24... | collective-permute-start | bytes 786440 | tf_op jit(solution)/shard_map/ppermute | solution.py:430
  141.0 1.2 collective-permute-start.27
  160.7 2.4 %collective-permute-start.28 = (bf16[16,256]{1,0:T(8,128)(2,1)S(1)}, bf16[16,256]{1,0:T(8,128)(2,1)S(1)}, u32[]{:S(2)}, u32[]{:S(2)}) collective-permute-start(bf16[16,256]{1,0:T(8,128)(2,1)S(1)} %get-tuple-element.88.mine_ref), channel_id=1, source_target_pairs={{0,1},{1,0},{2,3},{3,2},{4,5},{5,4},{6,7},{7,6},{8,9},{9,8},{10,11... | collective-permute-start | bytes 24584 | tf_op jit(solution)/shard_map/ppermute | solution.py:294
  163.1 3.9 %copy-start.5 = (bf16[8,2,32,128]{3,2,1,0:T(8,128)(2,1)S(1)}, bf16[8,2,32,128]{3,2,1,0:T(8,128)(2,1)}, u32[]{:S(2)}) copy-start(bf16[8,2,32,128]{3,2,1,0:T(8,128)(2,1)} %param.16) | copy-start | bytes 393220
  164.3 2.9 %collective-permute-start.29 = (f32[16,4096]{1,0:T(8,128)S(1)}, f32[16,4096]{1,0:T(8,128)S(1)}, u32[]{:S(2)}, u32[]{:S(2)}) collective-permute-start(f32[16,4096]{1,0:T(8,128)S(1)} %shard_map.114.x_ref.refs_0_), channel_id=1, source_target_pairs={{0,1},{1,0},{2,3},{3,2},{4,5},{5,4},{6,7},{7,6},{8,9},{9,8},{10,11... | collective-permute-start | bytes 786440 | tf_op jit(solution)/shard_map/ppermute | solution.py:294
  164.7 9.2 %collective-permute-start.30 = (f32[16,4096]{1,0:T(8,128)S(1)}, f32[16,4096]{1,0:T(8,128)S(1)}, u32[]{:S(2)}, u32[]{:S(2)}) collective-permute-start(f32[16,4096]{1,0:T(8,128)S(1)} %shard_map.114.x_ref.refs_0_), channel_id=1, source_target_pairs={{1,16},{16,1},{3,18},{18,3},{5,20},{20,5},{7,22},{22,7},{9,24},{24... | collective-permute-start | bytes 786440 | tf_op jit(solution)/shard_map/ppermute | solution.py:430
  167.1 15.7 %collective-permute-start.33 = (bf16[8,4096]{1,0:T(8,128)(2,1)S(1)}, bf16[8,4096]{1,0:T(8,128)(2,1)}, u32[]{:S(2)}, u32[]{:S(2)}) collective-permute-start(bf16[8,4096]{1,0:T(8,128)(2,1)S(1)} %bitcast.76), channel_id=1, source_target_pairs={{0,1},{1,0},{2,3},{3,2},{4,5},{5,4},{6,7},{7,6},{8,9},{9,8},{10,11... | collective-permute-start | bytes 196616 | tf_op jit(solution)/shard_map/ppermute | solution.py:294
  175.6 1.2 collective-permute-start.31
  177.6 18.0 %all-to-all-start.4 = ((f32[16,8,512]{2,1,0:T(8,128)}), f32[16,8,512]{2,1,0:T(8,128)S(1)}, u32[]{:S(2)}, u32[]{:S(2)}) async-start(f32[16,8,512]{2,1,0:T(8,128)} %shard_map.116), calls=%async_computation.4 | async-start | bytes 524288 | tf_op jit(solution)/shard_map/all_to_all | solution.py:409
  195.6 2.5 %collective-permute-start.32 = (bf16[16,256]{1,0:T(8,128)(2,1)S(1)}, bf16[16,256]{1,0:T(8,128)(2,1)S(1)}, u32[]{:S(2)}, u32[]{:S(2)}) collective-permute-start(bf16[16,256]{1,0:T(8,128)(2,1)S(1)} %get-tuple-element.92.mine_ref), channel_id=1, source_target_pairs={{0,1},{1,0},{2,3},{3,2},{4,5},{5,4},{6,7},{7,6},{8,9},{9,8},{10,11... | collective-permute-start | bytes 24584 | tf_op jit(solution)/shard_map/ppermute | solution.py:294
  198.1 1.6 copy-start.3
  199.7 9.9 %copy-start.7 = (f32[32,32]{1,0:T(8,128)S(1)}, f32[32,32]{1,0:T(8,128)}, u32[]{:S(2)}) copy-start(f32[32,32]{1,0:T(8,128)} %param.17) | copy-start | bytes 12292
  201.7 21.0 %all-to-all-start.5 = ((f32[256,2,128]{2,1,0:T(2,128)}), f32[256,2,128]{2,1,0:T(2,128)S(1)}, u32[]{:S(2)}, u32[]{:S(2)}) async-start(f32[256,2,128]{2,1,0:T(2,128)} %bitcast.20), calls=%async_computation.5 | async-start | bytes 524288 | tf_op jit(solution)/shard_map/all_to_all | solution.py:453
  207.3 4.0 %collective-permute-start.34 = (f32[8,4096]{1,0:T(8,128)S(1)}, f32[8,4096]{1,0:T(8,128)S(1)}, u32[]{:S(2)}, u32[]{:S(2)}) collective-permute-start(f32[8,4096]{1,0:T(8,128)S(1)} %get-tuple-element.95), channel_id=1, source_target_pairs={{0,1},{1,0},{2,3},{3,2},{4,5},{5,4},{6,7},{7,6},{8,9},{9,8},{10,11... | collective-permute-start | bytes 393224 | tf_op jit(solution)/shard_map/ppermute | solution.py:294
